TPU v7x, 32 devices: a whole 2x2x4 slice. The times are simulated.
32 devices in a mesh: dp: 8 (over y, x, core), expert: 4 (over z).
Axes of the slice: x: 2, y: 2, z: 4, core: 2. Of those that a mesh axis runs over, the one named last changes fastest.
Arguments:
- tokens: bfloat16 [4096, 2048], P(('dp', 'expert')), may hold values from -6 to 6
- cotangent: bfloat16 [4096, 2048], P(('dp', 'expert')), may hold values from -6 to 6
- expert_ids: int32 [4096, 8], P(('dp', 'expert')), may hold values from 0 to 127, as said below
- drop_mask: int32 [4096, 8], P(('dp', 'expert')), may hold values 0 or 1
- gate_table: float32 [4096, 8], P(('dp', 'expert')), may hold values from 0.1 to 1
- gate_weight: bfloat16 [2048, 768], P('dp', 'expert'), may hold values from -0.125 to 0.125
- up_weight: bfloat16 [2048, 768], P('dp', 'expert'), may hold values from -0.125 to 0.125
- down_weight: bfloat16 [768, 2048], P('expert', 'dp'), may hold values from -0.21875 to 0.21875
Outputs:
- grad_tokens: bfloat16 [4096, 2048], P(('dp', 'expert'))
- grad_gate: float32 [2048, 768], P('dp', 'expert')
- grad_up: float32 [2048, 768], P('dp', 'expert')
- grad_down: float32 [768, 2048], P('expert', 'dp')
Inputs may be any that keep to these rules, and one draw needn't show every extreme that they name: `expert_ids`: each row names 8 different experts.
All inputs are finite; a program needn't handle non-finite values. No bound on the sum of `drop_mask` on one device may be relied on, other than what follows from the above.
Results may differ from a plain program's by a relative error of at most 0.018.
Values may be sent and summed in bfloat16 or wider, within the bound.
No kernel may reach another device: no remote copies, remote signals or barrier semaphores. Data moves between devices by JAX's collectives and lax.ppermute only.
A program may use at most 64 MiB of HBM per device.

v0:
```python
import jax
import jax.numpy as jnp
from jax import lax
from jax.sharding import PartitionSpec as P

SPLIT = 4
CAP = 16


def silu_parts(pre_gate):
    sigmoid_value = jax.nn.sigmoid(pre_gate)
    return (pre_gate * sigmoid_value, sigmoid_value * (1.0 + pre_gate * (1.0 - sigmoid_value)))


def slot_table(expert_ids, drop_mask, block_rows, in_flight):
    window = jnp.arange(in_flight, dtype=jnp.int32)
    hit_table = (
        (expert_ids[:, :, None] == window[None, None, :]) & (drop_mask[:, :, None] == 1)
    ).astype(jnp.int32)
    per_token = jnp.sum(hit_table, axis=1)
    blocked = per_token.reshape(-1, block_rows, in_flight)
    earlier = (jnp.cumsum(blocked, axis=1) - blocked).reshape(-1, in_flight)
    slot_rank = jnp.sum(hit_table * earlier[:, None, :], axis=2)
    is_live = (jnp.sum(hit_table, axis=2) > 0) & (slot_rank < CAP)
    return jnp.where(is_live, expert_ids * CAP + slot_rank, in_flight * CAP)


def body(tokens, cotangent, expert_ids, drop_mask, gate_table, gate_weight, up_weight, down_weight):
    expert_count = lax.axis_size("expert")
    in_flight = expert_count // SPLIT
    row_count = tokens.shape[0]
    model_width = tokens.shape[1]
    per_device = in_flight * CAP
    hidden = gate_weight.shape[1]
    contract_last = (((1,), (1,)), ((), ()))
    contract_first = (((0,), (0,)), ((), ()))
    local = slot_table(expert_ids, drop_mask, row_count, in_flight).reshape(-1)
    token_of = jnp.broadcast_to(
        jnp.arange(row_count, dtype=jnp.int32)[:, None], expert_ids.shape
    ).reshape(-1)
    slot_token = jnp.zeros((per_device,), jnp.int32).at[local].set(token_of, mode="drop")
    slot_gate = (
        jnp.zeros((per_device,), jnp.float32).at[local].set(gate_table.reshape(-1), mode="drop")
    )
    filled = jnp.zeros((per_device,), jnp.float32).at[local].set(1.0, mode="drop")
    own_in = jnp.where(filled[:, None] > 0, tokens[slot_token], jnp.zeros((), tokens.dtype))
    own_grad = (slot_gate[:, None] * cotangent[slot_token].astype(jnp.float32)).astype(jnp.bfloat16)

    def spread(values):
        widened = jnp.broadcast_to(
            values.reshape(in_flight, 1, CAP, model_width), (in_flight, SPLIT, CAP, model_width)
        )
        return widened.reshape(expert_count, CAP, model_width)

    arrived_in, arrived_grad = (
        lax.all_to_all(spread(own_in), "expert", split_axis=0, concat_axis=0, tiled=True),
        lax.all_to_all(spread(own_grad), "expert", split_axis=0, concat_axis=0, tiled=True),
    )
    rows_in = arrived_in.reshape(-1, model_width)
    rows_grad = arrived_grad.reshape(-1, model_width)
    stacked = jnp.concatenate([gate_weight, up_weight], axis=1)
    columns = rows_in
    pre_both = jnp.dot(
        columns,
        lax.all_gather(stacked, "dp", axis=0, tiled=True),
        preferred_element_type=jnp.float32,
    )
    columns = rows_grad
    grad_act = lax.dot_general(
        columns,
        lax.all_gather(down_weight, "dp", axis=1, tiled=True),
        contract_last,
        preferred_element_type=jnp.float32,
    )
    pre_gate = pre_both[:, :hidden]
    pre_up = pre_both[:, hidden:]
    silu_value, silu_slope = silu_parts(pre_gate)
    activated = (silu_value * pre_up).astype(jnp.bfloat16)
    grad_gate_pre = (grad_act * pre_up * silu_slope).astype(jnp.bfloat16)
    grad_up_pre = (grad_act * silu_value).astype(jnp.bfloat16)
    grad_pair = jnp.concatenate([grad_gate_pre, grad_up_pre], axis=1)
    slot_grad = lax.dot_general(
        grad_pair,
        lax.all_gather(stacked, "dp", axis=0, tiled=True),
        contract_last,
        preferred_element_type=jnp.float32,
    )
    slot_part = slot_grad.astype(jnp.bfloat16).reshape(expert_count, CAP, model_width)
    returned = lax.all_to_all(slot_part, "expert", split_axis=0, concat_axis=0, tiled=True)
    per_slot = jnp.sum(
        returned.astype(jnp.float32).reshape(in_flight, SPLIT, CAP, model_width), axis=1
    ).reshape(per_device, model_width)
    grad_tokens = (
        jnp.zeros((row_count, model_width), jnp.float32)
        .at[slot_token]
        .add(per_slot * filled[:, None])
    )
    pair_term = lax.dot_general(
        rows_in, grad_pair, contract_first, preferred_element_type=jnp.float32
    )
    down_term = lax.dot_general(
        rows_grad, activated, contract_first, preferred_element_type=jnp.float32
    )
    summed = lax.psum_scatter(
        jnp.concatenate([pair_term, down_term], axis=1).astype(jnp.bfloat16),
        "dp",
        scatter_dimension=0,
        tiled=True,
    ).astype(jnp.float32)
    return (
        grad_tokens.astype(jnp.bfloat16),
        summed[:, :hidden],
        summed[:, hidden : 2 * hidden],
        summed[:, 2 * hidden :].T,
    )


def solution(mesh):
    return jax.shard_map(
        body,
        mesh=mesh,
        in_specs=(
            P(("dp", "expert"), None),
            P(("dp", "expert"), None),
            P(("dp", "expert"), None),
            P(("dp", "expert"), None),
            P(("dp", "expert"), None),
            P("dp", "expert"),
            P("dp", "expert"),
            P("expert", "dp"),
        ),
        out_specs=(
            P(("dp", "expert"), None),
            P("dp", "expert"),
            P("dp", "expert"),
            P("expert", "dp"),
        ),
        check_vma=False,
    )
```

profile of v0, /device:TPU:0, one launch (start us, length us, event | category | flops | bytes accessed | tf_op | source)
XLA Modules:
  0.0 110.7 jit_solution(15465819957817611424)
XLA Ops:
  7.2 0.0 copy-start
  7.2 0.0 copy-start.4
  7.2 0.0 copy-start.2
  7.2 0.0 all-gather.2.cloned.1.call-start
  7.2 1.7 %pad_maximum_fusion.1 = bf16[256,384]{0,1:T(8,128)(2,1)} fusion(bf16[256,192]{0,1:T(8,128)(2,1)} %param.14, bf16[256,192]{0,1:T(8,128)(2,1)} %param.13), kind=kLoop, calls=%fused_computation.14 | loop fusion | flops 393216 | bytes 393216 | tf_op jit(solution)/shard_map/concatenate | solution.py:61
  9.0 0.0 all-gather.2.cloned.1.call-update
  9.0 0.7 convert_reduce_fusion.1
  9.7 0.1 copy.13
  9.8 0.2 reduce-window.7
  10.0 0.1 reduce.4
  10.1 0.7 fusion.6
  10.8 0.1 copy.14
  10.9 0.1 reshape.150
  11.0 0.1 reshape.178
  11.1 4.3 %scatter_custom_fusion = s32[16]{0:T(128)S(1)} fusion(s32[1024]{0:T(1024)S(1)} %bitcast.22, s32[1024]{0:T(1024)S(1)} %reshape.178, s32[]{:T(128)} %constant.8.clone.1), kind=kCustom, calls=%fused_computation.40 | custom fusion | bytes 68 | tf_op jit(solution)/shard_map/scatter | solution.py:41
  15.4 4.3 %scatter_custom_fusion.2 = f32[16]{0:T(128)S(1)} fusion(s32[1024]{0:T(1024)S(1)} %bitcast.23, f32[1024]{0:T(1024)S(1)} %broadcast.73, f32[]{:T(128)} %constant.7.clone.1), kind=kCustom, calls=%fused_computation.36 | custom fusion | bytes 68 | tf_op jit(solution)/shard_map/scatter | solution.py:45
  19.8 0.0 copy-done
  19.8 0.0 copy-start.3
  19.8 0.6 gather_fusion.1
  20.4 0.1 broadcast_select_fusion
  20.5 0.7 reshape.155
  21.2 6.3 %all-to-all-start.1 = ((bf16[4,16,2048]{2,1,0:T(8,128)(2,1)}), bf16[4,16,2048]{2,1,0:T(8,128)(2,1)S(1)}, u32[]{:S(2)}, u32[]{:S(2)}) async-start(bf16[4,16,2048]{2,1,0:T(8,128)(2,1)} %reshape.155), calls=%async_computation.1 | async-start | bytes 524288 | tf_op jit(solution)/shard_map/all_to_all | solution.py:56
  27.5 0.1 copy.15
  27.6 0.1 reshape.186
  27.7 4.3 %scatter_custom_fusion.1 = f32[16]{0:T(128)S(1)} fusion(s32[1024]{0:T(1024)S(1)} %bitcast.24, f32[1024]{0:T(1024)S(1)} %reshape.186, f32[]{:T(128)} %constant.7.clone.1), kind=kCustom, calls=%fused_computation.38 | custom fusion | bytes 68 | tf_op jit(solution)/shard_map/scatter | solution.py:43
  32.0 0.0 copy-done.2
  32.1 0.6 gather_fusion
  32.7 0.1 multiply_convert_fusion
  32.7 3.7 %all-to-all-done.1 = bf16[4,16,2048]{2,1,0:T(8,128)(2,1)S(1)} async-done(((bf16[4,16,2048]{2,1,0:T(8,128)(2,1)}), bf16[4,16,2048]{2,1,0:T(8,128)(2,1)S(1)}, u32[]{:S(2)}, u32[]{:S(2)}) %all-to-all-start.1) | async-done | bytes 262176 | tf_op jit(solution)/shard_map/all_to_all | solution.py:56
  36.5 0.7 reshape.153
  37.2 3.4 %all-to-all-start = ((bf16[4,16,2048]{2,1,0:T(8,128)(2,1)}), bf16[4,16,2048]{2,1,0:T(8,128)(2,1)S(1)}, u32[]{:S(2)}, u32[]{:S(2)}) async-start(bf16[4,16,2048]{2,1,0:T(8,128)(2,1)} %reshape.153), calls=%async_computation | async-start | bytes 524288 | tf_op jit(solution)/shard_map/all_to_all | solution.py:57
  40.6 0.0 reduce-scatter.2.cloned.1.call-start
  40.7 13.1 %all_gather.7 = bf16[192,2048]{1,0:T(8,128)(2,1)S(1)} all-gather(bf16[192,256]{1,0:T(8,128)(2,1)S(1)} %copy-done.3), channel_id=1, replica_groups=mesh['dp'=8,'expert'=4] {'dp'}, dimensions={1}, use_global_device_ids=true | all-gather | bytes 884736 | tf_op jit(solution)/shard_map/all_gather | solution.py:71
  53.8 2.0 %fusion.18 = f32[64,384]{1,0:T(8,128)S(1)} fusion(bf16[64,2048]{1,0:T(8,128)(2,1)S(1)} %bitcast.17, bf16[2048,384]{0,1:T(8,128)(2,1)} %all-gather.2.cloned.1.call-done), kind=kOutput, calls=%fused_computation.46 | convolution fusion | flops 100663296 | bytes 1933312 | tf_op jit(solution)/shard_map/dot_general | solution.py:63
  55.8 0.0 all-to-all-done
  55.8 0.5 convolution_convert_fusion.1
  56.3 0.4 multiply_convert_fusion.3
  56.7 0.6 convolution_convert_fusion
  57.3 1.6 %pad_maximum_fusion = bf16[2048,576]{0,1:T(8,128)(2,1)} fusion(bf16[2048,192]{0,1:T(8,128)(2,1)S(1)} %convolution_convert_fusion.1, bf16[2048,384]{0,1:T(8,128)(2,1)S(1)} %convolution_convert_fusion), kind=kLoop, calls=%fused_computation.8 | loop fusion | flops 4718592 | bytes 4718592 | tf_op jit(solution)/shard_map/concatenate | solution.py:105
  58.9 0.0 reduce-scatter.2.cloned.1.call-update
  58.9 1.4 %copy-done.1 = bf16[2048,384]{0,1:T(8,128)(2,1)S(1)} copy-done((bf16[2048,384]{0,1:T(8,128)(2,1)S(1)}, bf16[2048,384]{0,1:T(8,128)(2,1)}, u32[]{:S(2)}) %copy-start.1) | copy-done | bytes 1572888
  60.3 0.4 convolution_convert_fusion.2
  60.7 14.2 %all_to_all.15 = bf16[4,16,2048]{2,1,0:T(8,128)(2,1)S(1)} all-to-all(bf16[4,16,2048]{2,1,0:T(8,128)(2,1)S(1)} %bitcast.21), channel_id=1, replica_groups=mesh['dp'=8,'expert'=4] {'expert'}, dimensions={0} | all-to-all | bytes 524288 | tf_op jit(solution)/shard_map/all_to_all | solution.py:89
  74.9 1.1 %scatter_custom_fusion.3 = f32[128,2048]{1,0:T(8,128)S(1)} fusion(s32[16]{0:T(128)S(1)} %compare_select_fusion.1, f32[]{:T(128)} %constant.7.clone.1, f32[16,2048]{1,0:T(8,128)S(1)} %convert_reduce_fusion, f32[16]{0:T(128)S(1)} %scatter_custom_fusion.2), kind=kCustom, calls=%fused_computation.11 | custom fusion | flops 65536 | bytes 1180164 | tf_op jit(solution)/shard_map/scatter-add | solution.py:96
  76.1 0.9 convert_element_type.47
  76.9 24.1 %reduce-scatter.2.cloned.1.call-done = bf16[256,576]{0,1:T(8,128)(2,1)} async-done(((bf16[2048,576]{0,1:T(8,128)(2,1)}), bf16[256,576]{0,1:T(8,128)(2,1)}) %reduce-scatter.2.cloned.1.call-update) | async-done | bytes 294928 | tf_op jit(solution)/shard_map/reduce_scatter | solution.py:104
  101.0 1.0 convert_element_type.49
  102.0 1.8 %fusion.17 = (f32[256,192]{0,1:T(8,128)}, f32[256,192]{0,1:T(8,128)}, f32[192,256]{1,0:T(8,128)}) fusion(bf16[256,576]{0,1:T(8,128)(2,1)} %reduce-scatter.2.cloned.1.call-done, f32[256,576]{0,1:T(8,128)S(1)} %convert_element_type.49), kind=kLoop, calls=%fused_computation.45 | loop fusion | bytes 1179648 | tf_op jit(solution)/shard_map/slice | solution.py:113
  (12 shorter events, 0.1 us)
Async XLA Ops:
  7.2 12.6 %copy-start = (bf16[128,2048]{1,0:T(8,128)(2,1)S(1)}, bf16[128,2048]{1,0:T(8,128)(2,1)}, u32[]{:S(2)}) copy-start(bf16[128,2048]{1,0:T(8,128)(2,1)} %param.8) | copy-start | bytes 1572868
  7.2 20.4 %copy-start.4 = (f32[128,8]{0,1:T(8,128)S(1)}, f32[128,8]{0,1:T(8,128)}, u32[]{:S(2)}) copy-start(f32[128,8]{0,1:T(8,128)} %param.12) | copy-start | bytes 12292
  7.2 24.9 %copy-start.2 = (bf16[128,2048]{1,0:T(8,128)(2,1)S(1)}, bf16[128,2048]{1,0:T(8,128)(2,1)}, u32[]{:S(2)}) copy-start(bf16[128,2048]{1,0:T(8,128)(2,1)} %param.9) | copy-start | bytes 1572868
  7.2 46.6 %all-gather.2.cloned.1.call-start = ((), (), s32[]{:S(2)}) async-start(), calls=%async_computation.4 | async-start | bytes 1769472 | tf_op jit(solution)/shard_map/all_gather | solution.py:65
  19.8 20.9 %copy-start.3 = (bf16[192,256]{1,0:T(8,128)(2,1)S(1)}, bf16[192,256]{1,0:T(8,128)(2,1)}, u32[]{:S(2)}) copy-start(bf16[192,256]{1,0:T(8,128)(2,1)} %param.15) | copy-start | bytes 294916
  21.2 15.2 %all-to-all-start.1 = ((bf16[4,16,2048]{2,1,0:T(8,128)(2,1)}), bf16[4,16,2048]{2,1,0:T(8,128)(2,1)S(1)}, u32[]{:S(2)}, u32[]{:S(2)}) async-start(bf16[4,16,2048]{2,1,0:T(8,128)(2,1)} %reshape.155), calls=%async_computation.1 | async-start | bytes 524288 | tf_op jit(solution)/shard_map/all_to_all | solution.py:56
  37.2 18.6 %all-to-all-start = ((bf16[4,16,2048]{2,1,0:T(8,128)(2,1)}), bf16[4,16,2048]{2,1,0:T(8,128)(2,1)S(1)}, u32[]{:S(2)}, u32[]{:S(2)}) async-start(bf16[4,16,2048]{2,1,0:T(8,128)(2,1)} %reshape.153), calls=%async_computation | async-start | bytes 524288 | tf_op jit(solution)/shard_map/all_to_all | solution.py:57
  40.6 60.5 %reduce-scatter.2.cloned.1.call-start = ((), (), s32[]{:S(2)}) async-start(), calls=%async_computation.5 | async-start | bytes 2654208 | tf_op jit(solution)/shard_map/reduce_scatter | solution.py:104
  58.9 1.4 %copy-start.1 = (bf16[2048,384]{0,1:T(8,128)(2,1)S(1)}, bf16[2048,384]{0,1:T(8,128)(2,1)}, u32[]{:S(2)}) copy-start(bf16[2048,384]{0,1:T(8,128)(2,1)} %all-gather.2.cloned.1.call-done) | copy-start | bytes 4718596
Sparse Core Ops, SparseCore 0:
  10.5 28.5 all-gather.1
  59.0 41.9 reduce-scatter.1
where the time goes:
time: 111 us
  waiting for transfers between devices  27.9 us (25%)
  blocking collectives  27.3 us (25%)
  local copies, waits for them, and re-layouts  19.3 us (17%)
  between operations  14.2 us (13%)
  starting transfers between devices  9.8 us (9%)
  other arithmetic  8.16 us (7%)
  matrix products  3.94 us (4%)
    reduce_scatter x1, waiting for transfers between devices, body(): lax.psum_scatter(jnp.concatenate([pair_term, down_term], axis=1).astype(j...  24.1 us
    all_to_all x1, blocking collectives, body(): lax.all_to_all(slot_part, 'expert', split_axis=0, concat_axis=0, tiled=True)  14.2 us
    all_gather x1, blocking collectives, body(): lax.all_gather(down_weight, 'dp', axis=1, tiled=True)  13.1 us
    all_to_all x1, starting transfers between devices, body(): lax.all_to_all(spread(own_in), 'expert', split_axis=0, concat_axis=0, til...  6.32 us
    scatter x1, local copies, waits for them, and re-layouts, body(): jnp.zeros((per_device,), jnp.float32).at[local].set(1.0, mode='drop')  4.3 us
    scatter x1, local copies, waits for them, and re-layouts, body(): jnp.zeros((per_device,), jnp.float32).at[local]  4.3 us
    scatter x1, local copies, waits for them, and re-layouts, body(): jnp.zeros((per_device,), jnp.int32).at[local].set(token_of, mode='drop')  4.3 us
    all_to_all x1, waiting for transfers between devices, body(): lax.all_to_all(spread(own_in), 'expert', split_axis=0, concat_axis=0, til...  3.72 us
  transfers between devices with their start and end apart: 4, of which 2 were waited for; matrix products, arithmetic and copies ran while one was open for 20% of the time, Pallas kernels for 0%

commit v1 on v0

v1 whole, which is shorter than its diff:
```python
import functools

import jax
import jax.numpy as jnp
from jax import lax
from jax.experimental import pallas as pl
from jax.experimental.pallas import tpu as pltpu
from jax.sharding import PartitionSpec as P

SPLIT = 4
CAP = 16
VMEM_LIMIT = 48 * 1024 * 1024

CONTRACT_LAST = (((1,), (1,)), ((), ()))
CONTRACT_FIRST = (((0,), (0,)), ((), ()))
PLAIN = (((1,), (0,)), ((), ()))


def dot(left, right, dims):
    return lax.dot_general(left, right, dims, preferred_element_type=jnp.float32)


def call(kernel, out_shape, args, after=(), flops=0):
    def run(*refs):
        kernel(*refs[: len(args)], *refs[len(args) + len(after) :])

    return pl.pallas_call(
        run,
        out_shape=out_shape,
        in_specs=[pl.BlockSpec(memory_space=pltpu.VMEM)] * len(args)
        + [pl.BlockSpec(memory_space=pl.ANY)] * len(after),
        out_specs=jax.tree.map(lambda _: pl.BlockSpec(memory_space=pltpu.VMEM), out_shape),
        compiler_params=pltpu.CompilerParams(vmem_limit_bytes=VMEM_LIMIT),
        cost_estimate=pl.CostEstimate(flops=flops, bytes_accessed=0, transcendentals=0),
    )(*args, *after)


def swap(values, axis, shift):
    size = lax.axis_size(axis)
    return lax.ppermute(values, axis, [(i, i ^ shift) for i in range(size)])


def begin_kernel(
    ids_hbm, mask_hbm, gate_hbm, tok_hbm, cot_hbm, gate_w_hbm, up_w_hbm, down_w_hbm,
    rows_ref, hot_ref, stack_ref,
    ids_ref, mask_ref, gate_ref, tok_ref, cot_ref, sems,
):
    flight, _, blocks, cap, width = rows_ref.shape
    hidden = gate_w_hbm.shape[0]
    pairs = [
        (ids_hbm, ids_ref),
        (mask_hbm, mask_ref),
        (gate_hbm, gate_ref),
        (tok_hbm, tok_ref),
        (cot_hbm, cot_ref),
        (gate_w_hbm, stack_ref.at[pl.ds(0, hidden)]),
        (up_w_hbm, stack_ref.at[pl.ds(hidden, hidden)]),
        (down_w_hbm, stack_ref.at[pl.ds(2 * hidden, hidden)]),
    ]
    copies = [
        pltpu.make_async_copy(source, target, sems.at[i])
        for i, (source, target) in enumerate(pairs)
    ]
    for copy in copies:
        copy.start()
    count = ids_ref.shape[1]
    earlier = (
        lax.broadcasted_iota(jnp.int32, (count, count), 0)
        < lax.broadcasted_iota(jnp.int32, (count, count), 1)
    ).astype(jnp.bfloat16)
    slot = lax.broadcasted_iota(jnp.int32, (cap, count), 0).astype(jnp.float32)
    for copy in copies[:5]:
        copy.wait()
    live = mask_ref[...] == 1
    for j in range(flight):
        hit = jnp.where((ids_ref[...] == j) & live, 1.0, 0.0)
        held = jnp.sum(hit, axis=0, keepdims=True)
        rank = jnp.sum(dot(hit.astype(jnp.bfloat16), earlier, PLAIN), axis=0, keepdims=True)
        gate = jnp.sum(hit * gate_ref[...], axis=0, keepdims=True)
        hot = jnp.where((slot == rank) & (held > 0.0), 1.0, 0.0)
        slot_gate = jnp.sum(hot * gate, axis=1, keepdims=True)
        hot = hot.astype(jnp.bfloat16)
        hot_ref[j] = hot
        picked = dot(hot, tok_ref[...], PLAIN).astype(jnp.bfloat16)
        graded = (slot_gate * dot(hot, cot_ref[...], PLAIN)).astype(jnp.bfloat16)
        for b in range(blocks):
            rows_ref[j, 0, b] = picked[:, b * width : (b + 1) * width]
            rows_ref[j, 1, b] = graded[:, b * width : (b + 1) * width]
    for copy in copies[5:]:
        copy.wait()


def join_kernel(*refs):
    for i, ref in enumerate(refs[:-1]):
        refs[-1][i] = ref[...]


def rows_of(row_refs, kind, block):
    return jnp.concatenate([r[kind, block] for r in row_refs], axis=0)


def repack_kernel(chunks, *refs):
    me = lax.axis_index("dp")
    for i, out_ref in enumerate(refs[chunks:]):
        first = ((me ^ (2 * i)) // 2) * 2
        for kind in range(2):
            for k in range(2):
                out_ref[kind, k] = rows_of(refs[:chunks], kind, first + k)


def expert_kernel(chunks, *refs):
    row_refs, (half_ref, other_ref, grads_ref) = refs[:chunks], refs[chunks : chunks + 3]
    part_refs = refs[chunks + 3 :]
    me = lax.axis_index("dp")
    blocks = 2 * half_ref.shape[0]
    weight_refs = [(half_ref, other_ref)[s % 2].at[s // 2] for s in range(blocks)]
    hidden = weight_refs[0].shape[0] // 3
    pre_gate, pre_up, grad_act = 0.0, 0.0, 0.0
    for s, weight_ref in enumerate(weight_refs):
        rows_in = rows_of(row_refs, 0, me ^ s)
        pre_gate += dot(rows_in, weight_ref[:hidden], CONTRACT_LAST)
        pre_up += dot(rows_in, weight_ref[hidden : 2 * hidden], CONTRACT_LAST)
        rows_grad = rows_of(row_refs, 1, me ^ s)
        grad_act += dot(rows_grad, weight_ref[2 * hidden :], CONTRACT_LAST)
    sigmoid_value = lax.logistic(pre_gate)
    silu_value = pre_gate * sigmoid_value
    slope = sigmoid_value * (1.0 + pre_gate * (1.0 - sigmoid_value))
    grad_gate_pre = (grad_act * pre_up * slope).astype(jnp.bfloat16)
    grad_up_pre = (grad_act * silu_value).astype(jnp.bfloat16)
    activated = (silu_value * pre_up).astype(jnp.bfloat16)
    grads_ref[...] = jnp.concatenate([grad_gate_pre, grad_up_pre, activated], axis=1)
    for s, weight_ref in enumerate(weight_refs):
        part = dot(grad_gate_pre, weight_ref[:hidden], PLAIN)
        part += dot(grad_up_pre, weight_ref[hidden : 2 * hidden], PLAIN)
        part = part.astype(jnp.bfloat16)
        for c, part_ref in enumerate(part_refs):
            part_ref[me ^ s] = part[c * CAP : (c + 1) * CAP]


def weight_grad_kernel(chips, *refs):
    row_refs, grad_refs = refs[:chips], refs[chips : 2 * chips]
    own_ref, other_ref = refs[-2:]
    hidden = own_ref.shape[0] // 3
    core = lax.rem(lax.axis_index("dp"), 2)
    grads = jnp.concatenate([g[...] for g in grad_refs], axis=0)
    for out_ref, block in ((other_ref, 1 - core), (own_ref, core)):
        rows_in = jnp.concatenate([r[0, block] for r in row_refs], axis=0)
        rows_grad = jnp.concatenate([r[1, block] for r in row_refs], axis=0)
        pair = dot(grads[:, : 2 * hidden], rows_in, CONTRACT_FIRST)
        down = dot(grads[:, 2 * hidden :], rows_grad, CONTRACT_FIRST)
        out_ref[: 2 * hidden] = pair.astype(out_ref.dtype)
        out_ref[2 * hidden :] = down.astype(out_ref.dtype)


def finish_kernel(own_ref, other_ref, gate_ref, up_ref, down_ref):
    hidden = gate_ref.shape[0]
    for i, out_ref in enumerate((gate_ref, up_ref, down_ref)):
        part = slice(i * hidden, (i + 1) * hidden)
        out_ref[...] = own_ref[part] + other_ref[part].astype(jnp.float32)


def place_kernel(chunks, hot_ref, *refs):
    part_refs, out_ref = refs[:chunks], refs[chunks]
    flight = hot_ref.shape[0]
    blocks, _, width = part_refs[0].shape
    home = lax.axis_index("expert") // SPLIT
    for b in range(blocks):
        total = 0.0
        for j in range(flight):
            summed = 0.0
            for c in range(j * SPLIT, (j + 1) * SPLIT):
                summed += part_refs[c][b].astype(jnp.float32)
            high = summed.astype(jnp.bfloat16)
            hot = hot_ref[home ^ j]
            total += dot(hot, high, CONTRACT_FIRST)
            if flight > 1:
                low = (summed - high.astype(jnp.float32)).astype(jnp.bfloat16)
                total += dot(hot, low, CONTRACT_FIRST)
        out_ref[:, b * width : (b + 1) * width] = total.astype(out_ref.dtype)


def body(tokens, cotangent, expert_ids, drop_mask, gate_table, gate_weight, up_weight, down_weight):
    chunks = lax.axis_size("expert")
    blocks = lax.axis_size("dp")
    flight = chunks // SPLIT
    count, model_width = tokens.shape
    width = model_width // blocks
    hidden = gate_weight.shape[1]
    rows = chunks * CAP
    struct = jax.ShapeDtypeStruct

    chips = blocks // 2
    dma = pltpu.SemaphoreType.DMA
    operands = (
        expert_ids.T, drop_mask.T, gate_table.T, tokens, cotangent,
        gate_weight.T, up_weight.T, down_weight,
    )
    own_rows, hot, own_weights = pl.pallas_call(
        begin_kernel,
        out_shape=(
            struct((flight, 2, blocks, CAP, width), jnp.bfloat16),
            struct((flight, CAP, count), jnp.bfloat16),
            struct((3 * hidden, width), jnp.bfloat16),
        ),
        in_specs=[pl.BlockSpec(memory_space=pltpu.HBM)] * 8,
        out_specs=(pl.BlockSpec(memory_space=pltpu.VMEM),) * 3,
        scratch_shapes=[pltpu.VMEM(v.shape, v.dtype) for v in operands[:5]] + [dma((8,))],
        compiler_params=pltpu.CompilerParams(vmem_limit_bytes=VMEM_LIMIT),
    )(*[pltpu.with_memory_space_constraint(v, pltpu.HBM) for v in operands])
    me = lax.axis_index("expert")

    def rows_for(c):
        if flight == 1:
            return own_rows[0]
        return lax.dynamic_index_in_dim(own_rows, (me ^ c) // SPLIT, 0, keepdims=False)

    arrived = [rows_for(0)]
    for c in range(1, chunks):
        if c % SPLIT == 3:
            arrived.append(swap(arrived[c - 1], "expert", 1))
        else:
            arrived.append(swap(rows_for(c), "expert", c))
    shards = [swap(own_weights, "dp", 2 * i) for i in reversed(range(1, chips))]
    shards = [own_weights] + shards[::-1]
    half = call(
        join_kernel,
        struct((chips, 3 * hidden, width), jnp.bfloat16),
        shards,
        after=arrived[1:],
    )
    other_half = swap(half, "dp", 1)
    packed = call(
        functools.partial(repack_kernel, chunks),
        [struct((2, 2, rows, width), jnp.bfloat16)] * chips,
        arrived,
    )
    block_rows = [packed[0]] + [swap(packed[i], "dp", 2 * i) for i in range(1, chips)]

    grads, *parts = call(
        functools.partial(expert_kernel, chunks),
        [struct((rows, 3 * hidden), jnp.bfloat16)]
        + [struct((blocks, CAP, width), jnp.bfloat16)] * chunks,
        (*arrived, half, other_half),
        flops=5 * 10**9,
    )
    all_grads = [grads] + [swap(grads, "dp", 2 * i) for i in range(1, chips)]
    returned = [parts[0]] + [swap(parts[c], "expert", c) for c in range(1, chunks)]

    own_sum, other_sum = call(
        functools.partial(weight_grad_kernel, chips),
        [
            struct((3 * hidden, width), jnp.float32),
            struct((3 * hidden, width), jnp.bfloat16),
        ],
        (*block_rows, *all_grads),
        after=returned[1:],
    )
    other_sum = swap(other_sum, "dp", 1)
    grad_tokens = call(
        functools.partial(place_kernel, chunks),
        struct((count, model_width), jnp.bfloat16),
        (hot, *returned),
    )
    grad_gate, grad_up, grad_down = call(
        finish_kernel,
        [struct((hidden, width), jnp.float32)] * 3,
        (own_sum, other_sum),
    )
    return grad_tokens, grad_gate.T, grad_up.T, grad_down


def solution(mesh):
    split_rows = P(("dp", "expert"), None)
    return jax.shard_map(
        body,
        mesh=mesh,
        in_specs=(split_rows,) * 5 + (P("dp", "expert"), P("dp", "expert"), P("expert", "dp")),
        out_specs=(split_rows, P("dp", "expert"), P("dp", "expert"), P("expert", "dp")),
        check_vma=False,
    )
```

time: 111 us -> 43.6 us (0.39)
  blocking collectives: 27.3 us -> 0 us
  local copies, waits for them, and re-layouts: 19.3 us -> 0 us
  waiting for transfers between devices: 27.9 us -> 14.4 us
  between operations: 14.2 us -> 0.71 us
  starting transfers between devices: 9.8 us -> 22.7 us
  other arithmetic: 8.16 us -> 0 us
  Pallas kernels: 0 us -> 5.71 us
  matrix products: 3.94 us -> 0 us
    reduce_scatter x1 -> x0, waiting for transfers between devices: 24.1 us -> none  [body(): lax.psum_scatter(jnp.concatenate([pair_term, down_term], axis=1).astype(j...]
    ppermute x0 -> x17, starting transfers between devices: none -> 22.7 us  [swap(): return lax.ppermute(values, axis, [(i, i ^ shift) for i in range(size)])]
    ppermute x0 -> x17, waiting for transfers between devices: none -> 14.4 us  [swap(): return lax.ppermute(values, axis, [(i, i ^ shift) for i in range(size)])]
    all_to_all x1 -> x0, blocking collectives: 14.2 us -> none  [body(): lax.all_to_all(slot_part, 'expert', split_axis=0, concat_axis=0, tiled=True)]
    all_gather x1 -> x0, blocking collectives: 13.1 us -> none  [body(): lax.all_gather(down_weight, 'dp', axis=1, tiled=True)]
    scatter x3 -> x0, local copies, waits for them, and re-layouts: 12.9 us -> none  [the longest x1 4.3 us: body(): jnp.zeros((per_device,), jnp.float32).at[local].set(1.0, mode='drop')]
    all_to_all x2 -> x0, starting transfers between devices: 9.72 us -> none  [the longest x1 6.32 us: body(): lax.all_to_all(spread(own_in), 'expert', split_axis=0, concat_axis=0, til...]
    pallas_call x0 -> x7, Pallas kernels: none -> 5.71 us  [the longest x6 4.01 us: call(): pl.pallas_call(run, out_shape=out_shape, in_specs=[pl.BlockSpec(memory_sp...]
  transfers between devices with their start and end apart: 4 -> 17, of which waited for: 2 -> 6; matrix products, arithmetic and copies ran while one was open for 20% -> 0% of each run, Pallas kernels for 0% -> 6%
where the time goes in v1:
time: 43.6 us; the launch traced here: 43.5 us
  starting transfers between devices  22.7 us (52%)
  waiting for transfers between devices  14.4 us (33%)
  Pallas kernels  5.71 us (13%)
  between operations  0.71 us (2%)
    ppermute x17, starting transfers between devices, swap(): return lax.ppermute(values, axis, [(i, i ^ shift) for i in range(size)])  22.7 us
    ppermute x17, waiting for transfers between devices, swap(): return lax.ppermute(values, axis, [(i, i ^ shift) for i in range(size)])  14.4 us
    pallas_call x6, Pallas kernels, call(): pl.pallas_call(run, out_shape=out_shape, in_specs=[pl.BlockSpec(memory_sp...  4.01 us
    pallas_call x1, Pallas kernels, body(): pl.pallas_call(begin_kernel, out_shape=(struct((flight, 2, blocks, CAP, w...  1.7 us
  transfers between devices with their start and end apart: 17, of which 6 were waited for; matrix products, arithmetic and copies ran while one was open for 0% of the time, Pallas kernels for 6%

profile of v1, /device:TPU:0, one launch (start us, length us, event | category | flops | bytes accessed | tf_op | source)
XLA Modules:
  0.0 43.5 jit_solution(11969874500453625705)
XLA Ops:
  0.6 1.7 %shard_map.111 = (bf16[1,2,8,16,256]{4,3,2,1,0:T(8,128)(2,1)S(1)}, bf16[1,16,128]{2,1,0:T(8,128)(2,1)S(1)}, bf16[576,256]{1,0:T(8,128)(2,1)S(1)}) custom-call(s32[8,128]{1,0:T(8,128)} %bitcast.14, s32[8,128]{1,0:T(8,128)} %bitcast.15, f32[8,128]{1,0:T(8,128)} %bitcast.16, bf16[128,2048]{1,0:T(8,128)(2,1)} %tok_hbm.1, bf16[128,2048]{1,0:T(8,128)(2,1)} %cot_hbm.1, ...), custom_call_target="tpu_custom_call" | custom-call | tf_op jit(solution)/shard_map/pallas_call | solution.py:198
  2.3 3.0 %collective-permute-start.3 = (bf16[576,256]{1,0:T(8,128)(2,1)S(1)}, bf16[576,256]{1,0:T(8,128)(2,1)S(1)}, u32[]{:S(2)}, u32[]{:S(2)}) collective-permute-start(bf16[576,256]{1,0:T(8,128)(2,1)S(1)} %get-tuple-element.23.refs_0_), channel_id=1, source_target_pairs={{0,8},{4,12},{8,0},{12,4},{16,24},{20,28},{24,16},{28,20},{1,9},{5... | collective-permute-start | bytes 884744 | tf_op jit(solution)/shard_map/ppermute | solution.py:40
  5.3 1.5 %collective-permute-start.4 = (bf16[576,256]{1,0:T(8,128)(2,1)S(1)}, bf16[576,256]{1,0:T(8,128)(2,1)S(1)}, u32[]{:S(2)}, u32[]{:S(2)}) collective-permute-start(bf16[576,256]{1,0:T(8,128)(2,1)S(1)} %get-tuple-element.23.refs_0_), channel_id=1, source_target_pairs={{0,16},{4,20},{8,24},{12,28},{16,0},{20,4},{24,8},{28,12},{1,17},{... | collective-permute-start | bytes 884744 | tf_op jit(solution)/shard_map/ppermute | solution.py:40
  6.9 0.0 collective-permute-start.5
  6.9 3.0 %collective-permute-start.1 = (bf16[2,8,16,256]{3,2,1,0:T(8,128)(2,1)S(1)}, bf16[2,8,16,256]{3,2,1,0:T(8,128)(2,1)S(1)}, u32[]{:S(2)}, u32[]{:S(2)}) collective-permute-start(bf16[2,8,16,256]{3,2,1,0:T(8,128)(2,1)S(1)} %bitcast.8), channel_id=1, source_target_pairs={{0,2},{1,3},{2,0},{3,1},{4,6},{5,7},{6,4},{7,5},{8,10},{9,11},{10,... | collective-permute-start | bytes 393224 | tf_op jit(solution)/shard_map/ppermute | solution.py:40
  9.9 1.6 %collective-permute-start = (bf16[2,8,16,256]{3,2,1,0:T(8,128)(2,1)S(1)}, bf16[2,8,16,256]{3,2,1,0:T(8,128)(2,1)S(1)}, u32[]{:S(2)}, u32[]{:S(2)}) collective-permute-start(bf16[2,8,16,256]{3,2,1,0:T(8,128)(2,1)S(1)} %bitcast.9), channel_id=1, source_target_pairs={{0,1},{1,0},{2,3},{3,2},{4,5},{5,4},{6,7},{7,6},{8,9},{9,8},{10,11... | collective-permute-start | bytes 393224 | tf_op jit(solution)/shard_map/ppermute | solution.py:40
  11.5 4.0 %collective-permute-done.1.refs_5_.refs_2_ = bf16[2,8,16,256]{3,2,1,0:T(8,128)(2,1)S(1)} collective-permute-done((bf16[2,8,16,256]{3,2,1,0:T(8,128)(2,1)S(1)}, bf16[2,8,16,256]{3,2,1,0:T(8,128)(2,1)S(1)}, u32[]{:S(2)}, u32[]{:S(2)}) %collective-permute-start.1) | collective-permute-done | bytes 131104 | tf_op jit(solution)/shard_map/ppermute | solution.py:40
  15.5 0.6 %collective-permute-start.2 = (bf16[2,8,16,256]{3,2,1,0:T(8,128)(2,1)S(1)}, bf16[2,8,16,256]{3,2,1,0:T(8,128)(2,1)S(1)}, u32[]{:S(2)}, u32[]{:S(2)}) collective-permute-start(bf16[2,8,16,256]{3,2,1,0:T(8,128)(2,1)S(1)} %collective-permute-done.1.refs_5_.refs_2_), channel_id=1, source_target_pairs={{0,1},{1,0},{2,3},{3,2},{4,5},{5,4},{6,7},{7,6},{8,9},{9,8},{10,11... | collective-permute-start | bytes 393224 | tf_op jit(solution)/shard_map/ppermute | solution.py:40
  16.1 0.0 collective-permute-done.refs_4_.refs_1_
  16.1 4.3 %collective-permute-done.2.refs_6_.refs_3_ = bf16[2,8,16,256]{3,2,1,0:T(8,128)(2,1)S(1)} collective-permute-done((bf16[2,8,16,256]{3,2,1,0:T(8,128)(2,1)S(1)}, bf16[2,8,16,256]{3,2,1,0:T(8,128)(2,1)S(1)}, u32[]{:S(2)}, u32[]{:S(2)}) %collective-permute-start.2) | collective-permute-done | bytes 131104 | tf_op jit(solution)/shard_map/ppermute | solution.py:40
  20.5 0.0 collective-permute-done.3.refs_1_
  20.5 0.0 collective-permute-done.4.refs_2_
  20.5 0.0 collective-permute-done.5.refs_3_
  20.5 0.1 shard_map.112.refs_4_
  20.6 0.1 collective-permute-start.6
  20.6 0.1 shard_map.115
  20.7 1.6 %collective-permute-start.10 = (bf16[2,2,64,256]{3,2,1,0:T(8,128)(2,1)S(1)}, bf16[2,2,64,256]{3,2,1,0:T(8,128)(2,1)S(1)}, u32[]{:S(2)}, u32[]{:S(2)}) collective-permute-start(bf16[2,2,64,256]{3,2,1,0:T(8,128)(2,1)S(1)} %get-tuple-element.29), channel_id=1, source_target_pairs={{0,8},{4,12},{8,0},{12,4},{16,24},{20,28},{24,16},{28,20},{1,9},{5... | collective-permute-start | bytes 393224 | tf_op jit(solution)/shard_map/ppermute | solution.py:40
  22.3 1.5 %collective-permute-start.11 = (bf16[2,2,64,256]{3,2,1,0:T(8,128)(2,1)S(1)}, bf16[2,2,64,256]{3,2,1,0:T(8,128)(2,1)S(1)}, u32[]{:S(2)}, u32[]{:S(2)}) collective-permute-start(bf16[2,2,64,256]{3,2,1,0:T(8,128)(2,1)S(1)} %get-tuple-element.30), channel_id=1, source_target_pairs={{0,16},{4,20},{8,24},{12,28},{16,0},{20,4},{24,8},{28,12},{1,17},{... | collective-permute-start | bytes 393224 | tf_op jit(solution)/shard_map/ppermute | solution.py:40
  23.8 0.4 collective-permute-start.12
  24.3 0.0 collective-permute-done.6.refs_5_
  24.3 1.5 %shard_map.113 = (bf16[64,576]{1,0:T(8,128)(2,1)S(1)}, bf16[8,16,256]{2,1,0:T(8,128)(2,1)S(1)}, bf16[8,16,256]{2,1,0:T(8,128)(2,1)S(1)}, bf16[8,16,256]{2,1,0:T(8,128)(2,1)S(1)}, bf16[8,16,256]{2,1,0:T(8,128)(2,1)S(1)}) custom-call(bf16[2,8,16,256]{3,2,1,0:T(8,128)(2,1)S(1)} %bitcast.11, bf16[2,8,16,256]{3,2,1,0:T(8,128)(2,1)S(1)} %collective-permute-done.refs_4_.refs_1_, ...), custom_call_target="tpu_custom_call" | custom-call | flops 5000000000 | tf_op jit(solution)/shard_map/pallas_call | solution.py:27
  25.8 1.3 %collective-permute-start.7 = (bf16[8,16,256]{2,1,0:T(8,128)(2,1)S(1)}, bf16[8,16,256]{2,1,0:T(8,128)(2,1)S(1)}, u32[]{:S(2)}, u32[]{:S(2)}) collective-permute-start(bf16[8,16,256]{2,1,0:T(8,128)(2,1)S(1)} %get-tuple-element.25), channel_id=1, source_target_pairs={{0,1},{1,0},{2,3},{3,2},{4,5},{5,4},{6,7},{7,6},{8,9},{9,8},{10,11... | collective-permute-start | bytes 196616 | tf_op jit(solution)/shard_map/ppermute | solution.py:40
  27.1 1.2 %collective-permute-start.13 = (bf16[64,576]{1,0:T(8,128)(2,1)S(1)}, bf16[64,576]{1,0:T(8,128)(2,1)S(1)}, u32[]{:S(2)}, u32[]{:S(2)}) collective-permute-start(bf16[64,576]{1,0:T(8,128)(2,1)S(1)} %get-tuple-element.32.refs_4_), channel_id=1, source_target_pairs={{0,8},{4,12},{8,0},{12,4},{16,24},{20,28},{24,16},{28,20},{1,9},{5... | collective-permute-start | bytes 221192 | tf_op jit(solution)/shard_map/ppermute | solution.py:40
  28.3 0.0 collective-permute-done.10.refs_1_
  28.3 1.2 %collective-permute-start.14 = (bf16[64,576]{1,0:T(8,128)(2,1)S(1)}, bf16[64,576]{1,0:T(8,128)(2,1)S(1)}, u32[]{:S(2)}, u32[]{:S(2)}) collective-permute-start(bf16[64,576]{1,0:T(8,128)(2,1)S(1)} %get-tuple-element.32.refs_4_), channel_id=1, source_target_pairs={{0,16},{4,20},{8,24},{12,28},{16,0},{20,4},{24,8},{28,12},{1,17},{... | collective-permute-start | bytes 221192 | tf_op jit(solution)/shard_map/ppermute | solution.py:40
  29.5 1.1 %collective-permute-done.11.refs_2_ = bf16[2,2,64,256]{3,2,1,0:T(8,128)(2,1)S(1)} collective-permute-done((bf16[2,2,64,256]{3,2,1,0:T(8,128)(2,1)S(1)}, bf16[2,2,64,256]{3,2,1,0:T(8,128)(2,1)S(1)}, u32[]{:S(2)}, u32[]{:S(2)}) %collective-permute-start.11) | collective-permute-done | bytes 131104 | tf_op jit(solution)/shard_map/ppermute | solution.py:40
  30.6 1.6 %collective-permute-start.15 = (bf16[64,576]{1,0:T(8,128)(2,1)S(1)}, bf16[64,576]{1,0:T(8,128)(2,1)S(1)}, u32[]{:S(2)}, u32[]{:S(2)}) collective-permute-start(bf16[64,576]{1,0:T(8,128)(2,1)S(1)} %get-tuple-element.32.refs_4_), channel_id=1, source_target_pairs={{0,24},{4,28},{8,16},{12,20},{16,8},{20,12},{24,0},{28,4},{1,25},{... | collective-permute-start | bytes 221192 | tf_op jit(solution)/shard_map/ppermute | solution.py:40
  32.2 0.0 collective-permute-done.12.refs_3_
  32.2 2.2 %collective-permute-start.8 = (bf16[8,16,256]{2,1,0:T(8,128)(2,1)S(1)}, bf16[8,16,256]{2,1,0:T(8,128)(2,1)S(1)}, u32[]{:S(2)}, u32[]{:S(2)}) collective-permute-start(bf16[8,16,256]{2,1,0:T(8,128)(2,1)S(1)} %get-tuple-element.26), channel_id=1, source_target_pairs={{0,2},{1,3},{2,0},{3,1},{4,6},{5,7},{6,4},{7,5},{8,10},{9,11},{10,... | collective-permute-start | bytes 196616 | tf_op jit(solution)/shard_map/ppermute | solution.py:40
  34.4 0.0 collective-permute-done.7.refs_2_.refs_8_
  34.4 1.7 %collective-permute-start.9 = (bf16[8,16,256]{2,1,0:T(8,128)(2,1)S(1)}, bf16[8,16,256]{2,1,0:T(8,128)(2,1)S(1)}, u32[]{:S(2)}, u32[]{:S(2)}) collective-permute-start(bf16[8,16,256]{2,1,0:T(8,128)(2,1)S(1)} %get-tuple-element.27), channel_id=1, source_target_pairs={{0,3},{1,2},{2,1},{3,0},{4,7},{5,6},{6,5},{7,4},{8,11},{9,10},{10,... | collective-permute-start | bytes 196616 | tf_op jit(solution)/shard_map/ppermute | solution.py:40
  36.1 1.6 %collective-permute-done.8.refs_3_.refs_9_ = bf16[8,16,256]{2,1,0:T(8,128)(2,1)S(1)} collective-permute-done((bf16[8,16,256]{2,1,0:T(8,128)(2,1)S(1)}, bf16[8,16,256]{2,1,0:T(8,128)(2,1)S(1)}, u32[]{:S(2)}, u32[]{:S(2)}) %collective-permute-start.8) | collective-permute-done | bytes 65568 | tf_op jit(solution)/shard_map/ppermute | solution.py:40
  37.8 2.8 %collective-permute-done.9.refs_4_.refs_10_ = bf16[8,16,256]{2,1,0:T(8,128)(2,1)S(1)} collective-permute-done((bf16[8,16,256]{2,1,0:T(8,128)(2,1)S(1)}, bf16[8,16,256]{2,1,0:T(8,128)(2,1)S(1)}, u32[]{:S(2)}, u32[]{:S(2)}) %collective-permute-start.9) | collective-permute-done | bytes 65568 | tf_op jit(solution)/shard_map/ppermute | solution.py:40
  40.6 0.0 collective-permute-done.13.refs_5_
  40.6 0.0 collective-permute-done.14.refs_6_
  40.6 0.0 collective-permute-done.15.refs_7_
  40.6 0.4 shard_map.116
  41.0 0.1 collective-permute-start.16
  41.0 1.1 %shard_map.114 = bf16[128,2048]{1,0:T(8,128)(2,1)} custom-call(bf16[1,16,128]{2,1,0:T(8,128)(2,1)S(1)} %get-tuple-element.21.refs_0_, bf16[8,16,256]{2,1,0:T(8,128)(2,1)S(1)} %get-tuple-element.24.refs_1_, bf16[8,16,256]{2,1,0:T(8,128)(2,1)S(1)} %collective-permute-done.7.refs_2_.refs_8_, bf16[8,16,256]{2,1,0:T(8,128)(2,1)S(1)} %collective-permute-done.8.refs_3_.refs_9_, ...), custom_call_target="tpu_custom_call" | custom-call | tf_op jit(solution)/shard_map/pallas_call | solution.py:27
  42.2 0.4 collective-permute-done.16.refs_1_
  42.6 0.9 %shard_map.117 = (f32[192,256]{1,0:T(8,128)}, f32[192,256]{1,0:T(8,128)}, f32[192,256]{1,0:T(8,128)}) custom-call(f32[576,256]{1,0:T(8,128)S(1)} %get-tuple-element.33.refs_0_, bf16[576,256]{1,0:T(8,128)(2,1)S(1)} %collective-permute-done.16.refs_1_), custom_call_target="tpu_custom_call" | custom-call | tf_op jit(solution)/shard_map/pallas_call | solution.py:27
Async XLA Ops:
  2.3 18.1 %collective-permute-start.3 = (bf16[576,256]{1,0:T(8,128)(2,1)S(1)}, bf16[576,256]{1,0:T(8,128)(2,1)S(1)}, u32[]{:S(2)}, u32[]{:S(2)}) collective-permute-start(bf16[576,256]{1,0:T(8,128)(2,1)S(1)} %get-tuple-element.23.refs_0_), channel_id=1, source_target_pairs={{0,8},{4,12},{8,0},{12,4},{16,24},{20,28},{24,16},{28,20},{1,9},{5... | collective-permute-start | bytes 884744 | tf_op jit(solution)/shard_map/ppermute | solution.py:40
  5.3 15.1 %collective-permute-start.4 = (bf16[576,256]{1,0:T(8,128)(2,1)S(1)}, bf16[576,256]{1,0:T(8,128)(2,1)S(1)}, u32[]{:S(2)}, u32[]{:S(2)}) collective-permute-start(bf16[576,256]{1,0:T(8,128)(2,1)S(1)} %get-tuple-element.23.refs_0_), channel_id=1, source_target_pairs={{0,16},{4,20},{8,24},{12,28},{16,0},{20,4},{24,8},{28,12},{1,17},{... | collective-permute-start | bytes 884744 | tf_op jit(solution)/shard_map/ppermute | solution.py:40
  6.9 13.6 %collective-permute-start.5 = (bf16[576,256]{1,0:T(8,128)(2,1)S(1)}, bf16[576,256]{1,0:T(8,128)(2,1)S(1)}, u32[]{:S(2)}, u32[]{:S(2)}) collective-permute-start(bf16[576,256]{1,0:T(8,128)(2,1)S(1)} %get-tuple-element.23.refs_0_), channel_id=1, source_target_pairs={{0,24},{4,28},{8,16},{12,20},{16,8},{20,12},{24,0},{28,4},{1,25},{... | collective-permute-start | bytes 884744 | tf_op jit(solution)/shard_map/ppermute | solution.py:40
  6.9 8.6 %collective-permute-start.1 = (bf16[2,8,16,256]{3,2,1,0:T(8,128)(2,1)S(1)}, bf16[2,8,16,256]{3,2,1,0:T(8,128)(2,1)S(1)}, u32[]{:S(2)}, u32[]{:S(2)}) collective-permute-start(bf16[2,8,16,256]{3,2,1,0:T(8,128)(2,1)S(1)} %bitcast.8), channel_id=1, source_target_pairs={{0,2},{1,3},{2,0},{3,1},{4,6},{5,7},{6,4},{7,5},{8,10},{9,11},{10,... | collective-permute-start | bytes 393224 | tf_op jit(solution)/shard_map/ppermute | solution.py:40
  9.9 6.2 %collective-permute-start = (bf16[2,8,16,256]{3,2,1,0:T(8,128)(2,1)S(1)}, bf16[2,8,16,256]{3,2,1,0:T(8,128)(2,1)S(1)}, u32[]{:S(2)}, u32[]{:S(2)}) collective-permute-start(bf16[2,8,16,256]{3,2,1,0:T(8,128)(2,1)S(1)} %bitcast.9), channel_id=1, source_target_pairs={{0,1},{1,0},{2,3},{3,2},{4,5},{5,4},{6,7},{7,6},{8,9},{9,8},{10,11... | collective-permute-start | bytes 393224 | tf_op jit(solution)/shard_map/ppermute | solution.py:40
  15.5 5.0 %collective-permute-start.2 = (bf16[2,8,16,256]{3,2,1,0:T(8,128)(2,1)S(1)}, bf16[2,8,16,256]{3,2,1,0:T(8,128)(2,1)S(1)}, u32[]{:S(2)}, u32[]{:S(2)}) collective-permute-start(bf16[2,8,16,256]{3,2,1,0:T(8,128)(2,1)S(1)} %collective-permute-done.1.refs_5_.refs_2_), channel_id=1, source_target_pairs={{0,1},{1,0},{2,3},{3,2},{4,5},{5,4},{6,7},{7,6},{8,9},{9,8},{10,11... | collective-permute-start | bytes 393224 | tf_op jit(solution)/shard_map/ppermute | solution.py:40
  20.6 3.7 %collective-permute-start.6 = (bf16[4,576,256]{2,1,0:T(8,128)(2,1)S(1)}, bf16[4,576,256]{2,1,0:T(8,128)(2,1)S(1)}, u32[]{:S(2)}, u32[]{:S(2)}) collective-permute-start(bf16[4,576,256]{2,1,0:T(8,128)(2,1)S(1)} %shard_map.112.refs_4_), channel_id=1, source_target_pairs={{0,4},{4,0},{8,12},{12,8},{16,20},{20,16},{24,28},{28,24},{1,5},{5... | collective-permute-start | bytes 3538952 | tf_op jit(solution)/shard_map/ppermute | solution.py:40
  20.7 7.6 %collective-permute-start.10 = (bf16[2,2,64,256]{3,2,1,0:T(8,128)(2,1)S(1)}, bf16[2,2,64,256]{3,2,1,0:T(8,128)(2,1)S(1)}, u32[]{:S(2)}, u32[]{:S(2)}) collective-permute-start(bf16[2,2,64,256]{3,2,1,0:T(8,128)(2,1)S(1)} %get-tuple-element.29), channel_id=1, source_target_pairs={{0,8},{4,12},{8,0},{12,4},{16,24},{20,28},{24,16},{28,20},{1,9},{5... | collective-permute-start | bytes 393224 | tf_op jit(solution)/shard_map/ppermute | solution.py:40
  22.3 8.3 %collective-permute-start.11 = (bf16[2,2,64,256]{3,2,1,0:T(8,128)(2,1)S(1)}, bf16[2,2,64,256]{3,2,1,0:T(8,128)(2,1)S(1)}, u32[]{:S(2)}, u32[]{:S(2)}) collective-permute-start(bf16[2,2,64,256]{3,2,1,0:T(8,128)(2,1)S(1)} %get-tuple-element.30), channel_id=1, source_target_pairs={{0,16},{4,20},{8,24},{12,28},{16,0},{20,4},{24,8},{28,12},{1,17},{... | collective-permute-start | bytes 393224 | tf_op jit(solution)/shard_map/ppermute | solution.py:40
  23.8 8.4 %collective-permute-start.12 = (bf16[2,2,64,256]{3,2,1,0:T(8,128)(2,1)S(1)}, bf16[2,2,64,256]{3,2,1,0:T(8,128)(2,1)S(1)}, u32[]{:S(2)}, u32[]{:S(2)}) collective-permute-start(bf16[2,2,64,256]{3,2,1,0:T(8,128)(2,1)S(1)} %get-tuple-element.31), channel_id=1, source_target_pairs={{0,24},{4,28},{8,16},{12,20},{16,8},{20,12},{24,0},{28,4},{1,25},{... | collective-permute-start | bytes 393224 | tf_op jit(solution)/shard_map/ppermute | solution.py:40
  25.8 8.6 %collective-permute-start.7 = (bf16[8,16,256]{2,1,0:T(8,128)(2,1)S(1)}, bf16[8,16,256]{2,1,0:T(8,128)(2,1)S(1)}, u32[]{:S(2)}, u32[]{:S(2)}) collective-permute-start(bf16[8,16,256]{2,1,0:T(8,128)(2,1)S(1)} %get-tuple-element.25), channel_id=1, source_target_pairs={{0,1},{1,0},{2,3},{3,2},{4,5},{5,4},{6,7},{7,6},{8,9},{9,8},{10,11... | collective-permute-start | bytes 196616 | tf_op jit(solution)/shard_map/ppermute | solution.py:40
  27.1 13.5 %collective-permute-start.13 = (bf16[64,576]{1,0:T(8,128)(2,1)S(1)}, bf16[64,576]{1,0:T(8,128)(2,1)S(1)}, u32[]{:S(2)}, u32[]{:S(2)}) collective-permute-start(bf16[64,576]{1,0:T(8,128)(2,1)S(1)} %get-tuple-element.32.refs_4_), channel_id=1, source_target_pairs={{0,8},{4,12},{8,0},{12,4},{16,24},{20,28},{24,16},{28,20},{1,9},{5... | collective-permute-start | bytes 221192 | tf_op jit(solution)/shard_map/ppermute | solution.py:40
  28.3 12.3 %collective-permute-start.14 = (bf16[64,576]{1,0:T(8,128)(2,1)S(1)}, bf16[64,576]{1,0:T(8,128)(2,1)S(1)}, u32[]{:S(2)}, u32[]{:S(2)}) collective-permute-start(bf16[64,576]{1,0:T(8,128)(2,1)S(1)} %get-tuple-element.32.refs_4_), channel_id=1, source_target_pairs={{0,16},{4,20},{8,24},{12,28},{16,0},{20,4},{24,8},{28,12},{1,17},{... | collective-permute-start | bytes 221192 | tf_op jit(solution)/shard_map/ppermute | solution.py:40
  30.6 9.9 %collective-permute-start.15 = (bf16[64,576]{1,0:T(8,128)(2,1)S(1)}, bf16[64,576]{1,0:T(8,128)(2,1)S(1)}, u32[]{:S(2)}, u32[]{:S(2)}) collective-permute-start(bf16[64,576]{1,0:T(8,128)(2,1)S(1)} %get-tuple-element.32.refs_4_), channel_id=1, source_target_pairs={{0,24},{4,28},{8,16},{12,20},{16,8},{20,12},{24,0},{28,4},{1,25},{... | collective-permute-start | bytes 221192 | tf_op jit(solution)/shard_map/ppermute | solution.py:40
  32.2 5.6 %collective-permute-start.8 = (bf16[8,16,256]{2,1,0:T(8,128)(2,1)S(1)}, bf16[8,16,256]{2,1,0:T(8,128)(2,1)S(1)}, u32[]{:S(2)}, u32[]{:S(2)}) collective-permute-start(bf16[8,16,256]{2,1,0:T(8,128)(2,1)S(1)} %get-tuple-element.26), channel_id=1, source_target_pairs={{0,2},{1,3},{2,0},{3,1},{4,6},{5,7},{6,4},{7,5},{8,10},{9,11},{10,... | collective-permute-start | bytes 196616 | tf_op jit(solution)/shard_map/ppermute | solution.py:40
  34.4 6.2 %collective-permute-start.9 = (bf16[8,16,256]{2,1,0:T(8,128)(2,1)S(1)}, bf16[8,16,256]{2,1,0:T(8,128)(2,1)S(1)}, u32[]{:S(2)}, u32[]{:S(2)}) collective-permute-start(bf16[8,16,256]{2,1,0:T(8,128)(2,1)S(1)} %get-tuple-element.27), channel_id=1, source_target_pairs={{0,3},{1,2},{2,1},{3,0},{4,7},{5,6},{6,5},{7,4},{8,11},{9,10},{10,... | collective-permute-start | bytes 196616 | tf_op jit(solution)/shard_map/ppermute | solution.py:40
  41.0 1.6 %collective-permute-start.16 = (bf16[576,256]{1,0:T(8,128)(2,1)S(1)}, bf16[576,256]{1,0:T(8,128)(2,1)S(1)}, u32[]{:S(2)}, u32[]{:S(2)}) collective-permute-start(bf16[576,256]{1,0:T(8,128)(2,1)S(1)} %get-tuple-element.34), channel_id=1, source_target_pairs={{0,4},{4,0},{8,12},{12,8},{16,20},{20,16},{24,28},{28,24},{1,5},{5... | collective-permute-start | bytes 884744 | tf_op jit(solution)/shard_map/ppermute | solution.py:40

commit v2 on v1

v2 whole, which is shorter than its diff:
```python
import functools

import jax
import jax.numpy as jnp
from jax import lax
from jax.experimental import pallas as pl
from jax.experimental.pallas import tpu as pltpu
from jax.sharding import PartitionSpec as P

SPLIT = 4
CAP = 16
SINGLE = 3
VMEM_LIMIT = 48 * 1024 * 1024

CONTRACT_LAST = (((1,), (1,)), ((), ()))
CONTRACT_FIRST = (((0,), (0,)), ((), ()))
PLAIN = (((1,), (0,)), ((), ()))


def dot(left, right, dims):
    return lax.dot_general(left, right, dims, preferred_element_type=jnp.float32)


def call(kernel, out_shape, args, after=(), flops=0):
    def run(*refs):
        kernel(*refs[: len(args)], *refs[len(args) + len(after) :])

    return pl.pallas_call(
        run,
        out_shape=out_shape,
        in_specs=[pl.BlockSpec(memory_space=pltpu.VMEM)] * len(args)
        + [pl.BlockSpec(memory_space=pl.ANY)] * len(after),
        out_specs=jax.tree.map(lambda _: pl.BlockSpec(memory_space=pltpu.VMEM), out_shape),
        compiler_params=pltpu.CompilerParams(vmem_limit_bytes=VMEM_LIMIT),
        cost_estimate=pl.CostEstimate(flops=flops, bytes_accessed=0, transcendentals=0),
    )(*args, *after)


def swap(values, axis, shift):
    size = lax.axis_size(axis)
    return lax.ppermute(values, axis, [(i, i ^ shift) for i in range(size)])


def cross(values, pair):
    size = lax.axis_size("dp")
    return lax.ppermute(values, "dp", [(i, i ^ (2 * pair[i % 2])) for i in range(size)])


def begin_kernel(
    ids_hbm, mask_hbm, gate_hbm, tok_hbm, cot_hbm, gate_w_hbm, up_w_hbm, down_w_hbm,
    rows_ref, hot_ref, stack_ref,
    ids_ref, mask_ref, gate_ref, tok_ref, cot_ref, sems,
):
    flight, _, blocks, cap, width = rows_ref.shape
    hidden = gate_w_hbm.shape[0]
    pairs = [
        (ids_hbm, ids_ref),
        (mask_hbm, mask_ref),
        (gate_hbm, gate_ref),
        (tok_hbm, tok_ref),
        (cot_hbm, cot_ref),
        (gate_w_hbm, stack_ref.at[pl.ds(0, hidden)]),
        (up_w_hbm, stack_ref.at[pl.ds(hidden, hidden)]),
        (down_w_hbm, stack_ref.at[pl.ds(2 * hidden, hidden)]),
    ]
    copies = [
        pltpu.make_async_copy(source, target, sems.at[i])
        for i, (source, target) in enumerate(pairs)
    ]
    for copy in copies:
        copy.start()
    count = ids_ref.shape[1]
    earlier = (
        lax.broadcasted_iota(jnp.int32, (count, count), 0)
        < lax.broadcasted_iota(jnp.int32, (count, count), 1)
    ).astype(jnp.bfloat16)
    slot = lax.broadcasted_iota(jnp.int32, (cap, count), 0).astype(jnp.float32)
    for copy in copies[:3]:
        copy.wait()
    live = mask_ref[...] == 1
    gates = []
    for j in range(flight):
        hit = jnp.where((ids_ref[...] == j) & live, 1.0, 0.0)
        held = jnp.sum(hit, axis=0, keepdims=True)
        rank = jnp.sum(dot(hit.astype(jnp.bfloat16), earlier, PLAIN), axis=0, keepdims=True)
        gate = jnp.sum(hit * gate_ref[...], axis=0, keepdims=True)
        hot = jnp.where((slot == rank) & (held > 0.0), 1.0, 0.0)
        gates.append(jnp.sum(hot * gate, axis=1, keepdims=True))
        hot_ref[j] = hot.astype(jnp.bfloat16)
    for copy in copies[3:5]:
        copy.wait()
    for j in range(flight):
        picked = dot(hot_ref[j], tok_ref[...], PLAIN).astype(jnp.bfloat16)
        graded = (gates[j] * dot(hot_ref[j], cot_ref[...], PLAIN)).astype(jnp.bfloat16)
        for b in range(blocks):
            rows_ref[j, 0, b] = picked[:, b * width : (b + 1) * width]
            rows_ref[j, 1, b] = graded[:, b * width : (b + 1) * width]
    for copy in copies[5:]:
        copy.wait()


def join_kernel(*refs):
    out_ref, low = refs[-1], 0
    for ref in refs[:-1]:
        out_ref[low : low + ref.shape[0]] = ref[...]
        low += ref.shape[0]


def join_rows_kernel(first_ref, second_ref, out_ref):
    size = first_ref.shape[2]
    out_ref[:, :, :size] = first_ref[...]
    out_ref[:, :, size:] = second_ref[...]


def rows_of(row_refs, kind, block):
    return jnp.concatenate([r[kind, block] for r in row_refs], axis=0)


def own_shift(me, pair):
    first = lax.rem(me, 2) == 0
    return [2 * jnp.where(first, pair[i], pair[1 - i]) for i in range(2)]


def repack_kernel(chunks, pairs, *refs):
    me = lax.axis_index("dp")
    shifts = [0, 2 * SINGLE]
    for pair in pairs:
        mine, other = own_shift(me, pair)
        shifts += [mine, other ^ 1]
    for shift, out_ref in zip(shifts, refs[chunks:]):
        for kind in range(2):
            for k in range(2):
                out_ref[kind, k] = rows_of(refs[:chunks], kind, me ^ shift ^ k)


def expert_kernel(chunks, *refs):
    row_refs, (half_ref, other_ref, grads_ref) = refs[:chunks], refs[chunks : chunks + 3]
    near_part_ref, far_part_ref = refs[chunks + 3 :]
    flight = chunks // SPLIT
    me = lax.axis_index("dp")
    weights = []
    for i in range(half_ref.shape[0]):
        weights += [(half_ref.at[i], me ^ (2 * i)), (other_ref.at[i], me ^ (2 * i + 1))]
    hidden = half_ref.shape[1] // 3
    pre_gate, pre_up, grad_act = 0.0, 0.0, 0.0
    for weight_ref, block in weights:
        rows_in = rows_of(row_refs, 0, block)
        pre_gate += dot(rows_in, weight_ref[:hidden], CONTRACT_LAST)
        pre_up += dot(rows_in, weight_ref[hidden : 2 * hidden], CONTRACT_LAST)
        grad_act += dot(rows_of(row_refs, 1, block), weight_ref[2 * hidden :], CONTRACT_LAST)
    sigmoid_value = lax.logistic(pre_gate)
    silu_value = pre_gate * sigmoid_value
    slope = sigmoid_value * (1.0 + pre_gate * (1.0 - sigmoid_value))
    grad_gate_pre = (grad_act * pre_up * slope).astype(jnp.bfloat16)
    grad_up_pre = (grad_act * silu_value).astype(jnp.bfloat16)
    activated = (silu_value * pre_up).astype(jnp.bfloat16)
    grads_ref[...] = jnp.concatenate([grad_gate_pre, grad_up_pre, activated], axis=1)
    for weight_ref, block in weights:
        part = dot(grad_gate_pre, weight_ref[:hidden], PLAIN)
        part += dot(grad_up_pre, weight_ref[hidden : 2 * hidden], PLAIN)
        part = part.astype(jnp.bfloat16)
        for j in range(flight):
            for half, first in ((0, 0), (flight, 2)):
                low = (SPLIT * j + first) * CAP
                near_part_ref[half + j, block] = part[low : low + CAP]
                far_part_ref[half + j, block] = part[low + CAP : low + 2 * CAP]


def weight_grad_kernel(sibling, *refs):
    out_ref, half = refs[-1], (len(refs) - 1) // 2
    row_refs, grad_refs = refs[:half], refs[half:-1]
    hidden = out_ref.shape[0] // 3
    grads = jnp.concatenate([g[...] for g in grad_refs], axis=0)
    rows_in = jnp.concatenate([r[0, sibling] for r in row_refs], axis=0)
    rows_grad = jnp.concatenate([r[1, sibling] for r in row_refs], axis=0)
    pair = dot(grads[:, : 2 * hidden], rows_in, CONTRACT_FIRST)
    down = dot(grads[:, 2 * hidden :], rows_grad, CONTRACT_FIRST)
    out_ref[: 2 * hidden] = pair.astype(out_ref.dtype)
    out_ref[2 * hidden :] = down.astype(out_ref.dtype)


def add_kernel(near_ref, far_ref, out_ref):
    half = out_ref.shape[0]
    total = near_ref[half:].astype(jnp.float32) + far_ref[half:].astype(jnp.float32)
    out_ref[...] = total.astype(out_ref.dtype)


def sum_kernel(near_ref, far_ref, pair_ref, out_ref):
    half = out_ref.shape[0]
    total = near_ref[:half].astype(jnp.float32) + far_ref[:half].astype(jnp.float32)
    out_ref[...] = (total + pair_ref[...].astype(jnp.float32)).astype(out_ref.dtype)


def finish_kernel(chunks, own_ref, other_ref, hot_ref, *refs):
    part_refs, refs = refs[:chunks], refs[chunks:]
    out_hbm, *grad_hbm = refs[:4]
    out_ref, grad_ref, sems = refs[4:]
    hidden = grad_hbm[0].shape[0]
    copies = []

    def send(source, target):
        copies.append(pltpu.make_async_copy(source, target, sems.at[len(copies)]))
        copies[-1].start()

    for i, hbm in enumerate(grad_hbm):
        part = pl.ds(i * hidden, hidden)
        grad_ref[part] = own_ref[part] + other_ref[part].astype(jnp.float32)
        send(grad_ref.at[part], hbm)
    flight = hot_ref.shape[0]
    blocks, _, width = part_refs[0].shape[-3:]
    step = blocks * width // 4
    home = lax.axis_index("expert") // SPLIT
    for b in range(blocks):
        total = 0.0
        for j in range(flight):
            if flight == 1:
                near_ref, far_ref, pair_ref = part_refs
                summed = near_ref[0, b].astype(jnp.float32) + far_ref[0, b].astype(jnp.float32)
                summed = (summed + pair_ref[0, b].astype(jnp.float32)).astype(jnp.bfloat16)
            else:
                summed = part_refs[j][b]
            total += dot(hot_ref[home ^ j], summed, CONTRACT_FIRST)
        out_ref[:, b * width : (b + 1) * width] = total.astype(out_ref.dtype)
        if (b + 1) * width % step == 0:
            columns = pl.ds((b + 1) * width - step, step)
            send(out_ref.at[:, columns], out_hbm.at[:, columns])
    for copy in copies:
        copy.wait()


def body(tokens, cotangent, expert_ids, drop_mask, gate_table, gate_weight, up_weight, down_weight):
    chunks = lax.axis_size("expert")
    blocks = lax.axis_size("dp")
    flight = chunks // SPLIT
    count, model_width = tokens.shape
    width = model_width // blocks
    hidden = gate_weight.shape[1]
    rows = chunks * CAP
    struct = jax.ShapeDtypeStruct

    chips = blocks // 2
    dma = pltpu.SemaphoreType.DMA
    operands = (
        expert_ids.T, drop_mask.T, gate_table.T, tokens, cotangent,
        gate_weight.T, up_weight.T, down_weight,
    )
    own_rows, hot, own_weights = pl.pallas_call(
        begin_kernel,
        out_shape=(
            struct((flight, 2, blocks, CAP, width), jnp.bfloat16),
            struct((flight, CAP, count), jnp.bfloat16),
            struct((3 * hidden, width), jnp.bfloat16),
        ),
        in_specs=[pl.BlockSpec(memory_space=pltpu.HBM)] * 8,
        out_specs=(pl.BlockSpec(memory_space=pltpu.VMEM),) * 3,
        scratch_shapes=[pltpu.VMEM(v.shape, v.dtype) for v in operands[:5]] + [dma((8,))],
        compiler_params=pltpu.CompilerParams(vmem_limit_bytes=VMEM_LIMIT),
    )(*[pltpu.with_memory_space_constraint(v, pltpu.HBM) for v in operands])
    me = lax.axis_index("expert")

    def rows_for(c):
        if flight == 1:
            return own_rows[0]
        return lax.dynamic_index_in_dim(own_rows, (me ^ c) // SPLIT, 0, keepdims=False)

    arrived = [rows_for(0)]
    for c in range(1, chunks):
        if c % SPLIT == 3:
            arrived.append(swap(arrived[c - 1], "expert", 1))
        else:
            arrived.append(swap(rows_for(c), "expert", c))
    pairs = [(1, 2)] + [(i, i + 1) for i in range(4, chips, 2)]
    shards = [swap(own_weights, "dp", 2 * i) for i in reversed(range(1, chips))]
    half = call(
        join_kernel,
        struct((chips, 3 * hidden, width), jnp.bfloat16),
        [v[None] for v in (own_weights, *shards[::-1])],
        after=arrived[1:],
    )
    other_half = swap(half, "dp", 1)
    rows_shape = (2, 2, rows, width)
    own_block, single_block, *packed = call(
        functools.partial(repack_kernel, chunks, pairs),
        [struct(rows_shape, jnp.bfloat16)] * (2 + 2 * len(pairs)),
        arrived,
    )
    block_rows = [own_block, swap(single_block, "dp", 2 * SINGLE)]
    for n, pair in enumerate(pairs):
        mine, other = packed[2 * n : 2 * n + 2]
        both = call(
            join_rows_kernel,
            struct((2, 2, 2 * rows, width), jnp.bfloat16),
            (mine, swap(other, "dp", 1)),
        )
        block_rows.append(cross(both, pair))

    grads, near_parts, far_parts = call(
        functools.partial(expert_kernel, chunks),
        [struct((rows, 3 * hidden), jnp.bfloat16)]
        + [struct((2 * flight, blocks, CAP, width), jnp.bfloat16)] * 2,
        (*arrived, half, other_half),
        flops=5 * 10**9,
    )
    chip_grads = call(
        join_kernel,
        struct((2 * rows, 3 * hidden), jnp.bfloat16),
        (grads, swap(grads, "dp", 1)),
    )
    all_grads = [grads, swap(grads, "dp", 2 * SINGLE)]
    all_grads += [cross(chip_grads, pair) for pair in pairs]
    far_parts = swap(far_parts, "expert", 1)
    pair = struct((flight, blocks, CAP, width), jnp.bfloat16)
    pair_sum = call(add_kernel, pair, (near_parts, far_parts), after=block_rows[1:], flops=3 * 10**9)
    half_sum, pair_sum = pair_sum, swap(pair_sum, "expert", 2)
    returned = (near_parts, far_parts, pair_sum)
    if flight > 1:
        slot_grad = call(sum_kernel, pair, returned)
        returned = [slot_grad[0]]
        returned += [swap(slot_grad[j], "expert", SPLIT * j) for j in range(1, flight)]

    terms = (*block_rows, *all_grads)
    other_sum = call(
        functools.partial(weight_grad_kernel, 1),
        struct((3 * hidden, width), jnp.bfloat16),
        terms,
        after=(half_sum,),
        flops=10**10,
    )
    own_sum = call(
        functools.partial(weight_grad_kernel, 0),
        struct((3 * hidden, width), jnp.float32),
        terms,
        after=(other_sum,),
        flops=10**10,
    )
    other_sum = swap(other_sum, "dp", 1)
    grad_tokens, grad_gate, grad_up, grad_down = pl.pallas_call(
        functools.partial(finish_kernel, len(returned)),
        out_shape=[struct((count, model_width), jnp.bfloat16)]
        + [struct((hidden, width), jnp.float32)] * 3,
        in_specs=[pl.BlockSpec(memory_space=pltpu.VMEM)] * (3 + len(returned)),
        out_specs=[pl.BlockSpec(memory_space=pltpu.HBM)] * 4,
        scratch_shapes=[
            pltpu.VMEM((count, model_width), jnp.bfloat16),
            pltpu.VMEM((3 * hidden, width), jnp.float32),
            dma((7,)),
        ],
        compiler_params=pltpu.CompilerParams(vmem_limit_bytes=VMEM_LIMIT),
    )(own_sum, other_sum, hot, *returned)
    return grad_tokens, grad_gate.T, grad_up.T, grad_down


def solution(mesh):
    split_rows = P(("dp", "expert"), None)
    return jax.shard_map(
        body,
        mesh=mesh,
        in_specs=(split_rows,) * 5 + (P("dp", "expert"), P("dp", "expert"), P("expert", "dp")),
        out_specs=(split_rows, P("dp", "expert"), P("dp", "expert"), P("expert", "dp")),
        check_vma=False,
    )
```

time: 43.6 us -> 38.7 us (0.89)
  waiting for transfers between devices: 14.4 us -> 12.2 us
  starting transfers between devices: 22.7 us -> 20.6 us
  Pallas kernels: 5.71 us -> 5.06 us
    ppermute x17 -> x14, starting transfers between devices: 22.7 us -> 18.1 us  [swap(): return lax.ppermute(values, axis, [(i, i ^ shift) for i in range(size)])]
    ppermute x17 -> x14, waiting for transfers between devices: 14.4 us -> 11.6 us  [swap(): return lax.ppermute(values, axis, [(i, i ^ shift) for i in range(size)])]
    ppermute x0 -> x2, starting transfers between devices: none -> 2.48 us  [cross(): lax.ppermute(values, 'dp', [(i, i ^ 2 * pair[i % 2]) for i in range(size)])]
    pallas_call x6 -> x8, Pallas kernels: 4.01 us -> 2.26 us  [call(): pl.pallas_call(run, out_shape=out_shape, in_specs=[pl.BlockSpec(memory_sp...]
    pallas_call x0 -> x1, Pallas kernels: none -> 1.23 us  [body(): pl.pallas_call(functools.partial(finish_kernel, len(returned)), out_shape...]
    ppermute x0 -> x2, waiting for transfers between devices: none -> 0.57 us  [cross(): lax.ppermute(values, 'dp', [(i, i ^ 2 * pair[i % 2]) for i in range(size)])]
  transfers between devices with their start and end apart: 17 -> 16, of which waited for: 6 -> 5; matrix products, arithmetic and copies ran while one was open for 0% -> 0% of each run, Pallas kernels for 6% -> 6%
where the time goes in v2:
time: 38.7 us; the launch traced here: 38.6 us
  starting transfers between devices  20.6 us (53%)
  waiting for transfers between devices  12.2 us (32%)
  Pallas kernels  5.06 us (13%)
  between operations  0.72 us (2%)
    ppermute x14, starting transfers between devices, swap(): return lax.ppermute(values, axis, [(i, i ^ shift) for i in range(size)])  18.1 us
    ppermute x14, waiting for transfers between devices, swap(): return lax.ppermute(values, axis, [(i, i ^ shift) for i in range(size)])  11.6 us
    ppermute x2, starting transfers between devices, cross(): lax.ppermute(values, 'dp', [(i, i ^ 2 * pair[i % 2]) for i in range(size)])  2.48 us
    pallas_call x8, Pallas kernels, call(): pl.pallas_call(run, out_shape=out_shape, in_specs=[pl.BlockSpec(memory_sp...  2.26 us
    pallas_call x1, Pallas kernels, body(): pl.pallas_call(begin_kernel, out_shape=(struct((flight, 2, blocks, CAP, w...  1.58 us
    pallas_call x1, Pallas kernels, body(): pl.pallas_call(functools.partial(finish_kernel, len(returned)), out_shape...  1.23 us
  transfers between devices with their start and end apart: 16, of which 5 were waited for; matrix products, arithmetic and copies ran while one was open for 0% of the time, Pallas kernels for 6%

profile of v2, /device:TPU:0, one launch (start us, length us, event | category | flops | bytes accessed | tf_op | source)
XLA Modules:
  0.0 38.6 jit_solution(9786458207991380968)
XLA Ops:
  0.6 1.6 %shard_map.111 = (bf16[1,2,8,16,256]{4,3,2,1,0:T(8,128)(2,1)S(1)}, bf16[1,16,128]{2,1,0:T(8,128)(2,1)S(1)}, bf16[576,256]{1,0:T(8,128)(2,1)S(1)}) custom-call(s32[8,128]{1,0:T(8,128)} %bitcast.22, s32[8,128]{1,0:T(8,128)} %bitcast.23, f32[8,128]{1,0:T(8,128)} %bitcast.24, bf16[128,2048]{1,0:T(8,128)(2,1)} %tok_hbm.1, bf16[128,2048]{1,0:T(8,128)(2,1)} %cot_hbm.1, ...), custom_call_target="tpu_custom_call" | custom-call | tf_op jit(solution)/shard_map/pallas_call | solution.py:247
  2.2 3.0 %collective-permute-start.6 = (bf16[576,256]{1,0:T(8,128)(2,1)S(1)}, bf16[576,256]{1,0:T(8,128)(2,1)S(1)}, u32[]{:S(2)}, u32[]{:S(2)}) collective-permute-start(bf16[576,256]{1,0:T(8,128)(2,1)S(1)} %get-tuple-element.23), channel_id=1, source_target_pairs={{0,8},{4,12},{8,0},{12,4},{16,24},{20,28},{24,16},{28,20},{1,9},{5... | collective-permute-start | bytes 884744 | tf_op jit(solution)/shard_map/ppermute | solution.py:41
  5.2 1.5 %collective-permute-start.7 = (bf16[576,256]{1,0:T(8,128)(2,1)S(1)}, bf16[576,256]{1,0:T(8,128)(2,1)S(1)}, u32[]{:S(2)}, u32[]{:S(2)}) collective-permute-start(bf16[576,256]{1,0:T(8,128)(2,1)S(1)} %get-tuple-element.23), channel_id=1, source_target_pairs={{0,16},{4,20},{8,24},{12,28},{16,0},{20,4},{24,8},{28,12},{1,17},{... | collective-permute-start | bytes 884744 | tf_op jit(solution)/shard_map/ppermute | solution.py:41
  6.7 0.0 collective-permute-start.8
  6.8 3.0 %collective-permute-start.1 = (bf16[2,8,16,256]{3,2,1,0:T(8,128)(2,1)S(1)}, bf16[2,8,16,256]{3,2,1,0:T(8,128)(2,1)S(1)}, u32[]{:S(2)}, u32[]{:S(2)}) collective-permute-start(bf16[2,8,16,256]{3,2,1,0:T(8,128)(2,1)S(1)} %bitcast.16), channel_id=1, source_target_pairs={{0,2},{1,3},{2,0},{3,1},{4,6},{5,7},{6,4},{7,5},{8,10},{9,11},{10,... | collective-permute-start | bytes 393224 | tf_op jit(solution)/shard_map/ppermute | solution.py:41
  9.8 1.6 %collective-permute-start = (bf16[2,8,16,256]{3,2,1,0:T(8,128)(2,1)S(1)}, bf16[2,8,16,256]{3,2,1,0:T(8,128)(2,1)S(1)}, u32[]{:S(2)}, u32[]{:S(2)}) collective-permute-start(bf16[2,8,16,256]{3,2,1,0:T(8,128)(2,1)S(1)} %bitcast.17), channel_id=1, source_target_pairs={{0,1},{1,0},{2,3},{3,2},{4,5},{5,4},{6,7},{7,6},{8,9},{9,8},{10,11... | collective-permute-start | bytes 393224 | tf_op jit(solution)/shard_map/ppermute | solution.py:41
  11.4 4.0 %collective-permute-done.1.refs_2_.refs_5_ = bf16[2,8,16,256]{3,2,1,0:T(8,128)(2,1)S(1)} collective-permute-done((bf16[2,8,16,256]{3,2,1,0:T(8,128)(2,1)S(1)}, bf16[2,8,16,256]{3,2,1,0:T(8,128)(2,1)S(1)}, u32[]{:S(2)}, u32[]{:S(2)}) %collective-permute-start.1) | collective-permute-done | bytes 131104 | tf_op jit(solution)/shard_map/ppermute | solution.py:41
  15.4 0.6 %collective-permute-start.2 = (bf16[2,8,16,256]{3,2,1,0:T(8,128)(2,1)S(1)}, bf16[2,8,16,256]{3,2,1,0:T(8,128)(2,1)S(1)}, u32[]{:S(2)}, u32[]{:S(2)}) collective-permute-start(bf16[2,8,16,256]{3,2,1,0:T(8,128)(2,1)S(1)} %collective-permute-done.1.refs_2_.refs_5_), channel_id=1, source_target_pairs={{0,1},{1,0},{2,3},{3,2},{4,5},{5,4},{6,7},{7,6},{8,9},{9,8},{10,11... | collective-permute-start | bytes 393224 | tf_op jit(solution)/shard_map/ppermute | solution.py:41
  16.0 0.0 collective-permute-done.refs_1_.refs_4_
  16.0 4.3 %collective-permute-done.2.refs_3_.refs_6_ = bf16[2,8,16,256]{3,2,1,0:T(8,128)(2,1)S(1)} collective-permute-done((bf16[2,8,16,256]{3,2,1,0:T(8,128)(2,1)S(1)}, bf16[2,8,16,256]{3,2,1,0:T(8,128)(2,1)S(1)}, u32[]{:S(2)}, u32[]{:S(2)}) %collective-permute-start.2) | collective-permute-done | bytes 131104 | tf_op jit(solution)/shard_map/ppermute | solution.py:41
  20.4 0.0 collective-permute-done.6
  20.4 0.0 collective-permute-done.7
  20.4 0.0 collective-permute-done.8
  20.4 0.1 shard_map.114.refs_4_
  20.5 0.1 collective-permute-start.9
  20.6 0.5 %collective-permute-start.4 = (bf16[2,2,64,256]{3,2,1,0:T(8,128)(2,1)S(1)}, bf16[2,2,64,256]{3,2,1,0:T(8,128)(2,1)S(1)}, u32[]{:S(2)}, u32[]{:S(2)}) collective-permute-start(bf16[2,2,64,256]{3,2,1,0:T(8,128)(2,1)S(1)} %get-tuple-element.22), channel_id=1, source_target_pairs={{0,4},{4,0},{8,12},{12,8},{16,20},{20,16},{24,28},{28,24},{1,5},{5... | collective-permute-start | bytes 393224 | tf_op jit(solution)/shard_map/ppermute | solution.py:41
  21.1 2.5 %collective-permute-start.3 = (bf16[2,2,64,256]{3,2,1,0:T(8,128)(2,1)S(1)}, bf16[2,2,64,256]{3,2,1,0:T(8,128)(2,1)S(1)}, u32[]{:S(2)}, u32[]{:S(2)}) collective-permute-start(bf16[2,2,64,256]{3,2,1,0:T(8,128)(2,1)S(1)} %get-tuple-element.20), channel_id=1, source_target_pairs={{0,24},{4,28},{8,16},{12,20},{16,8},{20,12},{24,0},{28,4},{1,25},{... | collective-permute-start | bytes 393224 | tf_op jit(solution)/shard_map/ppermute | solution.py:41
  23.6 0.0 collective-permute-done.4.refs_1_
  23.7 1.5 %collective-permute-start.5 = (bf16[2,2,128,256]{3,2,1,0:T(8,128)(2,1)S(1)}, bf16[2,2,128,256]{3,2,1,0:T(8,128)(2,1)S(1)}, u32[]{:S(2)}, u32[]{:S(2)}) collective-permute-start(bf16[2,2,128,256]{3,2,1,0:T(8,128)(2,1)S(1)} %shard_map.113), channel_id=1, source_target_pairs={{0,8},{4,20},{8,0},{12,28},{16,24},{20,4},{24,16},{28,12},{1,9},{5... | collective-permute-start | bytes 786440 | tf_op jit(solution)/shard_map/ppermute | solution.py:46
  25.2 0.0 collective-permute-done.9.refs_5_
  25.2 1.5 %shard_map.115 = (bf16[64,576]{1,0:T(8,128)(2,1)S(1)}, bf16[2,8,16,256]{3,2,1,0:T(8,128)(2,1)S(1)}, bf16[2,8,16,256]{3,2,1,0:T(8,128)(2,1)S(1)}) custom-call(bf16[2,8,16,256]{3,2,1,0:T(8,128)(2,1)S(1)} %bitcast.19, bf16[2,8,16,256]{3,2,1,0:T(8,128)(2,1)S(1)} %collective-permute-done.refs_1_.refs_4_, ...), custom_call_target="tpu_custom_call" | custom-call | flops 5000000000 | tf_op jit(solution)/shard_map/pallas_call | solution.py:28
  26.7 1.0 %collective-permute-start.13 = (bf16[2,8,16,256]{3,2,1,0:T(8,128)(2,1)S(1)}, bf16[2,8,16,256]{3,2,1,0:T(8,128)(2,1)S(1)}, u32[]{:S(2)}, u32[]{:S(2)}) collective-permute-start(bf16[2,8,16,256]{3,2,1,0:T(8,128)(2,1)S(1)} %get-tuple-element.26), channel_id=1, source_target_pairs={{0,1},{1,0},{2,3},{3,2},{4,5},{5,4},{6,7},{7,6},{8,9},{9,8},{10,11... | collective-permute-start | bytes 393224 | tf_op jit(solution)/shard_map/ppermute | solution.py:41
  27.7 0.0 collective-permute-start.11
  27.7 1.7 %collective-permute-start.10 = (bf16[64,576]{1,0:T(8,128)(2,1)S(1)}, bf16[64,576]{1,0:T(8,128)(2,1)S(1)}, u32[]{:S(2)}, u32[]{:S(2)}) collective-permute-start(bf16[64,576]{1,0:T(8,128)(2,1)S(1)} %get-tuple-element.24.refs_0_.refs_3_), channel_id=1, source_target_pairs={{0,24},{4,28},{8,16},{12,20},{16,8},{20,12},{24,0},{28,4},{1,25},{... | collective-permute-start | bytes 221192 | tf_op jit(solution)/shard_map/ppermute | solution.py:41
  29.4 0.0 collective-permute-done.11.refs_1_
  29.5 1.0 %collective-permute-start.12 = (bf16[128,576]{1,0:T(8,128)(2,1)S(1)}, bf16[128,576]{1,0:T(8,128)(2,1)S(1)}, u32[]{:S(2)}, u32[]{:S(2)}) collective-permute-start(bf16[128,576]{1,0:T(8,128)(2,1)S(1)} %shard_map.116), channel_id=1, source_target_pairs={{0,8},{4,20},{8,0},{12,28},{16,24},{20,4},{24,16},{28,12},{1,9},{5... | collective-permute-start | bytes 442376 | tf_op jit(solution)/shard_map/ppermute | solution.py:46
  30.4 0.0 collective-permute-done.3.refs_2_.refs_1_
  30.4 0.0 collective-permute-done.5.refs_3_.refs_2_
  30.4 1.6 %collective-permute-done.13.refs_1_ = bf16[2,8,16,256]{3,2,1,0:T(8,128)(2,1)S(1)} collective-permute-done((bf16[2,8,16,256]{3,2,1,0:T(8,128)(2,1)S(1)}, bf16[2,8,16,256]{3,2,1,0:T(8,128)(2,1)S(1)}, u32[]{:S(2)}, u32[]{:S(2)}) %collective-permute-start.13) | collective-permute-done | bytes 131104 | tf_op jit(solution)/shard_map/ppermute | solution.py:41
  32.1 2.3 %collective-permute-start.15 = (bf16[1,8,16,256]{3,2,1,0:T(8,128)(2,1)S(1)}, bf16[1,8,16,256]{3,2,1,0:T(8,128)(2,1)S(1)}, u32[]{:S(2)}, u32[]{:S(2)}) collective-permute-start(bf16[1,8,16,256]{3,2,1,0:T(8,128)(2,1)S(1)} %shard_map.117.refs_6_), channel_id=1, source_target_pairs={{0,2},{1,3},{2,0},{3,1},{4,6},{5,7},{6,4},{7,5},{8,10},{9,11},{10,... | collective-permute-start | bytes 196616 | tf_op jit(solution)/shard_map/ppermute | solution.py:41
  34.4 0.0 collective-permute-done.10.refs_4_
  34.4 0.6 %collective-permute-done.12.refs_5_ = bf16[128,576]{1,0:T(8,128)(2,1)S(1)} collective-permute-done((bf16[128,576]{1,0:T(8,128)(2,1)S(1)}, bf16[128,576]{1,0:T(8,128)(2,1)S(1)}, u32[]{:S(2)}, u32[]{:S(2)}) %collective-permute-start.12) | collective-permute-done | bytes 147488 | tf_op jit(solution)/shard_map/ppermute | solution.py:46
  34.9 0.3 shard_map.118.refs_6_
  35.2 0.2 collective-permute-start.14
  35.4 0.3 shard_map.119.own_ref
  35.7 1.6 %collective-permute-done.15.refs_2_ = bf16[1,8,16,256]{3,2,1,0:T(8,128)(2,1)S(1)} collective-permute-done((bf16[1,8,16,256]{3,2,1,0:T(8,128)(2,1)S(1)}, bf16[1,8,16,256]{3,2,1,0:T(8,128)(2,1)S(1)}, u32[]{:S(2)}, u32[]{:S(2)}) %collective-permute-start.15) | collective-permute-done | bytes 65568 | tf_op jit(solution)/shard_map/ppermute | solution.py:41
  37.3 0.0 collective-permute-done.14.other_ref
  37.3 1.2 %shard_map.120 = (bf16[128,2048]{1,0:T(8,128)(2,1)}, f32[192,256]{1,0:T(8,128)}, f32[192,256]{1,0:T(8,128)}, f32[192,256]{1,0:T(8,128)}) custom-call(f32[576,256]{1,0:T(8,128)S(1)} %shard_map.119.own_ref, bf16[576,256]{1,0:T(8,128)(2,1)S(1)} %collective-permute-done.14.other_ref, bf16[1,16,128]{2,1,0:T(8,128)(2,1)S(1)} %get-tuple-element.27.hot_ref, ...), custom_call_target="tpu_custom_call" | custom-call | tf_op jit(solution)/shard_map/pallas_call | solution.py:337
  (4 shorter events, 0.1 us)
Async XLA Ops:
  2.2 18.1 %collective-permute-start.6 = (bf16[576,256]{1,0:T(8,128)(2,1)S(1)}, bf16[576,256]{1,0:T(8,128)(2,1)S(1)}, u32[]{:S(2)}, u32[]{:S(2)}) collective-permute-start(bf16[576,256]{1,0:T(8,128)(2,1)S(1)} %get-tuple-element.23), channel_id=1, source_target_pairs={{0,8},{4,12},{8,0},{12,4},{16,24},{20,28},{24,16},{28,20},{1,9},{5... | collective-permute-start | bytes 884744 | tf_op jit(solution)/shard_map/ppermute | solution.py:41
  5.2 15.1 %collective-permute-start.7 = (bf16[576,256]{1,0:T(8,128)(2,1)S(1)}, bf16[576,256]{1,0:T(8,128)(2,1)S(1)}, u32[]{:S(2)}, u32[]{:S(2)}) collective-permute-start(bf16[576,256]{1,0:T(8,128)(2,1)S(1)} %get-tuple-element.23), channel_id=1, source_target_pairs={{0,16},{4,20},{8,24},{12,28},{16,0},{20,4},{24,8},{28,12},{1,17},{... | collective-permute-start | bytes 884744 | tf_op jit(solution)/shard_map/ppermute | solution.py:41
  6.7 13.6 %collective-permute-start.8 = (bf16[576,256]{1,0:T(8,128)(2,1)S(1)}, bf16[576,256]{1,0:T(8,128)(2,1)S(1)}, u32[]{:S(2)}, u32[]{:S(2)}) collective-permute-start(bf16[576,256]{1,0:T(8,128)(2,1)S(1)} %get-tuple-element.23), channel_id=1, source_target_pairs={{0,24},{4,28},{8,16},{12,20},{16,8},{20,12},{24,0},{28,4},{1,25},{... | collective-permute-start | bytes 884744 | tf_op jit(solution)/shard_map/ppermute | solution.py:41
  6.8 8.6 %collective-permute-start.1 = (bf16[2,8,16,256]{3,2,1,0:T(8,128)(2,1)S(1)}, bf16[2,8,16,256]{3,2,1,0:T(8,128)(2,1)S(1)}, u32[]{:S(2)}, u32[]{:S(2)}) collective-permute-start(bf16[2,8,16,256]{3,2,1,0:T(8,128)(2,1)S(1)} %bitcast.16), channel_id=1, source_target_pairs={{0,2},{1,3},{2,0},{3,1},{4,6},{5,7},{6,4},{7,5},{8,10},{9,11},{10,... | collective-permute-start | bytes 393224 | tf_op jit(solution)/shard_map/ppermute | solution.py:41
  9.8 6.2 %collective-permute-start = (bf16[2,8,16,256]{3,2,1,0:T(8,128)(2,1)S(1)}, bf16[2,8,16,256]{3,2,1,0:T(8,128)(2,1)S(1)}, u32[]{:S(2)}, u32[]{:S(2)}) collective-permute-start(bf16[2,8,16,256]{3,2,1,0:T(8,128)(2,1)S(1)} %bitcast.17), channel_id=1, source_target_pairs={{0,1},{1,0},{2,3},{3,2},{4,5},{5,4},{6,7},{7,6},{8,9},{9,8},{10,11... | collective-permute-start | bytes 393224 | tf_op jit(solution)/shard_map/ppermute | solution.py:41
  15.4 5.0 %collective-permute-start.2 = (bf16[2,8,16,256]{3,2,1,0:T(8,128)(2,1)S(1)}, bf16[2,8,16,256]{3,2,1,0:T(8,128)(2,1)S(1)}, u32[]{:S(2)}, u32[]{:S(2)}) collective-permute-start(bf16[2,8,16,256]{3,2,1,0:T(8,128)(2,1)S(1)} %collective-permute-done.1.refs_2_.refs_5_), channel_id=1, source_target_pairs={{0,1},{1,0},{2,3},{3,2},{4,5},{5,4},{6,7},{7,6},{8,9},{9,8},{10,11... | collective-permute-start | bytes 393224 | tf_op jit(solution)/shard_map/ppermute | solution.py:41
  20.5 4.7 %collective-permute-start.9 = (bf16[4,576,256]{2,1,0:T(8,128)(2,1)S(1)}, bf16[4,576,256]{2,1,0:T(8,128)(2,1)S(1)}, u32[]{:S(2)}, u32[]{:S(2)}) collective-permute-start(bf16[4,576,256]{2,1,0:T(8,128)(2,1)S(1)} %shard_map.114.refs_4_), channel_id=1, source_target_pairs={{0,4},{4,0},{8,12},{12,8},{16,20},{20,16},{24,28},{28,24},{1,5},{5... | collective-permute-start | bytes 3538952 | tf_op jit(solution)/shard_map/ppermute | solution.py:41
  20.6 3.0 %collective-permute-start.4 = (bf16[2,2,64,256]{3,2,1,0:T(8,128)(2,1)S(1)}, bf16[2,2,64,256]{3,2,1,0:T(8,128)(2,1)S(1)}, u32[]{:S(2)}, u32[]{:S(2)}) collective-permute-start(bf16[2,2,64,256]{3,2,1,0:T(8,128)(2,1)S(1)} %get-tuple-element.22), channel_id=1, source_target_pairs={{0,4},{4,0},{8,12},{12,8},{16,20},{20,16},{24,28},{28,24},{1,5},{5... | collective-permute-start | bytes 393224 | tf_op jit(solution)/shard_map/ppermute | solution.py:41
  21.1 9.3 %collective-permute-start.3 = (bf16[2,2,64,256]{3,2,1,0:T(8,128)(2,1)S(1)}, bf16[2,2,64,256]{3,2,1,0:T(8,128)(2,1)S(1)}, u32[]{:S(2)}, u32[]{:S(2)}) collective-permute-start(bf16[2,2,64,256]{3,2,1,0:T(8,128)(2,1)S(1)} %get-tuple-element.20), channel_id=1, source_target_pairs={{0,24},{4,28},{8,16},{12,20},{16,8},{20,12},{24,0},{28,4},{1,25},{... | collective-permute-start | bytes 393224 | tf_op jit(solution)/shard_map/ppermute | solution.py:41
  23.7 6.8 %collective-permute-start.5 = (bf16[2,2,128,256]{3,2,1,0:T(8,128)(2,1)S(1)}, bf16[2,2,128,256]{3,2,1,0:T(8,128)(2,1)S(1)}, u32[]{:S(2)}, u32[]{:S(2)}) collective-permute-start(bf16[2,2,128,256]{3,2,1,0:T(8,128)(2,1)S(1)} %shard_map.113), channel_id=1, source_target_pairs={{0,8},{4,20},{8,0},{12,28},{16,24},{20,4},{24,16},{28,12},{1,9},{5... | collective-permute-start | bytes 786440 | tf_op jit(solution)/shard_map/ppermute | solution.py:46
  26.7 5.4 %collective-permute-start.13 = (bf16[2,8,16,256]{3,2,1,0:T(8,128)(2,1)S(1)}, bf16[2,8,16,256]{3,2,1,0:T(8,128)(2,1)S(1)}, u32[]{:S(2)}, u32[]{:S(2)}) collective-permute-start(bf16[2,8,16,256]{3,2,1,0:T(8,128)(2,1)S(1)} %get-tuple-element.26), channel_id=1, source_target_pairs={{0,1},{1,0},{2,3},{3,2},{4,5},{5,4},{6,7},{7,6},{8,9},{9,8},{10,11... | collective-permute-start | bytes 393224 | tf_op jit(solution)/shard_map/ppermute | solution.py:41
  27.7 1.8 %collective-permute-start.11 = (bf16[64,576]{1,0:T(8,128)(2,1)S(1)}, bf16[64,576]{1,0:T(8,128)(2,1)S(1)}, u32[]{:S(2)}, u32[]{:S(2)}) collective-permute-start(bf16[64,576]{1,0:T(8,128)(2,1)S(1)} %get-tuple-element.24.refs_0_.refs_3_), channel_id=1, source_target_pairs={{0,4},{4,0},{8,12},{12,8},{16,20},{20,16},{24,28},{28,24},{1,5},{5... | collective-permute-start | bytes 221192 | tf_op jit(solution)/shard_map/ppermute | solution.py:41
  27.7 6.7 %collective-permute-start.10 = (bf16[64,576]{1,0:T(8,128)(2,1)S(1)}, bf16[64,576]{1,0:T(8,128)(2,1)S(1)}, u32[]{:S(2)}, u32[]{:S(2)}) collective-permute-start(bf16[64,576]{1,0:T(8,128)(2,1)S(1)} %get-tuple-element.24.refs_0_.refs_3_), channel_id=1, source_target_pairs={{0,24},{4,28},{8,16},{12,20},{16,8},{20,12},{24,0},{28,4},{1,25},{... | collective-permute-start | bytes 221192 | tf_op jit(solution)/shard_map/ppermute | solution.py:41
  29.5 5.5 %collective-permute-start.12 = (bf16[128,576]{1,0:T(8,128)(2,1)S(1)}, bf16[128,576]{1,0:T(8,128)(2,1)S(1)}, u32[]{:S(2)}, u32[]{:S(2)}) collective-permute-start(bf16[128,576]{1,0:T(8,128)(2,1)S(1)} %shard_map.116), channel_id=1, source_target_pairs={{0,8},{4,20},{8,0},{12,28},{16,24},{20,4},{24,16},{28,12},{1,9},{5... | collective-permute-start | bytes 442376 | tf_op jit(solution)/shard_map/ppermute | solution.py:46
  32.1 5.2 %collective-permute-start.15 = (bf16[1,8,16,256]{3,2,1,0:T(8,128)(2,1)S(1)}, bf16[1,8,16,256]{3,2,1,0:T(8,128)(2,1)S(1)}, u32[]{:S(2)}, u32[]{:S(2)}) collective-permute-start(bf16[1,8,16,256]{3,2,1,0:T(8,128)(2,1)S(1)} %shard_map.117.refs_6_), channel_id=1, source_target_pairs={{0,2},{1,3},{2,0},{3,1},{4,6},{5,7},{6,4},{7,5},{8,10},{9,11},{10,... | collective-permute-start | bytes 196616 | tf_op jit(solution)/shard_map/ppermute | solution.py:41
  35.2 2.1 %collective-permute-start.14 = (bf16[576,256]{1,0:T(8,128)(2,1)S(1)}, bf16[576,256]{1,0:T(8,128)(2,1)S(1)}, u32[]{:S(2)}, u32[]{:S(2)}) collective-permute-start(bf16[576,256]{1,0:T(8,128)(2,1)S(1)} %shard_map.118.refs_6_), channel_id=1, source_target_pairs={{0,4},{4,0},{8,12},{12,8},{16,20},{20,16},{24,28},{28,24},{1,5},{5... | collective-permute-start | bytes 884744 | tf_op jit(solution)/shard_map/ppermute | solution.py:41

commit v3 on v2

--- a/solution.py
+++ b/solution.py
@@ -135,7 +135,7 @@
 
 def expert_kernel(chunks, *refs):
     row_refs, (half_ref, other_ref, grads_ref) = refs[:chunks], refs[chunks : chunks + 3]
-    near_part_ref, far_part_ref = refs[chunks + 3 :]
+    near_ref, direct_ref, relay_ref = refs[chunks + 3 :]
     flight = chunks // SPLIT
     me = lax.axis_index("dp")
     weights = []
@@ -160,10 +160,10 @@
         part += dot(grad_up_pre, weight_ref[hidden : 2 * hidden], PLAIN)
         part = part.astype(jnp.bfloat16)
         for j in range(flight):
-            for half, first in ((0, 0), (flight, 2)):
-                low = (SPLIT * j + first) * CAP
-                near_part_ref[half + j, block] = part[low : low + CAP]
-                far_part_ref[half + j, block] = part[low + CAP : low + 2 * CAP]
+            targets = ((near_ref, j), (direct_ref, j), (near_ref, flight + j), (relay_ref, j))
+            for c, (part_ref, n) in enumerate(targets):
+                low = (SPLIT * j + c) * CAP
+                part_ref[n, block] = part[low : low + CAP]
 
 
 def weight_grad_kernel(sibling, *refs):
@@ -179,15 +179,16 @@
     out_ref[2 * hidden :] = down.astype(out_ref.dtype)
 
 
-def add_kernel(near_ref, far_ref, out_ref):
+def add_kernel(near_ref, relay_ref, direct_ref, out_ref, direct_out_ref):
+    direct_out_ref[...] = direct_ref[...]
     half = out_ref.shape[0]
-    total = near_ref[half:].astype(jnp.float32) + far_ref[half:].astype(jnp.float32)
+    total = near_ref[half:].astype(jnp.float32) + relay_ref[...].astype(jnp.float32)
     out_ref[...] = total.astype(out_ref.dtype)
 
 
-def sum_kernel(near_ref, far_ref, pair_ref, out_ref):
+def sum_kernel(near_ref, pair_ref, direct_ref, out_ref):
     half = out_ref.shape[0]
-    total = near_ref[:half].astype(jnp.float32) + far_ref[:half].astype(jnp.float32)
+    total = near_ref[:half].astype(jnp.float32) + direct_ref[...].astype(jnp.float32)
     out_ref[...] = (total + pair_ref[...].astype(jnp.float32)).astype(out_ref.dtype)
 
 
@@ -208,22 +209,25 @@
         send(grad_ref.at[part], hbm)
     flight = hot_ref.shape[0]
     blocks, _, width = part_refs[0].shape[-3:]
-    step = blocks * width // 4
     home = lax.axis_index("expert") // SPLIT
-    for b in range(blocks):
+    hots = [hot_ref[home ^ j].astype(jnp.float32).T.astype(jnp.bfloat16) for j in range(flight)]
+
+    def slot_rows(j, b):
+        if flight > 1:
+            return part_refs[j][b]
+        near_ref, pair_ref, direct_ref = part_refs
+        total = near_ref[0, b].astype(jnp.float32) + direct_ref[0, b].astype(jnp.float32)
+        return (total + pair_ref[0, b].astype(jnp.float32)).astype(jnp.bfloat16)
+
+    step = blocks // 4
+    for first in range(0, blocks, step):
         total = 0.0
         for j in range(flight):
-            if flight == 1:
-                near_ref, far_ref, pair_ref = part_refs
-                summed = near_ref[0, b].astype(jnp.float32) + far_ref[0, b].astype(jnp.float32)
-                summed = (summed + pair_ref[0, b].astype(jnp.float32)).astype(jnp.bfloat16)
-            else:
-                summed = part_refs[j][b]
-            total += dot(hot_ref[home ^ j], summed, CONTRACT_FIRST)
-        out_ref[:, b * width : (b + 1) * width] = total.astype(out_ref.dtype)
-        if (b + 1) * width % step == 0:
-            columns = pl.ds((b + 1) * width - step, step)
-            send(out_ref.at[:, columns], out_hbm.at[:, columns])
+            rows = [slot_rows(j, b) for b in range(first, first + step)]
+            total += dot(hots[j], jnp.concatenate(rows, axis=1), PLAIN)
+        columns = pl.ds(first * width, step * width)
+        out_ref[:, columns] = total.astype(out_ref.dtype)
+        send(out_ref.at[:, columns], out_hbm.at[:, columns])
     for copy in copies:
         copy.wait()
 
@@ -294,10 +298,10 @@
         )
         block_rows.append(cross(both, pair))
 
-    grads, near_parts, far_parts = call(
+    grads, near_parts, direct, relay = call(
         functools.partial(expert_kernel, chunks),
         [struct((rows, 3 * hidden), jnp.bfloat16)]
-        + [struct((2 * flight, blocks, CAP, width), jnp.bfloat16)] * 2,
+        + [struct((n * flight, blocks, CAP, width), jnp.bfloat16) for n in (2, 1, 1)],
         (*arrived, half, other_half),
         flops=5 * 10**9,
     )
@@ -308,13 +312,18 @@
     )
     all_grads = [grads, swap(grads, "dp", 2 * SINGLE)]
     all_grads += [cross(chip_grads, pair) for pair in pairs]
-    far_parts = swap(far_parts, "expert", 1)
-    pair = struct((flight, blocks, CAP, width), jnp.bfloat16)
-    pair_sum = call(add_kernel, pair, (near_parts, far_parts), after=block_rows[1:], flops=3 * 10**9)
-    half_sum, pair_sum = pair_sum, swap(pair_sum, "expert", 2)
-    returned = (near_parts, far_parts, pair_sum)
+    part = struct((flight, blocks, CAP, width), jnp.bfloat16)
+    half_sum, direct = call(
+        add_kernel,
+        (part, part),
+        (near_parts, swap(relay, "expert", 1), direct),
+        after=block_rows[1:],
+        flops=3 * 10**9,
+    )
+    pair_sum, direct = swap(half_sum, "expert", 2), swap(direct, "expert", 1)
+    returned = (near_parts, pair_sum, direct)
     if flight > 1:
-        slot_grad = call(sum_kernel, pair, returned)
+        slot_grad = call(sum_kernel, part, returned)
         returned = [slot_grad[0]]
         returned += [swap(slot_grad[j], "expert", SPLIT * j) for j in range(1, flight)]
 

time: 38.7 us -> 39.7 us (1.026)
  starting transfers between devices: 20.6 us -> 22.3 us
  waiting for transfers between devices: 12.2 us -> 11.4 us
    ppermute x14 -> x15, starting transfers between devices: 18.1 us -> 19.8 us  [swap(): return lax.ppermute(values, axis, [(i, i ^ shift) for i in range(size)])]
    ppermute x2, waiting for transfers between devices: 0.57 us -> 0.01 us  [cross(): lax.ppermute(values, 'dp', [(i, i ^ 2 * pair[i % 2]) for i in range(size)])]
    ppermute x14 -> x15, waiting for transfers between devices: 11.6 us -> 11.4 us  [swap(): return lax.ppermute(values, axis, [(i, i ^ shift) for i in range(size)])]
  transfers between devices with their start and end apart: 16 -> 17, of which waited for: 5 -> 5; matrix products, arithmetic and copies ran while one was open for 0% -> 0% of each run, Pallas kernels for 6% -> 6%
where the time goes in v3:
time: 39.7 us; the launch traced here: 39.5 us
  starting transfers between devices  22.3 us (56%)
  waiting for transfers between devices  11.4 us (29%)
  Pallas kernels  5.08 us (13%)
  between operations  0.73 us (2%)
    ppermute x15, starting transfers between devices, swap(): return lax.ppermute(values, axis, [(i, i ^ shift) for i in range(size)])  19.8 us
    ppermute x15, waiting for transfers between devices, swap(): return lax.ppermute(values, axis, [(i, i ^ shift) for i in range(size)])  11.4 us
    ppermute x2, starting transfers between devices, cross(): lax.ppermute(values, 'dp', [(i, i ^ 2 * pair[i % 2]) for i in range(size)])  2.48 us
    pallas_call x8, Pallas kernels, call(): pl.pallas_call(run, out_shape=out_shape, in_specs=[pl.BlockSpec(memory_sp...  2.27 us
    pallas_call x1, Pallas kernels, body(): pl.pallas_call(begin_kernel, out_shape=(struct((flight, 2, blocks, CAP, w...  1.58 us
    pallas_call x1, Pallas kernels, body(): pl.pallas_call(functools.partial(finish_kernel, len(returned)), out_shape...  1.23 us
  transfers between devices with their start and end apart: 17, of which 5 were waited for; matrix products, arithmetic and copies ran while one was open for 0% of the time, Pallas kernels for 6%

profile of v3, /device:TPU:0, one launch (start us, length us, event | category | flops | bytes accessed | tf_op | source)
XLA Modules:
  0.0 39.5 jit_solution(7436129102578479987)
XLA Ops:
  0.6 1.6 %shard_map.111 = (bf16[1,2,8,16,256]{4,3,2,1,0:T(8,128)(2,1)S(1)}, bf16[1,16,128]{2,1,0:T(8,128)(2,1)S(1)}, bf16[576,256]{1,0:T(8,128)(2,1)S(1)}) custom-call(s32[8,128]{1,0:T(8,128)} %bitcast.22, s32[8,128]{1,0:T(8,128)} %bitcast.23, f32[8,128]{1,0:T(8,128)} %bitcast.24, bf16[128,2048]{1,0:T(8,128)(2,1)} %tok_hbm.1, bf16[128,2048]{1,0:T(8,128)(2,1)} %cot_hbm.1, ...), custom_call_target="tpu_custom_call" | custom-call | tf_op jit(solution)/shard_map/pallas_call | solution.py:251
  2.2 3.0 %collective-permute-start.6 = (bf16[576,256]{1,0:T(8,128)(2,1)S(1)}, bf16[576,256]{1,0:T(8,128)(2,1)S(1)}, u32[]{:S(2)}, u32[]{:S(2)}) collective-permute-start(bf16[576,256]{1,0:T(8,128)(2,1)S(1)} %get-tuple-element.26), channel_id=1, source_target_pairs={{0,8},{4,12},{8,0},{12,4},{16,24},{20,28},{24,16},{28,20},{1,9},{5... | collective-permute-start | bytes 884744 | tf_op jit(solution)/shard_map/ppermute | solution.py:41
  5.2 1.5 %collective-permute-start.7 = (bf16[576,256]{1,0:T(8,128)(2,1)S(1)}, bf16[576,256]{1,0:T(8,128)(2,1)S(1)}, u32[]{:S(2)}, u32[]{:S(2)}) collective-permute-start(bf16[576,256]{1,0:T(8,128)(2,1)S(1)} %get-tuple-element.26), channel_id=1, source_target_pairs={{0,16},{4,20},{8,24},{12,28},{16,0},{20,4},{24,8},{28,12},{1,17},{... | collective-permute-start | bytes 884744 | tf_op jit(solution)/shard_map/ppermute | solution.py:41
  6.7 0.0 collective-permute-start.8
  6.8 3.0 %collective-permute-start.1 = (bf16[2,8,16,256]{3,2,1,0:T(8,128)(2,1)S(1)}, bf16[2,8,16,256]{3,2,1,0:T(8,128)(2,1)S(1)}, u32[]{:S(2)}, u32[]{:S(2)}) collective-permute-start(bf16[2,8,16,256]{3,2,1,0:T(8,128)(2,1)S(1)} %bitcast.16), channel_id=1, source_target_pairs={{0,2},{1,3},{2,0},{3,1},{4,6},{5,7},{6,4},{7,5},{8,10},{9,11},{10,... | collective-permute-start | bytes 393224 | tf_op jit(solution)/shard_map/ppermute | solution.py:41
  9.8 1.6 %collective-permute-start = (bf16[2,8,16,256]{3,2,1,0:T(8,128)(2,1)S(1)}, bf16[2,8,16,256]{3,2,1,0:T(8,128)(2,1)S(1)}, u32[]{:S(2)}, u32[]{:S(2)}) collective-permute-start(bf16[2,8,16,256]{3,2,1,0:T(8,128)(2,1)S(1)} %bitcast.17), channel_id=1, source_target_pairs={{0,1},{1,0},{2,3},{3,2},{4,5},{5,4},{6,7},{7,6},{8,9},{9,8},{10,11... | collective-permute-start | bytes 393224 | tf_op jit(solution)/shard_map/ppermute | solution.py:41
  11.4 4.0 %collective-permute-done.1.refs_2_.refs_5_ = bf16[2,8,16,256]{3,2,1,0:T(8,128)(2,1)S(1)} collective-permute-done((bf16[2,8,16,256]{3,2,1,0:T(8,128)(2,1)S(1)}, bf16[2,8,16,256]{3,2,1,0:T(8,128)(2,1)S(1)}, u32[]{:S(2)}, u32[]{:S(2)}) %collective-permute-start.1) | collective-permute-done | bytes 131104 | tf_op jit(solution)/shard_map/ppermute | solution.py:41
  15.4 0.6 %collective-permute-start.2 = (bf16[2,8,16,256]{3,2,1,0:T(8,128)(2,1)S(1)}, bf16[2,8,16,256]{3,2,1,0:T(8,128)(2,1)S(1)}, u32[]{:S(2)}, u32[]{:S(2)}) collective-permute-start(bf16[2,8,16,256]{3,2,1,0:T(8,128)(2,1)S(1)} %collective-permute-done.1.refs_2_.refs_5_), channel_id=1, source_target_pairs={{0,1},{1,0},{2,3},{3,2},{4,5},{5,4},{6,7},{7,6},{8,9},{9,8},{10,11... | collective-permute-start | bytes 393224 | tf_op jit(solution)/shard_map/ppermute | solution.py:41
  16.0 0.0 collective-permute-done.refs_1_.refs_4_
  16.0 4.3 %collective-permute-done.2.refs_3_.refs_6_ = bf16[2,8,16,256]{3,2,1,0:T(8,128)(2,1)S(1)} collective-permute-done((bf16[2,8,16,256]{3,2,1,0:T(8,128)(2,1)S(1)}, bf16[2,8,16,256]{3,2,1,0:T(8,128)(2,1)S(1)}, u32[]{:S(2)}, u32[]{:S(2)}) %collective-permute-start.2) | collective-permute-done | bytes 131104 | tf_op jit(solution)/shard_map/ppermute | solution.py:41
  20.4 0.0 collective-permute-done.6
  20.4 0.0 collective-permute-done.7
  20.4 0.0 collective-permute-done.8
  20.4 0.1 shard_map.114.refs_4_
  20.5 0.1 collective-permute-start.9
  20.6 0.5 %collective-permute-start.4 = (bf16[2,2,64,256]{3,2,1,0:T(8,128)(2,1)S(1)}, bf16[2,2,64,256]{3,2,1,0:T(8,128)(2,1)S(1)}, u32[]{:S(2)}, u32[]{:S(2)}) collective-permute-start(bf16[2,2,64,256]{3,2,1,0:T(8,128)(2,1)S(1)} %get-tuple-element.25), channel_id=1, source_target_pairs={{0,4},{4,0},{8,12},{12,8},{16,20},{20,16},{24,28},{28,24},{1,5},{5... | collective-permute-start | bytes 393224 | tf_op jit(solution)/shard_map/ppermute | solution.py:41
  21.1 2.5 %collective-permute-start.3 = (bf16[2,2,64,256]{3,2,1,0:T(8,128)(2,1)S(1)}, bf16[2,2,64,256]{3,2,1,0:T(8,128)(2,1)S(1)}, u32[]{:S(2)}, u32[]{:S(2)}) collective-permute-start(bf16[2,2,64,256]{3,2,1,0:T(8,128)(2,1)S(1)} %get-tuple-element.23), channel_id=1, source_target_pairs={{0,24},{4,28},{8,16},{12,20},{16,8},{20,12},{24,0},{28,4},{1,25},{... | collective-permute-start | bytes 393224 | tf_op jit(solution)/shard_map/ppermute | solution.py:41
  23.6 0.0 collective-permute-done.4.refs_1_
  23.7 1.5 %collective-permute-start.5 = (bf16[2,2,128,256]{3,2,1,0:T(8,128)(2,1)S(1)}, bf16[2,2,128,256]{3,2,1,0:T(8,128)(2,1)S(1)}, u32[]{:S(2)}, u32[]{:S(2)}) collective-permute-start(bf16[2,2,128,256]{3,2,1,0:T(8,128)(2,1)S(1)} %shard_map.113), channel_id=1, source_target_pairs={{0,8},{4,20},{8,0},{12,28},{16,24},{20,4},{24,16},{28,12},{1,9},{5... | collective-permute-start | bytes 786440 | tf_op jit(solution)/shard_map/ppermute | solution.py:46
  25.2 0.0 collective-permute-done.9.refs_5_
  25.2 1.5 %shard_map.115 = (bf16[64,576]{1,0:T(8,128)(2,1)S(1)}, bf16[2,8,16,256]{3,2,1,0:T(8,128)(2,1)S(1)}, bf16[1,8,16,256]{3,2,1,0:T(8,128)(2,1)S(1)}, bf16[1,8,16,256]{3,2,1,0:T(8,128)(2,1)S(1)}) custom-call(bf16[2,8,16,256]{3,2,1,0:T(8,128)(2,1)S(1)} %bitcast.19, bf16[2,8,16,256]{3,2,1,0:T(8,128)(2,1)S(1)} %collective-permute-done.refs_1_.refs_4_, ...), custom_call_target="tpu_custom_call" | custom-call | flops 5000000000 | tf_op jit(solution)/shard_map/pallas_call | solution.py:28
  26.7 0.1 collective-permute-start.11
  26.8 1.1 %collective-permute-start.13 = (bf16[1,8,16,256]{3,2,1,0:T(8,128)(2,1)S(1)}, bf16[1,8,16,256]{3,2,1,0:T(8,128)(2,1)S(1)}, u32[]{:S(2)}, u32[]{:S(2)}) collective-permute-start(bf16[1,8,16,256]{3,2,1,0:T(8,128)(2,1)S(1)} %get-tuple-element.29), channel_id=1, source_target_pairs={{0,1},{1,0},{2,3},{3,2},{4,5},{5,4},{6,7},{7,6},{8,9},{9,8},{10,11... | collective-permute-start | bytes 196616 | tf_op jit(solution)/shard_map/ppermute | solution.py:41
  27.8 1.7 %collective-permute-start.10 = (bf16[64,576]{1,0:T(8,128)(2,1)S(1)}, bf16[64,576]{1,0:T(8,128)(2,1)S(1)}, u32[]{:S(2)}, u32[]{:S(2)}) collective-permute-start(bf16[64,576]{1,0:T(8,128)(2,1)S(1)} %get-tuple-element.27.refs_0_.refs_3_), channel_id=1, source_target_pairs={{0,24},{4,28},{8,16},{12,20},{16,8},{20,12},{24,0},{28,4},{1,25},{... | collective-permute-start | bytes 221192 | tf_op jit(solution)/shard_map/ppermute | solution.py:41
  29.5 0.0 collective-permute-done.11.refs_1_
  29.5 1.0 %collective-permute-start.12 = (bf16[128,576]{1,0:T(8,128)(2,1)S(1)}, bf16[128,576]{1,0:T(8,128)(2,1)S(1)}, u32[]{:S(2)}, u32[]{:S(2)}) collective-permute-start(bf16[128,576]{1,0:T(8,128)(2,1)S(1)} %shard_map.116), channel_id=1, source_target_pairs={{0,8},{4,20},{8,0},{12,28},{16,24},{20,4},{24,16},{28,12},{1,9},{5... | collective-permute-start | bytes 442376 | tf_op jit(solution)/shard_map/ppermute | solution.py:46
  30.5 0.0 collective-permute-done.3.refs_3_.refs_1_
  30.5 0.0 collective-permute-done.5.refs_4_.refs_2_
  30.5 0.8 %collective-permute-done.13.refs_1_ = bf16[1,8,16,256]{3,2,1,0:T(8,128)(2,1)S(1)} collective-permute-done((bf16[1,8,16,256]{3,2,1,0:T(8,128)(2,1)S(1)}, bf16[1,8,16,256]{3,2,1,0:T(8,128)(2,1)S(1)}, u32[]{:S(2)}, u32[]{:S(2)}) %collective-permute-start.13) | collective-permute-done | bytes 65568 | tf_op jit(solution)/shard_map/ppermute | solution.py:41
  31.3 2.7 %collective-permute-start.15 = (bf16[1,8,16,256]{3,2,1,0:T(8,128)(2,1)S(1)}, bf16[1,8,16,256]{3,2,1,0:T(8,128)(2,1)S(1)}, u32[]{:S(2)}, u32[]{:S(2)}) collective-permute-start(bf16[1,8,16,256]{3,2,1,0:T(8,128)(2,1)S(1)} %get-tuple-element.31.refs_6_), channel_id=1, source_target_pairs={{0,2},{1,3},{2,0},{3,1},{4,6},{5,7},{6,4},{7,5},{8,10},{9,11},{10,... | collective-permute-start | bytes 196616 | tf_op jit(solution)/shard_map/ppermute | solution.py:41
  34.0 1.4 %collective-permute-start.16 = (bf16[1,8,16,256]{3,2,1,0:T(8,128)(2,1)S(1)}, bf16[1,8,16,256]{3,2,1,0:T(8,128)(2,1)S(1)}, u32[]{:S(2)}, u32[]{:S(2)}) collective-permute-start(bf16[1,8,16,256]{3,2,1,0:T(8,128)(2,1)S(1)} %get-tuple-element.33), channel_id=1, source_target_pairs={{0,1},{1,0},{2,3},{3,2},{4,5},{5,4},{6,7},{7,6},{8,9},{9,8},{10,11... | collective-permute-start | bytes 196616 | tf_op jit(solution)/shard_map/ppermute | solution.py:41
  35.3 0.0 collective-permute-done.10.refs_4_
  35.3 0.0 collective-permute-done.12.refs_5_
  35.3 0.3 shard_map.118.refs_6_
  35.6 0.1 collective-permute-start.14
  35.7 0.3 shard_map.119.own_ref
  36.0 1.1 %collective-permute-done.15.refs_1_ = bf16[1,8,16,256]{3,2,1,0:T(8,128)(2,1)S(1)} collective-permute-done((bf16[1,8,16,256]{3,2,1,0:T(8,128)(2,1)S(1)}, bf16[1,8,16,256]{3,2,1,0:T(8,128)(2,1)S(1)}, u32[]{:S(2)}, u32[]{:S(2)}) %collective-permute-start.15) | collective-permute-done | bytes 65568 | tf_op jit(solution)/shard_map/ppermute | solution.py:41
  37.1 1.2 %collective-permute-done.16.refs_2_ = bf16[1,8,16,256]{3,2,1,0:T(8,128)(2,1)S(1)} collective-permute-done((bf16[1,8,16,256]{3,2,1,0:T(8,128)(2,1)S(1)}, bf16[1,8,16,256]{3,2,1,0:T(8,128)(2,1)S(1)}, u32[]{:S(2)}, u32[]{:S(2)}) %collective-permute-start.16) | collective-permute-done | bytes 65568 | tf_op jit(solution)/shard_map/ppermute | solution.py:41
  38.2 0.0 collective-permute-done.14.other_ref
  38.3 1.2 %shard_map.120 = (bf16[128,2048]{1,0:T(8,128)(2,1)}, f32[192,256]{1,0:T(8,128)}, f32[192,256]{1,0:T(8,128)}, f32[192,256]{1,0:T(8,128)}) custom-call(f32[576,256]{1,0:T(8,128)S(1)} %shard_map.119.own_ref, bf16[576,256]{1,0:T(8,128)(2,1)S(1)} %collective-permute-done.14.other_ref, bf16[1,16,128]{2,1,0:T(8,128)(2,1)S(1)} %get-tuple-element.32.hot_ref, ...), custom_call_target="tpu_custom_call" | custom-call | tf_op jit(solution)/shard_map/pallas_call | solution.py:346
  (4 shorter events, 0.1 us)
Async XLA Ops:
  2.2 18.1 %collective-permute-start.6 = (bf16[576,256]{1,0:T(8,128)(2,1)S(1)}, bf16[576,256]{1,0:T(8,128)(2,1)S(1)}, u32[]{:S(2)}, u32[]{:S(2)}) collective-permute-start(bf16[576,256]{1,0:T(8,128)(2,1)S(1)} %get-tuple-element.26), channel_id=1, source_target_pairs={{0,8},{4,12},{8,0},{12,4},{16,24},{20,28},{24,16},{28,20},{1,9},{5... | collective-permute-start | bytes 884744 | tf_op jit(solution)/shard_map/ppermute | solution.py:41
  5.2 15.1 %collective-permute-start.7 = (bf16[576,256]{1,0:T(8,128)(2,1)S(1)}, bf16[576,256]{1,0:T(8,128)(2,1)S(1)}, u32[]{:S(2)}, u32[]{:S(2)}) collective-permute-start(bf16[576,256]{1,0:T(8,128)(2,1)S(1)} %get-tuple-element.26), channel_id=1, source_target_pairs={{0,16},{4,20},{8,24},{12,28},{16,0},{20,4},{24,8},{28,12},{1,17},{... | collective-permute-start | bytes 884744 | tf_op jit(solution)/shard_map/ppermute | solution.py:41
  6.7 13.6 %collective-permute-start.8 = (bf16[576,256]{1,0:T(8,128)(2,1)S(1)}, bf16[576,256]{1,0:T(8,128)(2,1)S(1)}, u32[]{:S(2)}, u32[]{:S(2)}) collective-permute-start(bf16[576,256]{1,0:T(8,128)(2,1)S(1)} %get-tuple-element.26), channel_id=1, source_target_pairs={{0,24},{4,28},{8,16},{12,20},{16,8},{20,12},{24,0},{28,4},{1,25},{... | collective-permute-start | bytes 884744 | tf_op jit(solution)/shard_map/ppermute | solution.py:41
  6.8 8.6 %collective-permute-start.1 = (bf16[2,8,16,256]{3,2,1,0:T(8,128)(2,1)S(1)}, bf16[2,8,16,256]{3,2,1,0:T(8,128)(2,1)S(1)}, u32[]{:S(2)}, u32[]{:S(2)}) collective-permute-start(bf16[2,8,16,256]{3,2,1,0:T(8,128)(2,1)S(1)} %bitcast.16), channel_id=1, source_target_pairs={{0,2},{1,3},{2,0},{3,1},{4,6},{5,7},{6,4},{7,5},{8,10},{9,11},{10,... | collective-permute-start | bytes 393224 | tf_op jit(solution)/shard_map/ppermute | solution.py:41
  9.8 6.2 %collective-permute-start = (bf16[2,8,16,256]{3,2,1,0:T(8,128)(2,1)S(1)}, bf16[2,8,16,256]{3,2,1,0:T(8,128)(2,1)S(1)}, u32[]{:S(2)}, u32[]{:S(2)}) collective-permute-start(bf16[2,8,16,256]{3,2,1,0:T(8,128)(2,1)S(1)} %bitcast.17), channel_id=1, source_target_pairs={{0,1},{1,0},{2,3},{3,2},{4,5},{5,4},{6,7},{7,6},{8,9},{9,8},{10,11... | collective-permute-start | bytes 393224 | tf_op jit(solution)/shard_map/ppermute | solution.py:41
  15.4 5.0 %collective-permute-start.2 = (bf16[2,8,16,256]{3,2,1,0:T(8,128)(2,1)S(1)}, bf16[2,8,16,256]{3,2,1,0:T(8,128)(2,1)S(1)}, u32[]{:S(2)}, u32[]{:S(2)}) collective-permute-start(bf16[2,8,16,256]{3,2,1,0:T(8,128)(2,1)S(1)} %collective-permute-done.1.refs_2_.refs_5_), channel_id=1, source_target_pairs={{0,1},{1,0},{2,3},{3,2},{4,5},{5,4},{6,7},{7,6},{8,9},{9,8},{10,11... | collective-permute-start | bytes 393224 | tf_op jit(solution)/shard_map/ppermute | solution.py:41
  20.5 4.7 %collective-permute-start.9 = (bf16[4,576,256]{2,1,0:T(8,128)(2,1)S(1)}, bf16[4,576,256]{2,1,0:T(8,128)(2,1)S(1)}, u32[]{:S(2)}, u32[]{:S(2)}) collective-permute-start(bf16[4,576,256]{2,1,0:T(8,128)(2,1)S(1)} %shard_map.114.refs_4_), channel_id=1, source_target_pairs={{0,4},{4,0},{8,12},{12,8},{16,20},{20,16},{24,28},{28,24},{1,5},{5... | collective-permute-start | bytes 3538952 | tf_op jit(solution)/shard_map/ppermute | solution.py:41
  20.6 3.0 %collective-permute-start.4 = (bf16[2,2,64,256]{3,2,1,0:T(8,128)(2,1)S(1)}, bf16[2,2,64,256]{3,2,1,0:T(8,128)(2,1)S(1)}, u32[]{:S(2)}, u32[]{:S(2)}) collective-permute-start(bf16[2,2,64,256]{3,2,1,0:T(8,128)(2,1)S(1)} %get-tuple-element.25), channel_id=1, source_target_pairs={{0,4},{4,0},{8,12},{12,8},{16,20},{20,16},{24,28},{28,24},{1,5},{5... | collective-permute-start | bytes 393224 | tf_op jit(solution)/shard_map/ppermute | solution.py:41
  21.1 9.4 %collective-permute-start.3 = (bf16[2,2,64,256]{3,2,1,0:T(8,128)(2,1)S(1)}, bf16[2,2,64,256]{3,2,1,0:T(8,128)(2,1)S(1)}, u32[]{:S(2)}, u32[]{:S(2)}) collective-permute-start(bf16[2,2,64,256]{3,2,1,0:T(8,128)(2,1)S(1)} %get-tuple-element.23), channel_id=1, source_target_pairs={{0,24},{4,28},{8,16},{12,20},{16,8},{20,12},{24,0},{28,4},{1,25},{... | collective-permute-start | bytes 393224 | tf_op jit(solution)/shard_map/ppermute | solution.py:41
  23.7 6.9 %collective-permute-start.5 = (bf16[2,2,128,256]{3,2,1,0:T(8,128)(2,1)S(1)}, bf16[2,2,128,256]{3,2,1,0:T(8,128)(2,1)S(1)}, u32[]{:S(2)}, u32[]{:S(2)}) collective-permute-start(bf16[2,2,128,256]{3,2,1,0:T(8,128)(2,1)S(1)} %shard_map.113), channel_id=1, source_target_pairs={{0,8},{4,20},{8,0},{12,28},{16,24},{20,4},{24,16},{28,12},{1,9},{5... | collective-permute-start | bytes 786440 | tf_op jit(solution)/shard_map/ppermute | solution.py:46
  26.7 2.8 %collective-permute-start.11 = (bf16[64,576]{1,0:T(8,128)(2,1)S(1)}, bf16[64,576]{1,0:T(8,128)(2,1)S(1)}, u32[]{:S(2)}, u32[]{:S(2)}) collective-permute-start(bf16[64,576]{1,0:T(8,128)(2,1)S(1)} %get-tuple-element.27.refs_0_.refs_3_), channel_id=1, source_target_pairs={{0,4},{4,0},{8,12},{12,8},{16,20},{20,16},{24,28},{28,24},{1,5},{5... | collective-permute-start | bytes 221192 | tf_op jit(solution)/shard_map/ppermute | solution.py:41
  26.8 4.5 %collective-permute-start.13 = (bf16[1,8,16,256]{3,2,1,0:T(8,128)(2,1)S(1)}, bf16[1,8,16,256]{3,2,1,0:T(8,128)(2,1)S(1)}, u32[]{:S(2)}, u32[]{:S(2)}) collective-permute-start(bf16[1,8,16,256]{3,2,1,0:T(8,128)(2,1)S(1)} %get-tuple-element.29), channel_id=1, source_target_pairs={{0,1},{1,0},{2,3},{3,2},{4,5},{5,4},{6,7},{7,6},{8,9},{9,8},{10,11... | collective-permute-start | bytes 196616 | tf_op jit(solution)/shard_map/ppermute | solution.py:41
  27.8 7.5 %collective-permute-start.10 = (bf16[64,576]{1,0:T(8,128)(2,1)S(1)}, bf16[64,576]{1,0:T(8,128)(2,1)S(1)}, u32[]{:S(2)}, u32[]{:S(2)}) collective-permute-start(bf16[64,576]{1,0:T(8,128)(2,1)S(1)} %get-tuple-element.27.refs_0_.refs_3_), channel_id=1, source_target_pairs={{0,24},{4,28},{8,16},{12,20},{16,8},{20,12},{24,0},{28,4},{1,25},{... | collective-permute-start | bytes 221192 | tf_op jit(solution)/shard_map/ppermute | solution.py:41
  29.5 5.8 %collective-permute-start.12 = (bf16[128,576]{1,0:T(8,128)(2,1)S(1)}, bf16[128,576]{1,0:T(8,128)(2,1)S(1)}, u32[]{:S(2)}, u32[]{:S(2)}) collective-permute-start(bf16[128,576]{1,0:T(8,128)(2,1)S(1)} %shard_map.116), channel_id=1, source_target_pairs={{0,8},{4,20},{8,0},{12,28},{16,24},{20,4},{24,16},{28,12},{1,9},{5... | collective-permute-start | bytes 442376 | tf_op jit(solution)/shard_map/ppermute | solution.py:46
  31.3 5.7 %collective-permute-start.15 = (bf16[1,8,16,256]{3,2,1,0:T(8,128)(2,1)S(1)}, bf16[1,8,16,256]{3,2,1,0:T(8,128)(2,1)S(1)}, u32[]{:S(2)}, u32[]{:S(2)}) collective-permute-start(bf16[1,8,16,256]{3,2,1,0:T(8,128)(2,1)S(1)} %get-tuple-element.31.refs_6_), channel_id=1, source_target_pairs={{0,2},{1,3},{2,0},{3,1},{4,6},{5,7},{6,4},{7,5},{8,10},{9,11},{10,... | collective-permute-start | bytes 196616 | tf_op jit(solution)/shard_map/ppermute | solution.py:41
  34.0 4.3 %collective-permute-start.16 = (bf16[1,8,16,256]{3,2,1,0:T(8,128)(2,1)S(1)}, bf16[1,8,16,256]{3,2,1,0:T(8,128)(2,1)S(1)}, u32[]{:S(2)}, u32[]{:S(2)}) collective-permute-start(bf16[1,8,16,256]{3,2,1,0:T(8,128)(2,1)S(1)} %get-tuple-element.33), channel_id=1, source_target_pairs={{0,1},{1,0},{2,3},{3,2},{4,5},{5,4},{6,7},{7,6},{8,9},{9,8},{10,11... | collective-permute-start | bytes 196616 | tf_op jit(solution)/shard_map/ppermute | solution.py:41
  35.6 2.6 %collective-permute-start.14 = (bf16[576,256]{1,0:T(8,128)(2,1)S(1)}, bf16[576,256]{1,0:T(8,128)(2,1)S(1)}, u32[]{:S(2)}, u32[]{:S(2)}) collective-permute-start(bf16[576,256]{1,0:T(8,128)(2,1)S(1)} %shard_map.118.refs_6_), channel_id=1, source_target_pairs={{0,4},{4,0},{8,12},{12,8},{16,20},{20,16},{24,28},{28,24},{1,5},{5... | collective-permute-start | bytes 884744 | tf_op jit(solution)/shard_map/ppermute | solution.py:41

commit v4 on v2

--- a/solution.py
+++ b/solution.py
@@ -44,6 +44,11 @@
 def cross(values, pair):
     size = lax.axis_size("dp")
     return lax.ppermute(values, "dp", [(i, i ^ (2 * pair[i % 2])) for i in range(size)])
+
+
+def cross_cores(values, pair):
+    size = lax.axis_size("dp")
+    return lax.ppermute(values, "dp", [(i, i ^ (2 * pair[1 - i % 2] + 1)) for i in range(size)])
 
 
 def begin_kernel(
@@ -106,12 +111,6 @@
         low += ref.shape[0]
 
 
-def join_rows_kernel(first_ref, second_ref, out_ref):
-    size = first_ref.shape[2]
-    out_ref[:, :, :size] = first_ref[...]
-    out_ref[:, :, size:] = second_ref[...]
-
-
 def rows_of(row_refs, kind, block):
     return jnp.concatenate([r[kind, block] for r in row_refs], axis=0)
 
@@ -160,15 +159,15 @@
         part += dot(grad_up_pre, weight_ref[hidden : 2 * hidden], PLAIN)
         part = part.astype(jnp.bfloat16)
         for j in range(flight):
-            for half, first in ((0, 0), (flight, 2)):
-                low = (SPLIT * j + first) * CAP
-                near_part_ref[half + j, block] = part[low : low + CAP]
-                far_part_ref[half + j, block] = part[low + CAP : low + 2 * CAP]
-
-
-def weight_grad_kernel(sibling, *refs):
-    out_ref, half = refs[-1], (len(refs) - 1) // 2
-    row_refs, grad_refs = refs[:half], refs[half:-1]
+            for c, (part_ref, n) in enumerate(
+                ((near_part_ref, j), (far_part_ref, j), (far_part_ref, flight + j), (near_part_ref, flight + j))
+            ):
+                low = (SPLIT * j + c) * CAP
+                part_ref[n, block] = part[low : low + CAP]
+
+
+def weight_grad_kernel(chips, sibling, *refs):
+    out_ref, row_refs, grad_refs = refs[-1], refs[:chips], refs[chips:-1]
     hidden = out_ref.shape[0] // 3
     grads = jnp.concatenate([g[...] for g in grad_refs], axis=0)
     rows_in = jnp.concatenate([r[0, sibling] for r in row_refs], axis=0)
@@ -263,12 +262,12 @@
             return own_rows[0]
         return lax.dynamic_index_in_dim(own_rows, (me ^ c) // SPLIT, 0, keepdims=False)
 
-    arrived = [rows_for(0)]
-    for c in range(1, chunks):
-        if c % SPLIT == 3:
-            arrived.append(swap(arrived[c - 1], "expert", 1))
+    arrived = [rows_for(0)] + [None] * (chunks - 1)
+    for c in sorted(range(1, chunks), key=lambda c: c % SPLIT == 2):
+        if c % SPLIT == 2:
+            arrived[c] = swap(arrived[c + 1], "expert", 1)
         else:
-            arrived.append(swap(rows_for(c), "expert", c))
+            arrived[c] = swap(rows_for(c), "expert", c)
     pairs = [(1, 2)] + [(i, i + 1) for i in range(4, chips, 2)]
     shards = [swap(own_weights, "dp", 2 * i) for i in reversed(range(1, chips))]
     half = call(
@@ -286,13 +285,8 @@
     )
     block_rows = [own_block, swap(single_block, "dp", 2 * SINGLE)]
     for n, pair in enumerate(pairs):
-        mine, other = packed[2 * n : 2 * n + 2]
-        both = call(
-            join_rows_kernel,
-            struct((2, 2, 2 * rows, width), jnp.bfloat16),
-            (mine, swap(other, "dp", 1)),
-        )
-        block_rows.append(cross(both, pair))
+        block_rows.append(cross(packed[2 * n], pair))
+        block_rows.append(cross_cores(packed[2 * n + 1], pair))
 
     grads, near_parts, far_parts = call(
         functools.partial(expert_kernel, chunks),
@@ -311,7 +305,7 @@
     far_parts = swap(far_parts, "expert", 1)
     pair = struct((flight, blocks, CAP, width), jnp.bfloat16)
     pair_sum = call(add_kernel, pair, (near_parts, far_parts), after=block_rows[1:], flops=3 * 10**9)
-    half_sum, pair_sum = pair_sum, swap(pair_sum, "expert", 2)
+    half_sum, pair_sum = pair_sum, swap(pair_sum, "expert", 3)
     returned = (near_parts, far_parts, pair_sum)
     if flight > 1:
         slot_grad = call(sum_kernel, pair, returned)
@@ -320,14 +314,14 @@
 
     terms = (*block_rows, *all_grads)
     other_sum = call(
-        functools.partial(weight_grad_kernel, 1),
+        functools.partial(weight_grad_kernel, chips, 1),
         struct((3 * hidden, width), jnp.bfloat16),
         terms,
         after=(half_sum,),
         flops=10**10,
     )
     own_sum = call(
-        functools.partial(weight_grad_kernel, 0),
+        functools.partial(weight_grad_kernel, chips, 0),
         struct((3 * hidden, width), jnp.float32),
         terms,
         after=(other_sum,),

time: 38.7 us -> 39.5 us (1.021)
  starting transfers between devices: 20.6 us -> 21 us
    ppermute x0 -> x1, starting transfers between devices: none -> 1.02 us  [cross_cores(): lax.ppermute(values, 'dp', [(i, i ^ 2 * pair[1 - i % 2] + 1) for i in ran...]
    ppermute x14 -> x13, waiting for transfers between devices: 11.6 us -> 12.5 us  [swap(): return lax.ppermute(values, axis, [(i, i ^ shift) for i in range(size)])]
    ppermute x2, starting transfers between devices: 2.48 us -> 1.75 us  [cross(): lax.ppermute(values, 'dp', [(i, i ^ 2 * pair[i % 2]) for i in range(size)])]
    ppermute x2, waiting for transfers between devices: 0.57 us -> 0.01 us  [cross(): lax.ppermute(values, 'dp', [(i, i ^ 2 * pair[i % 2]) for i in range(size)])]
    ppermute x14 -> x13, starting transfers between devices: 18.1 us -> 18.3 us  [swap(): return lax.ppermute(values, axis, [(i, i ^ shift) for i in range(size)])]
    pallas_call x8 -> x7, Pallas kernels: 2.26 us -> 2.25 us  [call(): pl.pallas_call(run, out_shape=out_shape, in_specs=[pl.BlockSpec(memory_sp...]
  transfers between devices with their start and end apart: 16 -> 16, of which waited for: 5 -> 7; matrix products, arithmetic and copies ran while one was open for 0% -> 0% of each run, Pallas kernels for 6% -> 6%
where the time goes in v4:
time: 39.5 us; the launch traced here: 39.3 us
  starting transfers between devices  21 us (53%)
  waiting for transfers between devices  12.5 us (32%)
  Pallas kernels  5.05 us (13%)
  between operations  0.72 us (2%)
    ppermute x13, starting transfers between devices, swap(): return lax.ppermute(values, axis, [(i, i ^ shift) for i in range(size)])  18.3 us
    ppermute x13, waiting for transfers between devices, swap(): return lax.ppermute(values, axis, [(i, i ^ shift) for i in range(size)])  12.5 us
    pallas_call x7, Pallas kernels, call(): pl.pallas_call(run, out_shape=out_shape, in_specs=[pl.BlockSpec(memory_sp...  2.25 us
    ppermute x2, starting transfers between devices, cross(): lax.ppermute(values, 'dp', [(i, i ^ 2 * pair[i % 2]) for i in range(size)])  1.75 us
    pallas_call x1, Pallas kernels, body(): pl.pallas_call(begin_kernel, out_shape=(struct((flight, 2, blocks, CAP, w...  1.58 us
    pallas_call x1, Pallas kernels, body(): pl.pallas_call(functools.partial(finish_kernel, len(returned)), out_shape...  1.23 us
    ppermute x1, starting transfers between devices, cross_cores(): lax.ppermute(values, 'dp', [(i, i ^ 2 * pair[1 - i % 2] + 1) for i in ran...  1.02 us
  transfers between devices with their start and end apart: 16, of which 7 were waited for; matrix products, arithmetic and copies ran while one was open for 0% of the time, Pallas kernels for 6%

profile of v4, /device:TPU:0, one launch (start us, length us, event | category | flops | bytes accessed | tf_op | source)
XLA Modules:
  0.0 39.3 jit_solution(11524653491378555567)
XLA Ops:
  0.6 1.6 %shard_map.111 = (bf16[1,2,8,16,256]{4,3,2,1,0:T(8,128)(2,1)S(1)}, bf16[1,16,128]{2,1,0:T(8,128)(2,1)S(1)}, bf16[576,256]{1,0:T(8,128)(2,1)S(1)}) custom-call(s32[8,128]{1,0:T(8,128)} %bitcast.22, s32[8,128]{1,0:T(8,128)} %bitcast.23, f32[8,128]{1,0:T(8,128)} %bitcast.24, bf16[128,2048]{1,0:T(8,128)(2,1)} %tok_hbm.1, bf16[128,2048]{1,0:T(8,128)(2,1)} %cot_hbm.1, ...), custom_call_target="tpu_custom_call" | custom-call | tf_op jit(solution)/shard_map/pallas_call | solution.py:246
  2.2 3.0 %collective-permute-start.6 = (bf16[576,256]{1,0:T(8,128)(2,1)S(1)}, bf16[576,256]{1,0:T(8,128)(2,1)S(1)}, u32[]{:S(2)}, u32[]{:S(2)}) collective-permute-start(bf16[576,256]{1,0:T(8,128)(2,1)S(1)} %get-tuple-element.23), channel_id=1, source_target_pairs={{0,8},{4,12},{8,0},{12,4},{16,24},{20,28},{24,16},{28,20},{1,9},{5... | collective-permute-start | bytes 884744 | tf_op jit(solution)/shard_map/ppermute | solution.py:41
  5.2 1.5 %collective-permute-start.7 = (bf16[576,256]{1,0:T(8,128)(2,1)S(1)}, bf16[576,256]{1,0:T(8,128)(2,1)S(1)}, u32[]{:S(2)}, u32[]{:S(2)}) collective-permute-start(bf16[576,256]{1,0:T(8,128)(2,1)S(1)} %get-tuple-element.23), channel_id=1, source_target_pairs={{0,16},{4,20},{8,24},{12,28},{16,0},{20,4},{24,8},{28,12},{1,17},{... | collective-permute-start | bytes 884744 | tf_op jit(solution)/shard_map/ppermute | solution.py:41
  6.7 0.0 collective-permute-start.8
  6.8 4.1 %collective-permute-start.1 = (bf16[2,8,16,256]{3,2,1,0:T(8,128)(2,1)S(1)}, bf16[2,8,16,256]{3,2,1,0:T(8,128)(2,1)S(1)}, u32[]{:S(2)}, u32[]{:S(2)}) collective-permute-start(bf16[2,8,16,256]{3,2,1,0:T(8,128)(2,1)S(1)} %bitcast.16), channel_id=1, source_target_pairs={{0,3},{1,2},{2,1},{3,0},{4,7},{5,6},{6,5},{7,4},{8,11},{9,10},{10,... | collective-permute-start | bytes 393224 | tf_op jit(solution)/shard_map/ppermute | solution.py:41
  10.8 0.0 collective-permute-start
  10.8 4.1 %collective-permute-done.1.refs_3_.refs_6_ = bf16[2,8,16,256]{3,2,1,0:T(8,128)(2,1)S(1)} collective-permute-done((bf16[2,8,16,256]{3,2,1,0:T(8,128)(2,1)S(1)}, bf16[2,8,16,256]{3,2,1,0:T(8,128)(2,1)S(1)}, u32[]{:S(2)}, u32[]{:S(2)}) %collective-permute-start.1) | collective-permute-done | bytes 131104 | tf_op jit(solution)/shard_map/ppermute | solution.py:41
  15.0 1.0 %collective-permute-start.2 = (bf16[2,8,16,256]{3,2,1,0:T(8,128)(2,1)S(1)}, bf16[2,8,16,256]{3,2,1,0:T(8,128)(2,1)S(1)}, u32[]{:S(2)}, u32[]{:S(2)}) collective-permute-start(bf16[2,8,16,256]{3,2,1,0:T(8,128)(2,1)S(1)} %collective-permute-done.1.refs_3_.refs_6_), channel_id=1, source_target_pairs={{0,1},{1,0},{2,3},{3,2},{4,5},{5,4},{6,7},{7,6},{8,9},{9,8},{10,11... | collective-permute-start | bytes 393224 | tf_op jit(solution)/shard_map/ppermute | solution.py:41
  16.0 1.6 %collective-permute-done.refs_1_.refs_4_ = bf16[2,8,16,256]{3,2,1,0:T(8,128)(2,1)S(1)} collective-permute-done((bf16[2,8,16,256]{3,2,1,0:T(8,128)(2,1)S(1)}, bf16[2,8,16,256]{3,2,1,0:T(8,128)(2,1)S(1)}, u32[]{:S(2)}, u32[]{:S(2)}) %collective-permute-start) | collective-permute-done | bytes 131104 | tf_op jit(solution)/shard_map/ppermute | solution.py:41
  17.6 2.3 %collective-permute-done.2.refs_2_.refs_5_ = bf16[2,8,16,256]{3,2,1,0:T(8,128)(2,1)S(1)} collective-permute-done((bf16[2,8,16,256]{3,2,1,0:T(8,128)(2,1)S(1)}, bf16[2,8,16,256]{3,2,1,0:T(8,128)(2,1)S(1)}, u32[]{:S(2)}, u32[]{:S(2)}) %collective-permute-start.2) | collective-permute-done | bytes 131104 | tf_op jit(solution)/shard_map/ppermute | solution.py:41
  19.9 0.0 collective-permute-done.6
  19.9 0.1 collective-permute-done.7
  20.0 0.0 collective-permute-done.8
  20.0 0.1 shard_map.113.refs_4_
  20.1 0.1 collective-permute-start.9
  20.2 2.6 %collective-permute-start.3 = (bf16[2,2,64,256]{3,2,1,0:T(8,128)(2,1)S(1)}, bf16[2,2,64,256]{3,2,1,0:T(8,128)(2,1)S(1)}, u32[]{:S(2)}, u32[]{:S(2)}) collective-permute-start(bf16[2,2,64,256]{3,2,1,0:T(8,128)(2,1)S(1)} %get-tuple-element.20), channel_id=1, source_target_pairs={{0,24},{4,28},{8,16},{12,20},{16,8},{20,12},{24,0},{28,4},{1,25},{... | collective-permute-start | bytes 393224 | tf_op jit(solution)/shard_map/ppermute | solution.py:41
  22.8 0.5 %collective-permute-start.4 = (bf16[2,2,64,256]{3,2,1,0:T(8,128)(2,1)S(1)}, bf16[2,2,64,256]{3,2,1,0:T(8,128)(2,1)S(1)}, u32[]{:S(2)}, u32[]{:S(2)}) collective-permute-start(bf16[2,2,64,256]{3,2,1,0:T(8,128)(2,1)S(1)} %get-tuple-element.21), channel_id=1, source_target_pairs={{0,8},{4,20},{8,0},{12,28},{16,24},{20,4},{24,16},{28,12},{1,9},{5... | collective-permute-start | bytes 393224 | tf_op jit(solution)/shard_map/ppermute | solution.py:46
  23.3 1.0 %collective-permute-start.5 = (bf16[2,2,64,256]{3,2,1,0:T(8,128)(2,1)S(1)}, bf16[2,2,64,256]{3,2,1,0:T(8,128)(2,1)S(1)}, u32[]{:S(2)}, u32[]{:S(2)}) collective-permute-start(bf16[2,2,64,256]{3,2,1,0:T(8,128)(2,1)S(1)} %get-tuple-element.22), channel_id=1, source_target_pairs={{0,20},{4,8},{8,28},{12,0},{16,4},{20,24},{24,12},{28,16},{1,21},{... | collective-permute-start | bytes 393224 | tf_op jit(solution)/shard_map/ppermute | solution.py:51
  24.4 0.0 collective-permute-done.9.refs_5_
  24.4 1.5 %shard_map.114 = (bf16[64,576]{1,0:T(8,128)(2,1)S(1)}, bf16[2,8,16,256]{3,2,1,0:T(8,128)(2,1)S(1)}, bf16[2,8,16,256]{3,2,1,0:T(8,128)(2,1)S(1)}) custom-call(bf16[2,8,16,256]{3,2,1,0:T(8,128)(2,1)S(1)} %bitcast.19, bf16[2,8,16,256]{3,2,1,0:T(8,128)(2,1)S(1)} %collective-permute-done.refs_1_.refs_4_, ...), custom_call_target="tpu_custom_call" | custom-call | flops 5000000000 | tf_op jit(solution)/shard_map/pallas_call | solution.py:28
  25.9 1.0 %collective-permute-start.13 = (bf16[2,8,16,256]{3,2,1,0:T(8,128)(2,1)S(1)}, bf16[2,8,16,256]{3,2,1,0:T(8,128)(2,1)S(1)}, u32[]{:S(2)}, u32[]{:S(2)}) collective-permute-start(bf16[2,8,16,256]{3,2,1,0:T(8,128)(2,1)S(1)} %get-tuple-element.26), channel_id=1, source_target_pairs={{0,1},{1,0},{2,3},{3,2},{4,5},{5,4},{6,7},{7,6},{8,9},{9,8},{10,11... | collective-permute-start | bytes 393224 | tf_op jit(solution)/shard_map/ppermute | solution.py:41
  26.9 0.3 collective-permute-start.11
  27.2 1.0 %collective-permute-done.11.refs_1_ = bf16[64,576]{1,0:T(8,128)(2,1)S(1)} collective-permute-done((bf16[64,576]{1,0:T(8,128)(2,1)S(1)}, bf16[64,576]{1,0:T(8,128)(2,1)S(1)}, u32[]{:S(2)}, u32[]{:S(2)}) %collective-permute-start.11) | collective-permute-done | bytes 73760 | tf_op jit(solution)/shard_map/ppermute | solution.py:41
  28.1 1.2 %collective-permute-start.10 = (bf16[64,576]{1,0:T(8,128)(2,1)S(1)}, bf16[64,576]{1,0:T(8,128)(2,1)S(1)}, u32[]{:S(2)}, u32[]{:S(2)}) collective-permute-start(bf16[64,576]{1,0:T(8,128)(2,1)S(1)} %get-tuple-element.24.refs_0_.refs_4_), channel_id=1, source_target_pairs={{0,24},{4,28},{8,16},{12,20},{16,8},{20,12},{24,0},{28,4},{1,25},{... | collective-permute-start | bytes 221192 | tf_op jit(solution)/shard_map/ppermute | solution.py:41
  29.3 0.0 collective-permute-done.3.refs_2_.refs_1_
  29.3 1.2 %collective-permute-start.12 = (bf16[128,576]{1,0:T(8,128)(2,1)S(1)}, bf16[128,576]{1,0:T(8,128)(2,1)S(1)}, u32[]{:S(2)}, u32[]{:S(2)}) collective-permute-start(bf16[128,576]{1,0:T(8,128)(2,1)S(1)} %shard_map.115), channel_id=1, source_target_pairs={{0,8},{4,20},{8,0},{12,28},{16,24},{20,4},{24,16},{28,12},{1,9},{5... | collective-permute-start | bytes 442376 | tf_op jit(solution)/shard_map/ppermute | solution.py:46
  30.6 0.0 collective-permute-done.4.refs_3_.refs_2_
  30.6 0.0 collective-permute-done.5.refs_4_.refs_3_
  30.6 1.4 %collective-permute-done.13.refs_1_ = bf16[2,8,16,256]{3,2,1,0:T(8,128)(2,1)S(1)} collective-permute-done((bf16[2,8,16,256]{3,2,1,0:T(8,128)(2,1)S(1)}, bf16[2,8,16,256]{3,2,1,0:T(8,128)(2,1)S(1)}, u32[]{:S(2)}, u32[]{:S(2)}) %collective-permute-start.13) | collective-permute-done | bytes 131104 | tf_op jit(solution)/shard_map/ppermute | solution.py:41
  32.0 3.5 %collective-permute-start.15 = (bf16[1,8,16,256]{3,2,1,0:T(8,128)(2,1)S(1)}, bf16[1,8,16,256]{3,2,1,0:T(8,128)(2,1)S(1)}, u32[]{:S(2)}, u32[]{:S(2)}) collective-permute-start(bf16[1,8,16,256]{3,2,1,0:T(8,128)(2,1)S(1)} %shard_map.116.refs_7_), channel_id=1, source_target_pairs={{0,3},{1,2},{2,1},{3,0},{4,7},{5,6},{6,5},{7,4},{8,11},{9,10},{10,... | collective-permute-start | bytes 196616 | tf_op jit(solution)/shard_map/ppermute | solution.py:41
  35.4 0.0 collective-permute-done.10.refs_5_
  35.4 0.0 collective-permute-done.12.refs_6_
  35.4 0.3 shard_map.117.refs_7_
  35.7 0.1 collective-permute-start.14
  35.8 0.3 shard_map.118.own_ref
  36.1 2.0 %collective-permute-done.15.refs_2_ = bf16[1,8,16,256]{3,2,1,0:T(8,128)(2,1)S(1)} collective-permute-done((bf16[1,8,16,256]{3,2,1,0:T(8,128)(2,1)S(1)}, bf16[1,8,16,256]{3,2,1,0:T(8,128)(2,1)S(1)}, u32[]{:S(2)}, u32[]{:S(2)}) %collective-permute-start.15) | collective-permute-done | bytes 65568 | tf_op jit(solution)/shard_map/ppermute | solution.py:41
  38.1 0.0 collective-permute-done.14.other_ref
  38.1 1.2 %shard_map.119 = (bf16[128,2048]{1,0:T(8,128)(2,1)}, f32[192,256]{1,0:T(8,128)}, f32[192,256]{1,0:T(8,128)}, f32[192,256]{1,0:T(8,128)}) custom-call(f32[576,256]{1,0:T(8,128)S(1)} %shard_map.118.own_ref, bf16[576,256]{1,0:T(8,128)(2,1)S(1)} %collective-permute-done.14.other_ref, bf16[1,16,128]{2,1,0:T(8,128)(2,1)S(1)} %get-tuple-element.27.hot_ref, ...), custom_call_target="tpu_custom_call" | custom-call | tf_op jit(solution)/shard_map/pallas_call | solution.py:331
  (3 shorter events, 0.1 us)
Async XLA Ops:
  2.2 17.7 %collective-permute-start.6 = (bf16[576,256]{1,0:T(8,128)(2,1)S(1)}, bf16[576,256]{1,0:T(8,128)(2,1)S(1)}, u32[]{:S(2)}, u32[]{:S(2)}) collective-permute-start(bf16[576,256]{1,0:T(8,128)(2,1)S(1)} %get-tuple-element.23), channel_id=1, source_target_pairs={{0,8},{4,12},{8,0},{12,4},{16,24},{20,28},{24,16},{28,20},{1,9},{5... | collective-permute-start | bytes 884744 | tf_op jit(solution)/shard_map/ppermute | solution.py:41
  5.2 14.8 %collective-permute-start.7 = (bf16[576,256]{1,0:T(8,128)(2,1)S(1)}, bf16[576,256]{1,0:T(8,128)(2,1)S(1)}, u32[]{:S(2)}, u32[]{:S(2)}) collective-permute-start(bf16[576,256]{1,0:T(8,128)(2,1)S(1)} %get-tuple-element.23), channel_id=1, source_target_pairs={{0,16},{4,20},{8,24},{12,28},{16,0},{20,4},{24,8},{28,12},{1,17},{... | collective-permute-start | bytes 884744 | tf_op jit(solution)/shard_map/ppermute | solution.py:41
  6.7 13.3 %collective-permute-start.8 = (bf16[576,256]{1,0:T(8,128)(2,1)S(1)}, bf16[576,256]{1,0:T(8,128)(2,1)S(1)}, u32[]{:S(2)}, u32[]{:S(2)}) collective-permute-start(bf16[576,256]{1,0:T(8,128)(2,1)S(1)} %get-tuple-element.23), channel_id=1, source_target_pairs={{0,24},{4,28},{8,16},{12,20},{16,8},{20,12},{24,0},{28,4},{1,25},{... | collective-permute-start | bytes 884744 | tf_op jit(solution)/shard_map/ppermute | solution.py:41
  6.8 8.2 %collective-permute-start.1 = (bf16[2,8,16,256]{3,2,1,0:T(8,128)(2,1)S(1)}, bf16[2,8,16,256]{3,2,1,0:T(8,128)(2,1)S(1)}, u32[]{:S(2)}, u32[]{:S(2)}) collective-permute-start(bf16[2,8,16,256]{3,2,1,0:T(8,128)(2,1)S(1)} %bitcast.16), channel_id=1, source_target_pairs={{0,3},{1,2},{2,1},{3,0},{4,7},{5,6},{6,5},{7,4},{8,11},{9,10},{10,... | collective-permute-start | bytes 393224 | tf_op jit(solution)/shard_map/ppermute | solution.py:41
  10.8 6.8 %collective-permute-start = (bf16[2,8,16,256]{3,2,1,0:T(8,128)(2,1)S(1)}, bf16[2,8,16,256]{3,2,1,0:T(8,128)(2,1)S(1)}, u32[]{:S(2)}, u32[]{:S(2)}) collective-permute-start(bf16[2,8,16,256]{3,2,1,0:T(8,128)(2,1)S(1)} %bitcast.17), channel_id=1, source_target_pairs={{0,1},{1,0},{2,3},{3,2},{4,5},{5,4},{6,7},{7,6},{8,9},{9,8},{10,11... | collective-permute-start | bytes 393224 | tf_op jit(solution)/shard_map/ppermute | solution.py:41
  15.0 5.0 %collective-permute-start.2 = (bf16[2,8,16,256]{3,2,1,0:T(8,128)(2,1)S(1)}, bf16[2,8,16,256]{3,2,1,0:T(8,128)(2,1)S(1)}, u32[]{:S(2)}, u32[]{:S(2)}) collective-permute-start(bf16[2,8,16,256]{3,2,1,0:T(8,128)(2,1)S(1)} %collective-permute-done.1.refs_3_.refs_6_), channel_id=1, source_target_pairs={{0,1},{1,0},{2,3},{3,2},{4,5},{5,4},{6,7},{7,6},{8,9},{9,8},{10,11... | collective-permute-start | bytes 393224 | tf_op jit(solution)/shard_map/ppermute | solution.py:41
  20.1 4.3 %collective-permute-start.9 = (bf16[4,576,256]{2,1,0:T(8,128)(2,1)S(1)}, bf16[4,576,256]{2,1,0:T(8,128)(2,1)S(1)}, u32[]{:S(2)}, u32[]{:S(2)}) collective-permute-start(bf16[4,576,256]{2,1,0:T(8,128)(2,1)S(1)} %shard_map.113.refs_4_), channel_id=1, source_target_pairs={{0,4},{4,0},{8,12},{12,8},{16,20},{20,16},{24,28},{28,24},{1,5},{5... | collective-permute-start | bytes 3538952 | tf_op jit(solution)/shard_map/ppermute | solution.py:41
  20.2 9.1 %collective-permute-start.3 = (bf16[2,2,64,256]{3,2,1,0:T(8,128)(2,1)S(1)}, bf16[2,2,64,256]{3,2,1,0:T(8,128)(2,1)S(1)}, u32[]{:S(2)}, u32[]{:S(2)}) collective-permute-start(bf16[2,2,64,256]{3,2,1,0:T(8,128)(2,1)S(1)} %get-tuple-element.20), channel_id=1, source_target_pairs={{0,24},{4,28},{8,16},{12,20},{16,8},{20,12},{24,0},{28,4},{1,25},{... | collective-permute-start | bytes 393224 | tf_op jit(solution)/shard_map/ppermute | solution.py:41
  22.8 7.8 %collective-permute-start.4 = (bf16[2,2,64,256]{3,2,1,0:T(8,128)(2,1)S(1)}, bf16[2,2,64,256]{3,2,1,0:T(8,128)(2,1)S(1)}, u32[]{:S(2)}, u32[]{:S(2)}) collective-permute-start(bf16[2,2,64,256]{3,2,1,0:T(8,128)(2,1)S(1)} %get-tuple-element.21), channel_id=1, source_target_pairs={{0,8},{4,20},{8,0},{12,28},{16,24},{20,4},{24,16},{28,12},{1,9},{5... | collective-permute-start | bytes 393224 | tf_op jit(solution)/shard_map/ppermute | solution.py:46
  23.3 7.2 %collective-permute-start.5 = (bf16[2,2,64,256]{3,2,1,0:T(8,128)(2,1)S(1)}, bf16[2,2,64,256]{3,2,1,0:T(8,128)(2,1)S(1)}, u32[]{:S(2)}, u32[]{:S(2)}) collective-permute-start(bf16[2,2,64,256]{3,2,1,0:T(8,128)(2,1)S(1)} %get-tuple-element.22), channel_id=1, source_target_pairs={{0,20},{4,8},{8,28},{12,0},{16,4},{20,24},{24,12},{28,16},{1,21},{... | collective-permute-start | bytes 393224 | tf_op jit(solution)/shard_map/ppermute | solution.py:51
  25.9 6.1 %collective-permute-start.13 = (bf16[2,8,16,256]{3,2,1,0:T(8,128)(2,1)S(1)}, bf16[2,8,16,256]{3,2,1,0:T(8,128)(2,1)S(1)}, u32[]{:S(2)}, u32[]{:S(2)}) collective-permute-start(bf16[2,8,16,256]{3,2,1,0:T(8,128)(2,1)S(1)} %get-tuple-element.26), channel_id=1, source_target_pairs={{0,1},{1,0},{2,3},{3,2},{4,5},{5,4},{6,7},{7,6},{8,9},{9,8},{10,11... | collective-permute-start | bytes 393224 | tf_op jit(solution)/shard_map/ppermute | solution.py:41
  26.9 1.3 %collective-permute-start.11 = (bf16[64,576]{1,0:T(8,128)(2,1)S(1)}, bf16[64,576]{1,0:T(8,128)(2,1)S(1)}, u32[]{:S(2)}, u32[]{:S(2)}) collective-permute-start(bf16[64,576]{1,0:T(8,128)(2,1)S(1)} %get-tuple-element.24.refs_0_.refs_4_), channel_id=1, source_target_pairs={{0,4},{4,0},{8,12},{12,8},{16,20},{20,16},{24,28},{28,24},{1,5},{5... | collective-permute-start | bytes 221192 | tf_op jit(solution)/shard_map/ppermute | solution.py:41
  28.1 7.3 %collective-permute-start.10 = (bf16[64,576]{1,0:T(8,128)(2,1)S(1)}, bf16[64,576]{1,0:T(8,128)(2,1)S(1)}, u32[]{:S(2)}, u32[]{:S(2)}) collective-permute-start(bf16[64,576]{1,0:T(8,128)(2,1)S(1)} %get-tuple-element.24.refs_0_.refs_4_), channel_id=1, source_target_pairs={{0,24},{4,28},{8,16},{12,20},{16,8},{20,12},{24,0},{28,4},{1,25},{... | collective-permute-start | bytes 221192 | tf_op jit(solution)/shard_map/ppermute | solution.py:41
  29.3 6.1 %collective-permute-start.12 = (bf16[128,576]{1,0:T(8,128)(2,1)S(1)}, bf16[128,576]{1,0:T(8,128)(2,1)S(1)}, u32[]{:S(2)}, u32[]{:S(2)}) collective-permute-start(bf16[128,576]{1,0:T(8,128)(2,1)S(1)} %shard_map.115), channel_id=1, source_target_pairs={{0,8},{4,20},{8,0},{12,28},{16,24},{20,4},{24,16},{28,12},{1,9},{5... | collective-permute-start | bytes 442376 | tf_op jit(solution)/shard_map/ppermute | solution.py:46
  32.0 6.1 %collective-permute-start.15 = (bf16[1,8,16,256]{3,2,1,0:T(8,128)(2,1)S(1)}, bf16[1,8,16,256]{3,2,1,0:T(8,128)(2,1)S(1)}, u32[]{:S(2)}, u32[]{:S(2)}) collective-permute-start(bf16[1,8,16,256]{3,2,1,0:T(8,128)(2,1)S(1)} %shard_map.116.refs_7_), channel_id=1, source_target_pairs={{0,3},{1,2},{2,1},{3,0},{4,7},{5,6},{6,5},{7,4},{8,11},{9,10},{10,... | collective-permute-start | bytes 196616 | tf_op jit(solution)/shard_map/ppermute | solution.py:41
  35.7 2.4 %collective-permute-start.14 = (bf16[576,256]{1,0:T(8,128)(2,1)S(1)}, bf16[576,256]{1,0:T(8,128)(2,1)S(1)}, u32[]{:S(2)}, u32[]{:S(2)}) collective-permute-start(bf16[576,256]{1,0:T(8,128)(2,1)S(1)} %shard_map.117.refs_7_), channel_id=1, source_target_pairs={{0,4},{4,0},{8,12},{12,8},{16,20},{20,16},{24,28},{28,24},{1,5},{5... | collective-permute-start | bytes 884744 | tf_op jit(solution)/shard_map/ppermute | solution.py:41

commit v5 on v4

--- a/solution.py
+++ b/solution.py
@@ -134,7 +134,7 @@
 
 def expert_kernel(chunks, *refs):
     row_refs, (half_ref, other_ref, grads_ref) = refs[:chunks], refs[chunks : chunks + 3]
-    near_part_ref, far_part_ref = refs[chunks + 3 :]
+    near_ref, direct_ref, relay_ref = refs[chunks + 3 :]
     flight = chunks // SPLIT
     me = lax.axis_index("dp")
     weights = []
@@ -159,9 +159,8 @@
         part += dot(grad_up_pre, weight_ref[hidden : 2 * hidden], PLAIN)
         part = part.astype(jnp.bfloat16)
         for j in range(flight):
-            for c, (part_ref, n) in enumerate(
-                ((near_part_ref, j), (far_part_ref, j), (far_part_ref, flight + j), (near_part_ref, flight + j))
-            ):
+            targets = ((near_ref, j), (direct_ref, j), (relay_ref, j), (near_ref, flight + j))
+            for c, (part_ref, n) in enumerate(targets):
                 low = (SPLIT * j + c) * CAP
                 part_ref[n, block] = part[low : low + CAP]
 
@@ -178,15 +177,16 @@
     out_ref[2 * hidden :] = down.astype(out_ref.dtype)
 
 
-def add_kernel(near_ref, far_ref, out_ref):
+def add_kernel(near_ref, relay_ref, direct_ref, out_ref, direct_out_ref):
+    direct_out_ref[...] = direct_ref[...]
     half = out_ref.shape[0]
-    total = near_ref[half:].astype(jnp.float32) + far_ref[half:].astype(jnp.float32)
+    total = near_ref[half:].astype(jnp.float32) + relay_ref[...].astype(jnp.float32)
     out_ref[...] = total.astype(out_ref.dtype)
 
 
-def sum_kernel(near_ref, far_ref, pair_ref, out_ref):
+def sum_kernel(near_ref, pair_ref, direct_ref, out_ref):
     half = out_ref.shape[0]
-    total = near_ref[:half].astype(jnp.float32) + far_ref[:half].astype(jnp.float32)
+    total = near_ref[:half].astype(jnp.float32) + direct_ref[...].astype(jnp.float32)
     out_ref[...] = (total + pair_ref[...].astype(jnp.float32)).astype(out_ref.dtype)
 
 
@@ -213,8 +213,8 @@
         total = 0.0
         for j in range(flight):
             if flight == 1:
-                near_ref, far_ref, pair_ref = part_refs
-                summed = near_ref[0, b].astype(jnp.float32) + far_ref[0, b].astype(jnp.float32)
+                near_ref, pair_ref, direct_ref = part_refs
+                summed = near_ref[0, b].astype(jnp.float32) + direct_ref[0, b].astype(jnp.float32)
                 summed = (summed + pair_ref[0, b].astype(jnp.float32)).astype(jnp.bfloat16)
             else:
                 summed = part_refs[j][b]
@@ -288,10 +288,10 @@
         block_rows.append(cross(packed[2 * n], pair))
         block_rows.append(cross_cores(packed[2 * n + 1], pair))
 
-    grads, near_parts, far_parts = call(
+    grads, near_parts, direct, relay = call(
         functools.partial(expert_kernel, chunks),
         [struct((rows, 3 * hidden), jnp.bfloat16)]
-        + [struct((2 * flight, blocks, CAP, width), jnp.bfloat16)] * 2,
+        + [struct((n * flight, blocks, CAP, width), jnp.bfloat16) for n in (2, 1, 1)],
         (*arrived, half, other_half),
         flops=5 * 10**9,
     )
@@ -302,13 +302,18 @@
     )
     all_grads = [grads, swap(grads, "dp", 2 * SINGLE)]
     all_grads += [cross(chip_grads, pair) for pair in pairs]
-    far_parts = swap(far_parts, "expert", 1)
-    pair = struct((flight, blocks, CAP, width), jnp.bfloat16)
-    pair_sum = call(add_kernel, pair, (near_parts, far_parts), after=block_rows[1:], flops=3 * 10**9)
-    half_sum, pair_sum = pair_sum, swap(pair_sum, "expert", 3)
-    returned = (near_parts, far_parts, pair_sum)
+    part = struct((flight, blocks, CAP, width), jnp.bfloat16)
+    half_sum, direct = call(
+        add_kernel,
+        (part, part),
+        (near_parts, swap(relay, "expert", 1), direct),
+        after=block_rows[1:],
+        flops=3 * 10**9,
+    )
+    pair_sum, direct = swap(half_sum, "expert", 3), swap(direct, "expert", 1)
+    returned = (near_parts, pair_sum, direct)
     if flight > 1:
-        slot_grad = call(sum_kernel, pair, returned)
+        slot_grad = call(sum_kernel, part, returned)
         returned = [slot_grad[0]]
         returned += [swap(slot_grad[j], "expert", SPLIT * j) for j in range(1, flight)]
 

time: 39.5 us -> 40 us (1.013)
    ppermute x13 -> x14, starting transfers between devices: 18.3 us -> 18.5 us  [swap(): return lax.ppermute(values, axis, [(i, i ^ shift) for i in range(size)])]
    ppermute x13 -> x14, waiting for transfers between devices: 12.5 us -> 12.5 us  [swap(): return lax.ppermute(values, axis, [(i, i ^ shift) for i in range(size)])]
  transfers between devices with their start and end apart: 16 -> 17, of which waited for: 7 -> 8; matrix products, arithmetic and copies ran while one was open for 0% -> 0% of each run, Pallas kernels for 6% -> 5%
where the time goes in v5:
time: 40 us; the launch traced here: 39.8 us
  starting transfers between devices  21.3 us (53%)
  waiting for transfers between devices  12.7 us (32%)
  Pallas kernels  5.07 us (13%)
  between operations  0.73 us (2%)
    ppermute x14, starting transfers between devices, swap(): return lax.ppermute(values, axis, [(i, i ^ shift) for i in range(size)])  18.5 us
    ppermute x14, waiting for transfers between devices, swap(): return lax.ppermute(values, axis, [(i, i ^ shift) for i in range(size)])  12.5 us
    pallas_call x7, Pallas kernels, call(): pl.pallas_call(run, out_shape=out_shape, in_specs=[pl.BlockSpec(memory_sp...  2.26 us
    ppermute x2, starting transfers between devices, cross(): lax.ppermute(values, 'dp', [(i, i ^ 2 * pair[i % 2]) for i in range(size)])  1.84 us
    pallas_call x1, Pallas kernels, body(): pl.pallas_call(begin_kernel, out_shape=(struct((flight, 2, blocks, CAP, w...  1.58 us
    pallas_call x1, Pallas kernels, body(): pl.pallas_call(functools.partial(finish_kernel, len(returned)), out_shape...  1.23 us
    ppermute x1, starting transfers between devices, cross_cores(): lax.ppermute(values, 'dp', [(i, i ^ 2 * pair[1 - i % 2] + 1) for i in ran...  1.02 us
  transfers between devices with their start and end apart: 17, of which 8 were waited for; matrix products, arithmetic and copies ran while one was open for 0% of the time, Pallas kernels for 5%

profile of v5, /device:TPU:0, one launch (start us, length us, event | category | flops | bytes accessed | tf_op | source)
XLA Modules:
  0.0 39.8 jit_solution(17359845644930955049)
XLA Ops:
  0.6 1.6 %shard_map.111 = (bf16[1,2,8,16,256]{4,3,2,1,0:T(8,128)(2,1)S(1)}, bf16[1,16,128]{2,1,0:T(8,128)(2,1)S(1)}, bf16[576,256]{1,0:T(8,128)(2,1)S(1)}) custom-call(s32[8,128]{1,0:T(8,128)} %bitcast.22, s32[8,128]{1,0:T(8,128)} %bitcast.23, f32[8,128]{1,0:T(8,128)} %bitcast.24, bf16[128,2048]{1,0:T(8,128)(2,1)} %tok_hbm.1, bf16[128,2048]{1,0:T(8,128)(2,1)} %cot_hbm.1, ...), custom_call_target="tpu_custom_call" | custom-call | tf_op jit(solution)/shard_map/pallas_call | solution.py:246
  2.2 3.0 %collective-permute-start.6 = (bf16[576,256]{1,0:T(8,128)(2,1)S(1)}, bf16[576,256]{1,0:T(8,128)(2,1)S(1)}, u32[]{:S(2)}, u32[]{:S(2)}) collective-permute-start(bf16[576,256]{1,0:T(8,128)(2,1)S(1)} %get-tuple-element.26), channel_id=1, source_target_pairs={{0,8},{4,12},{8,0},{12,4},{16,24},{20,28},{24,16},{28,20},{1,9},{5... | collective-permute-start | bytes 884744 | tf_op jit(solution)/shard_map/ppermute | solution.py:41
  5.2 1.5 %collective-permute-start.7 = (bf16[576,256]{1,0:T(8,128)(2,1)S(1)}, bf16[576,256]{1,0:T(8,128)(2,1)S(1)}, u32[]{:S(2)}, u32[]{:S(2)}) collective-permute-start(bf16[576,256]{1,0:T(8,128)(2,1)S(1)} %get-tuple-element.26), channel_id=1, source_target_pairs={{0,16},{4,20},{8,24},{12,28},{16,0},{20,4},{24,8},{28,12},{1,17},{... | collective-permute-start | bytes 884744 | tf_op jit(solution)/shard_map/ppermute | solution.py:41
  6.7 0.0 collective-permute-start.8
  6.8 4.1 %collective-permute-start.1 = (bf16[2,8,16,256]{3,2,1,0:T(8,128)(2,1)S(1)}, bf16[2,8,16,256]{3,2,1,0:T(8,128)(2,1)S(1)}, u32[]{:S(2)}, u32[]{:S(2)}) collective-permute-start(bf16[2,8,16,256]{3,2,1,0:T(8,128)(2,1)S(1)} %bitcast.16), channel_id=1, source_target_pairs={{0,3},{1,2},{2,1},{3,0},{4,7},{5,6},{6,5},{7,4},{8,11},{9,10},{10,... | collective-permute-start | bytes 393224 | tf_op jit(solution)/shard_map/ppermute | solution.py:41
  10.8 0.0 collective-permute-start
  10.8 4.1 %collective-permute-done.1.refs_3_.refs_6_ = bf16[2,8,16,256]{3,2,1,0:T(8,128)(2,1)S(1)} collective-permute-done((bf16[2,8,16,256]{3,2,1,0:T(8,128)(2,1)S(1)}, bf16[2,8,16,256]{3,2,1,0:T(8,128)(2,1)S(1)}, u32[]{:S(2)}, u32[]{:S(2)}) %collective-permute-start.1) | collective-permute-done | bytes 131104 | tf_op jit(solution)/shard_map/ppermute | solution.py:41
  15.0 1.0 %collective-permute-start.2 = (bf16[2,8,16,256]{3,2,1,0:T(8,128)(2,1)S(1)}, bf16[2,8,16,256]{3,2,1,0:T(8,128)(2,1)S(1)}, u32[]{:S(2)}, u32[]{:S(2)}) collective-permute-start(bf16[2,8,16,256]{3,2,1,0:T(8,128)(2,1)S(1)} %collective-permute-done.1.refs_3_.refs_6_), channel_id=1, source_target_pairs={{0,1},{1,0},{2,3},{3,2},{4,5},{5,4},{6,7},{7,6},{8,9},{9,8},{10,11... | collective-permute-start | bytes 393224 | tf_op jit(solution)/shard_map/ppermute | solution.py:41
  16.0 1.6 %collective-permute-done.refs_1_.refs_4_ = bf16[2,8,16,256]{3,2,1,0:T(8,128)(2,1)S(1)} collective-permute-done((bf16[2,8,16,256]{3,2,1,0:T(8,128)(2,1)S(1)}, bf16[2,8,16,256]{3,2,1,0:T(8,128)(2,1)S(1)}, u32[]{:S(2)}, u32[]{:S(2)}) %collective-permute-start) | collective-permute-done | bytes 131104 | tf_op jit(solution)/shard_map/ppermute | solution.py:41
  17.6 2.3 %collective-permute-done.2.refs_2_.refs_5_ = bf16[2,8,16,256]{3,2,1,0:T(8,128)(2,1)S(1)} collective-permute-done((bf16[2,8,16,256]{3,2,1,0:T(8,128)(2,1)S(1)}, bf16[2,8,16,256]{3,2,1,0:T(8,128)(2,1)S(1)}, u32[]{:S(2)}, u32[]{:S(2)}) %collective-permute-start.2) | collective-permute-done | bytes 131104 | tf_op jit(solution)/shard_map/ppermute | solution.py:41
  19.9 0.0 collective-permute-done.6
  19.9 0.1 collective-permute-done.7
  20.0 0.0 collective-permute-done.8
  20.0 0.1 shard_map.113.refs_4_
  20.1 0.1 collective-permute-start.9
  20.2 2.6 %collective-permute-start.3 = (bf16[2,2,64,256]{3,2,1,0:T(8,128)(2,1)S(1)}, bf16[2,2,64,256]{3,2,1,0:T(8,128)(2,1)S(1)}, u32[]{:S(2)}, u32[]{:S(2)}) collective-permute-start(bf16[2,2,64,256]{3,2,1,0:T(8,128)(2,1)S(1)} %get-tuple-element.23), channel_id=1, source_target_pairs={{0,24},{4,28},{8,16},{12,20},{16,8},{20,12},{24,0},{28,4},{1,25},{... | collective-permute-start | bytes 393224 | tf_op jit(solution)/shard_map/ppermute | solution.py:41
  22.8 0.5 %collective-permute-start.4 = (bf16[2,2,64,256]{3,2,1,0:T(8,128)(2,1)S(1)}, bf16[2,2,64,256]{3,2,1,0:T(8,128)(2,1)S(1)}, u32[]{:S(2)}, u32[]{:S(2)}) collective-permute-start(bf16[2,2,64,256]{3,2,1,0:T(8,128)(2,1)S(1)} %get-tuple-element.24), channel_id=1, source_target_pairs={{0,8},{4,20},{8,0},{12,28},{16,24},{20,4},{24,16},{28,12},{1,9},{5... | collective-permute-start | bytes 393224 | tf_op jit(solution)/shard_map/ppermute | solution.py:46
  23.3 1.0 %collective-permute-start.5 = (bf16[2,2,64,256]{3,2,1,0:T(8,128)(2,1)S(1)}, bf16[2,2,64,256]{3,2,1,0:T(8,128)(2,1)S(1)}, u32[]{:S(2)}, u32[]{:S(2)}) collective-permute-start(bf16[2,2,64,256]{3,2,1,0:T(8,128)(2,1)S(1)} %get-tuple-element.25), channel_id=1, source_target_pairs={{0,20},{4,8},{8,28},{12,0},{16,4},{20,24},{24,12},{28,16},{1,21},{... | collective-permute-start | bytes 393224 | tf_op jit(solution)/shard_map/ppermute | solution.py:51
  24.4 0.0 collective-permute-done.9.refs_5_
  24.4 1.5 %shard_map.114 = (bf16[64,576]{1,0:T(8,128)(2,1)S(1)}, bf16[2,8,16,256]{3,2,1,0:T(8,128)(2,1)S(1)}, bf16[1,8,16,256]{3,2,1,0:T(8,128)(2,1)S(1)}, bf16[1,8,16,256]{3,2,1,0:T(8,128)(2,1)S(1)}) custom-call(bf16[2,8,16,256]{3,2,1,0:T(8,128)(2,1)S(1)} %bitcast.19, bf16[2,8,16,256]{3,2,1,0:T(8,128)(2,1)S(1)} %collective-permute-done.refs_1_.refs_4_, ...), custom_call_target="tpu_custom_call" | custom-call | flops 5000000000 | tf_op jit(solution)/shard_map/pallas_call | solution.py:28
  25.9 0.7 %collective-permute-start.11 = (bf16[64,576]{1,0:T(8,128)(2,1)S(1)}, bf16[64,576]{1,0:T(8,128)(2,1)S(1)}, u32[]{:S(2)}, u32[]{:S(2)}) collective-permute-start(bf16[64,576]{1,0:T(8,128)(2,1)S(1)} %get-tuple-element.27.refs_0_.refs_4_), channel_id=1, source_target_pairs={{0,4},{4,0},{8,12},{12,8},{16,20},{20,16},{24,28},{28,24},{1,5},{5... | collective-permute-start | bytes 221192 | tf_op jit(solution)/shard_map/ppermute | solution.py:41
  26.5 0.9 %collective-permute-start.13 = (bf16[1,8,16,256]{3,2,1,0:T(8,128)(2,1)S(1)}, bf16[1,8,16,256]{3,2,1,0:T(8,128)(2,1)S(1)}, u32[]{:S(2)}, u32[]{:S(2)}) collective-permute-start(bf16[1,8,16,256]{3,2,1,0:T(8,128)(2,1)S(1)} %get-tuple-element.29), channel_id=1, source_target_pairs={{0,1},{1,0},{2,3},{3,2},{4,5},{5,4},{6,7},{7,6},{8,9},{9,8},{10,11... | collective-permute-start | bytes 196616 | tf_op jit(solution)/shard_map/ppermute | solution.py:41
  27.5 0.0 collective-permute-done.11.refs_1_
  27.5 1.1 %collective-permute-start.10 = (bf16[64,576]{1,0:T(8,128)(2,1)S(1)}, bf16[64,576]{1,0:T(8,128)(2,1)S(1)}, u32[]{:S(2)}, u32[]{:S(2)}) collective-permute-start(bf16[64,576]{1,0:T(8,128)(2,1)S(1)} %get-tuple-element.27.refs_0_.refs_4_), channel_id=1, source_target_pairs={{0,24},{4,28},{8,16},{12,20},{16,8},{20,12},{24,0},{28,4},{1,25},{... | collective-permute-start | bytes 221192 | tf_op jit(solution)/shard_map/ppermute | solution.py:41
  28.6 0.0 collective-permute-done.3.refs_3_.refs_1_
  28.6 1.3 %collective-permute-start.12 = (bf16[128,576]{1,0:T(8,128)(2,1)S(1)}, bf16[128,576]{1,0:T(8,128)(2,1)S(1)}, u32[]{:S(2)}, u32[]{:S(2)}) collective-permute-start(bf16[128,576]{1,0:T(8,128)(2,1)S(1)} %shard_map.115), channel_id=1, source_target_pairs={{0,8},{4,20},{8,0},{12,28},{16,24},{20,4},{24,16},{28,12},{1,9},{5... | collective-permute-start | bytes 442376 | tf_op jit(solution)/shard_map/ppermute | solution.py:46
  29.9 0.2 collective-permute-done.4.refs_4_.refs_2_
  30.0 0.0 collective-permute-done.5.refs_5_.refs_3_
  30.0 0.8 %collective-permute-done.13.refs_1_ = bf16[1,8,16,256]{3,2,1,0:T(8,128)(2,1)S(1)} collective-permute-done((bf16[1,8,16,256]{3,2,1,0:T(8,128)(2,1)S(1)}, bf16[1,8,16,256]{3,2,1,0:T(8,128)(2,1)S(1)}, u32[]{:S(2)}, u32[]{:S(2)}) %collective-permute-start.13) | collective-permute-done | bytes 65568 | tf_op jit(solution)/shard_map/ppermute | solution.py:41
  30.8 3.5 %collective-permute-start.15 = (bf16[1,8,16,256]{3,2,1,0:T(8,128)(2,1)S(1)}, bf16[1,8,16,256]{3,2,1,0:T(8,128)(2,1)S(1)}, u32[]{:S(2)}, u32[]{:S(2)}) collective-permute-start(bf16[1,8,16,256]{3,2,1,0:T(8,128)(2,1)S(1)} %get-tuple-element.31.refs_7_), channel_id=1, source_target_pairs={{0,3},{1,2},{2,1},{3,0},{4,7},{5,6},{6,5},{7,4},{8,11},{9,10},{10,... | collective-permute-start | bytes 196616 | tf_op jit(solution)/shard_map/ppermute | solution.py:41
  34.3 0.0 collective-permute-start.16
  34.3 0.0 collective-permute-done.10.refs_5_
  34.3 0.0 collective-permute-done.12.refs_6_
  34.3 0.3 shard_map.117.refs_7_
  34.6 0.1 collective-permute-start.14
  34.7 0.3 shard_map.118.own_ref
  35.0 2.1 %collective-permute-done.15.refs_1_ = bf16[1,8,16,256]{3,2,1,0:T(8,128)(2,1)S(1)} collective-permute-done((bf16[1,8,16,256]{3,2,1,0:T(8,128)(2,1)S(1)}, bf16[1,8,16,256]{3,2,1,0:T(8,128)(2,1)S(1)}, u32[]{:S(2)}, u32[]{:S(2)}) %collective-permute-start.15) | collective-permute-done | bytes 65568 | tf_op jit(solution)/shard_map/ppermute | solution.py:41
  37.1 1.5 %collective-permute-done.16.refs_2_ = bf16[1,8,16,256]{3,2,1,0:T(8,128)(2,1)S(1)} collective-permute-done((bf16[1,8,16,256]{3,2,1,0:T(8,128)(2,1)S(1)}, bf16[1,8,16,256]{3,2,1,0:T(8,128)(2,1)S(1)}, u32[]{:S(2)}, u32[]{:S(2)}) %collective-permute-start.16) | collective-permute-done | bytes 65568 | tf_op jit(solution)/shard_map/ppermute | solution.py:41
  38.6 0.0 collective-permute-done.14.other_ref
  38.6 1.2 %shard_map.119 = (bf16[128,2048]{1,0:T(8,128)(2,1)}, f32[192,256]{1,0:T(8,128)}, f32[192,256]{1,0:T(8,128)}, f32[192,256]{1,0:T(8,128)}) custom-call(f32[576,256]{1,0:T(8,128)S(1)} %shard_map.118.own_ref, bf16[576,256]{1,0:T(8,128)(2,1)S(1)} %collective-permute-done.14.other_ref, bf16[1,16,128]{2,1,0:T(8,128)(2,1)S(1)} %get-tuple-element.32.hot_ref, ...), custom_call_target="tpu_custom_call" | custom-call | tf_op jit(solution)/shard_map/pallas_call | solution.py:336
  (3 shorter events, 0.1 us)
Async XLA Ops:
  2.2 17.7 %collective-permute-start.6 = (bf16[576,256]{1,0:T(8,128)(2,1)S(1)}, bf16[576,256]{1,0:T(8,128)(2,1)S(1)}, u32[]{:S(2)}, u32[]{:S(2)}) collective-permute-start(bf16[576,256]{1,0:T(8,128)(2,1)S(1)} %get-tuple-element.26), channel_id=1, source_target_pairs={{0,8},{4,12},{8,0},{12,4},{16,24},{20,28},{24,16},{28,20},{1,9},{5... | collective-permute-start | bytes 884744 | tf_op jit(solution)/shard_map/ppermute | solution.py:41
  5.2 14.8 %collective-permute-start.7 = (bf16[576,256]{1,0:T(8,128)(2,1)S(1)}, bf16[576,256]{1,0:T(8,128)(2,1)S(1)}, u32[]{:S(2)}, u32[]{:S(2)}) collective-permute-start(bf16[576,256]{1,0:T(8,128)(2,1)S(1)} %get-tuple-element.26), channel_id=1, source_target_pairs={{0,16},{4,20},{8,24},{12,28},{16,0},{20,4},{24,8},{28,12},{1,17},{... | collective-permute-start | bytes 884744 | tf_op jit(solution)/shard_map/ppermute | solution.py:41
  6.7 13.3 %collective-permute-start.8 = (bf16[576,256]{1,0:T(8,128)(2,1)S(1)}, bf16[576,256]{1,0:T(8,128)(2,1)S(1)}, u32[]{:S(2)}, u32[]{:S(2)}) collective-permute-start(bf16[576,256]{1,0:T(8,128)(2,1)S(1)} %get-tuple-element.26), channel_id=1, source_target_pairs={{0,24},{4,28},{8,16},{12,20},{16,8},{20,12},{24,0},{28,4},{1,25},{... | collective-permute-start | bytes 884744 | tf_op jit(solution)/shard_map/ppermute | solution.py:41
  6.8 8.2 %collective-permute-start.1 = (bf16[2,8,16,256]{3,2,1,0:T(8,128)(2,1)S(1)}, bf16[2,8,16,256]{3,2,1,0:T(8,128)(2,1)S(1)}, u32[]{:S(2)}, u32[]{:S(2)}) collective-permute-start(bf16[2,8,16,256]{3,2,1,0:T(8,128)(2,1)S(1)} %bitcast.16), channel_id=1, source_target_pairs={{0,3},{1,2},{2,1},{3,0},{4,7},{5,6},{6,5},{7,4},{8,11},{9,10},{10,... | collective-permute-start | bytes 393224 | tf_op jit(solution)/shard_map/ppermute | solution.py:41
  10.8 6.8 %collective-permute-start = (bf16[2,8,16,256]{3,2,1,0:T(8,128)(2,1)S(1)}, bf16[2,8,16,256]{3,2,1,0:T(8,128)(2,1)S(1)}, u32[]{:S(2)}, u32[]{:S(2)}) collective-permute-start(bf16[2,8,16,256]{3,2,1,0:T(8,128)(2,1)S(1)} %bitcast.17), channel_id=1, source_target_pairs={{0,1},{1,0},{2,3},{3,2},{4,5},{5,4},{6,7},{7,6},{8,9},{9,8},{10,11... | collective-permute-start | bytes 393224 | tf_op jit(solution)/shard_map/ppermute | solution.py:41
  15.0 5.0 %collective-permute-start.2 = (bf16[2,8,16,256]{3,2,1,0:T(8,128)(2,1)S(1)}, bf16[2,8,16,256]{3,2,1,0:T(8,128)(2,1)S(1)}, u32[]{:S(2)}, u32[]{:S(2)}) collective-permute-start(bf16[2,8,16,256]{3,2,1,0:T(8,128)(2,1)S(1)} %collective-permute-done.1.refs_3_.refs_6_), channel_id=1, source_target_pairs={{0,1},{1,0},{2,3},{3,2},{4,5},{5,4},{6,7},{7,6},{8,9},{9,8},{10,11... | collective-permute-start | bytes 393224 | tf_op jit(solution)/shard_map/ppermute | solution.py:41
  20.1 4.3 %collective-permute-start.9 = (bf16[4,576,256]{2,1,0:T(8,128)(2,1)S(1)}, bf16[4,576,256]{2,1,0:T(8,128)(2,1)S(1)}, u32[]{:S(2)}, u32[]{:S(2)}) collective-permute-start(bf16[4,576,256]{2,1,0:T(8,128)(2,1)S(1)} %shard_map.113.refs_4_), channel_id=1, source_target_pairs={{0,4},{4,0},{8,12},{12,8},{16,20},{20,16},{24,28},{28,24},{1,5},{5... | collective-permute-start | bytes 3538952 | tf_op jit(solution)/shard_map/ppermute | solution.py:41
  20.2 8.3 %collective-permute-start.3 = (bf16[2,2,64,256]{3,2,1,0:T(8,128)(2,1)S(1)}, bf16[2,2,64,256]{3,2,1,0:T(8,128)(2,1)S(1)}, u32[]{:S(2)}, u32[]{:S(2)}) collective-permute-start(bf16[2,2,64,256]{3,2,1,0:T(8,128)(2,1)S(1)} %get-tuple-element.23), channel_id=1, source_target_pairs={{0,24},{4,28},{8,16},{12,20},{16,8},{20,12},{24,0},{28,4},{1,25},{... | collective-permute-start | bytes 393224 | tf_op jit(solution)/shard_map/ppermute | solution.py:41
  22.8 7.2 %collective-permute-start.4 = (bf16[2,2,64,256]{3,2,1,0:T(8,128)(2,1)S(1)}, bf16[2,2,64,256]{3,2,1,0:T(8,128)(2,1)S(1)}, u32[]{:S(2)}, u32[]{:S(2)}) collective-permute-start(bf16[2,2,64,256]{3,2,1,0:T(8,128)(2,1)S(1)} %get-tuple-element.24), channel_id=1, source_target_pairs={{0,8},{4,20},{8,0},{12,28},{16,24},{20,4},{24,16},{28,12},{1,9},{5... | collective-permute-start | bytes 393224 | tf_op jit(solution)/shard_map/ppermute | solution.py:46
  23.3 6.7 %collective-permute-start.5 = (bf16[2,2,64,256]{3,2,1,0:T(8,128)(2,1)S(1)}, bf16[2,2,64,256]{3,2,1,0:T(8,128)(2,1)S(1)}, u32[]{:S(2)}, u32[]{:S(2)}) collective-permute-start(bf16[2,2,64,256]{3,2,1,0:T(8,128)(2,1)S(1)} %get-tuple-element.25), channel_id=1, source_target_pairs={{0,20},{4,8},{8,28},{12,0},{16,4},{20,24},{24,12},{28,16},{1,21},{... | collective-permute-start | bytes 393224 | tf_op jit(solution)/shard_map/ppermute | solution.py:51
  25.9 1.6 %collective-permute-start.11 = (bf16[64,576]{1,0:T(8,128)(2,1)S(1)}, bf16[64,576]{1,0:T(8,128)(2,1)S(1)}, u32[]{:S(2)}, u32[]{:S(2)}) collective-permute-start(bf16[64,576]{1,0:T(8,128)(2,1)S(1)} %get-tuple-element.27.refs_0_.refs_4_), channel_id=1, source_target_pairs={{0,4},{4,0},{8,12},{12,8},{16,20},{20,16},{24,28},{28,24},{1,5},{5... | collective-permute-start | bytes 221192 | tf_op jit(solution)/shard_map/ppermute | solution.py:41
  26.5 4.3 %collective-permute-start.13 = (bf16[1,8,16,256]{3,2,1,0:T(8,128)(2,1)S(1)}, bf16[1,8,16,256]{3,2,1,0:T(8,128)(2,1)S(1)}, u32[]{:S(2)}, u32[]{:S(2)}) collective-permute-start(bf16[1,8,16,256]{3,2,1,0:T(8,128)(2,1)S(1)} %get-tuple-element.29), channel_id=1, source_target_pairs={{0,1},{1,0},{2,3},{3,2},{4,5},{5,4},{6,7},{7,6},{8,9},{9,8},{10,11... | collective-permute-start | bytes 196616 | tf_op jit(solution)/shard_map/ppermute | solution.py:41
  27.5 6.8 %collective-permute-start.10 = (bf16[64,576]{1,0:T(8,128)(2,1)S(1)}, bf16[64,576]{1,0:T(8,128)(2,1)S(1)}, u32[]{:S(2)}, u32[]{:S(2)}) collective-permute-start(bf16[64,576]{1,0:T(8,128)(2,1)S(1)} %get-tuple-element.27.refs_0_.refs_4_), channel_id=1, source_target_pairs={{0,24},{4,28},{8,16},{12,20},{16,8},{20,12},{24,0},{28,4},{1,25},{... | collective-permute-start | bytes 221192 | tf_op jit(solution)/shard_map/ppermute | solution.py:41
  28.6 5.7 %collective-permute-start.12 = (bf16[128,576]{1,0:T(8,128)(2,1)S(1)}, bf16[128,576]{1,0:T(8,128)(2,1)S(1)}, u32[]{:S(2)}, u32[]{:S(2)}) collective-permute-start(bf16[128,576]{1,0:T(8,128)(2,1)S(1)} %shard_map.115), channel_id=1, source_target_pairs={{0,8},{4,20},{8,0},{12,28},{16,24},{20,4},{24,16},{28,12},{1,9},{5... | collective-permute-start | bytes 442376 | tf_op jit(solution)/shard_map/ppermute | solution.py:46
  30.8 6.2 %collective-permute-start.15 = (bf16[1,8,16,256]{3,2,1,0:T(8,128)(2,1)S(1)}, bf16[1,8,16,256]{3,2,1,0:T(8,128)(2,1)S(1)}, u32[]{:S(2)}, u32[]{:S(2)}) collective-permute-start(bf16[1,8,16,256]{3,2,1,0:T(8,128)(2,1)S(1)} %get-tuple-element.31.refs_7_), channel_id=1, source_target_pairs={{0,3},{1,2},{2,1},{3,0},{4,7},{5,6},{6,5},{7,4},{8,11},{9,10},{10,... | collective-permute-start | bytes 196616 | tf_op jit(solution)/shard_map/ppermute | solution.py:41
  34.3 4.3 %collective-permute-start.16 = (bf16[1,8,16,256]{3,2,1,0:T(8,128)(2,1)S(1)}, bf16[1,8,16,256]{3,2,1,0:T(8,128)(2,1)S(1)}, u32[]{:S(2)}, u32[]{:S(2)}) collective-permute-start(bf16[1,8,16,256]{3,2,1,0:T(8,128)(2,1)S(1)} %get-tuple-element.33), channel_id=1, source_target_pairs={{0,1},{1,0},{2,3},{3,2},{4,5},{5,4},{6,7},{7,6},{8,9},{9,8},{10,11... | collective-permute-start | bytes 196616 | tf_op jit(solution)/shard_map/ppermute | solution.py:41
  34.6 4.0 %collective-permute-start.14 = (bf16[576,256]{1,0:T(8,128)(2,1)S(1)}, bf16[576,256]{1,0:T(8,128)(2,1)S(1)}, u32[]{:S(2)}, u32[]{:S(2)}) collective-permute-start(bf16[576,256]{1,0:T(8,128)(2,1)S(1)} %shard_map.117.refs_7_), channel_id=1, source_target_pairs={{0,4},{4,0},{8,12},{12,8},{16,20},{20,16},{24,28},{28,24},{1,5},{5... | collective-permute-start | bytes 884744 | tf_op jit(solution)/shard_map/ppermute | solution.py:41

commit v6 on v5

--- a/solution.py
+++ b/solution.py
@@ -177,8 +177,7 @@
     out_ref[2 * hidden :] = down.astype(out_ref.dtype)
 
 
-def add_kernel(near_ref, relay_ref, direct_ref, out_ref, direct_out_ref):
-    direct_out_ref[...] = direct_ref[...]
+def add_kernel(near_ref, relay_ref, out_ref):
     half = out_ref.shape[0]
     total = near_ref[half:].astype(jnp.float32) + relay_ref[...].astype(jnp.float32)
     out_ref[...] = total.astype(out_ref.dtype)
@@ -303,14 +302,15 @@
     all_grads = [grads, swap(grads, "dp", 2 * SINGLE)]
     all_grads += [cross(chip_grads, pair) for pair in pairs]
     part = struct((flight, blocks, CAP, width), jnp.bfloat16)
-    half_sum, direct = call(
+    direct = swap(direct, "expert", 1)
+    half_sum = call(
         add_kernel,
-        (part, part),
-        (near_parts, swap(relay, "expert", 1), direct),
+        part,
+        (near_parts, swap(relay, "expert", 1)),
         after=block_rows[1:],
-        flops=3 * 10**9,
-    )
-    pair_sum, direct = swap(half_sum, "expert", 3), swap(direct, "expert", 1)
+        flops=15 * 10**8,
+    )
+    pair_sum = swap(half_sum, "expert", 3)
     returned = (near_parts, pair_sum, direct)
     if flight > 1:
         slot_grad = call(sum_kernel, part, returned)

time: 40 us -> 39.2 us (0.980)
  waiting for transfers between devices: 12.7 us -> 11 us
  starting transfers between devices: 21.3 us -> 22.2 us
    ppermute x14, waiting for transfers between devices: 12.5 us -> 11 us  [swap(): return lax.ppermute(values, axis, [(i, i ^ shift) for i in range(size)])]
    ppermute x14, starting transfers between devices: 18.5 us -> 19.5 us  [swap(): return lax.ppermute(values, axis, [(i, i ^ shift) for i in range(size)])]
  transfers between devices with their start and end apart: 17 -> 17, of which waited for: 8 -> 6; matrix products, arithmetic and copies ran while one was open for 0% -> 0% of each run, Pallas kernels for 5% -> 6%
where the time goes in v6:
time: 39.2 us; the launch traced here: 39 us
  starting transfers between devices  22.2 us (57%)
  waiting for transfers between devices  11 us (28%)
  Pallas kernels  5.05 us (13%)
  between operations  0.72 us (2%)
    ppermute x14, starting transfers between devices, swap(): return lax.ppermute(values, axis, [(i, i ^ shift) for i in range(size)])  19.5 us
    ppermute x14, waiting for transfers between devices, swap(): return lax.ppermute(values, axis, [(i, i ^ shift) for i in range(size)])  11 us
    pallas_call x7, Pallas kernels, call(): pl.pallas_call(run, out_shape=out_shape, in_specs=[pl.BlockSpec(memory_sp...  2.25 us
    ppermute x2, starting transfers between devices, cross(): lax.ppermute(values, 'dp', [(i, i ^ 2 * pair[i % 2]) for i in range(size)])  1.73 us
    pallas_call x1, Pallas kernels, body(): pl.pallas_call(begin_kernel, out_shape=(struct((flight, 2, blocks, CAP, w...  1.58 us
    pallas_call x1, Pallas kernels, body(): pl.pallas_call(functools.partial(finish_kernel, len(returned)), out_shape...  1.23 us
    ppermute x1, starting transfers between devices, cross_cores(): lax.ppermute(values, 'dp', [(i, i ^ 2 * pair[1 - i % 2] + 1) for i in ran...  1.02 us
  transfers between devices with their start and end apart: 17, of which 6 were waited for; matrix products, arithmetic and copies ran while one was open for 0% of the time, Pallas kernels for 6%

profile of v6, /device:TPU:0, one launch (start us, length us, event | category | flops | bytes accessed | tf_op | source)
XLA Modules:
  0.0 39.0 jit_solution(13387505015222821647)
XLA Ops:
  0.6 1.6 %shard_map.111 = (bf16[1,2,8,16,256]{4,3,2,1,0:T(8,128)(2,1)S(1)}, bf16[1,16,128]{2,1,0:T(8,128)(2,1)S(1)}, bf16[576,256]{1,0:T(8,128)(2,1)S(1)}) custom-call(s32[8,128]{1,0:T(8,128)} %bitcast.22, s32[8,128]{1,0:T(8,128)} %bitcast.23, f32[8,128]{1,0:T(8,128)} %bitcast.24, bf16[128,2048]{1,0:T(8,128)(2,1)} %tok_hbm.1, bf16[128,2048]{1,0:T(8,128)(2,1)} %cot_hbm.1, ...), custom_call_target="tpu_custom_call" | custom-call | tf_op jit(solution)/shard_map/pallas_call | solution.py:245
  2.2 3.0 %collective-permute-start.6 = (bf16[576,256]{1,0:T(8,128)(2,1)S(1)}, bf16[576,256]{1,0:T(8,128)(2,1)S(1)}, u32[]{:S(2)}, u32[]{:S(2)}) collective-permute-start(bf16[576,256]{1,0:T(8,128)(2,1)S(1)} %get-tuple-element.24), channel_id=1, source_target_pairs={{0,8},{4,12},{8,0},{12,4},{16,24},{20,28},{24,16},{28,20},{1,9},{5... | collective-permute-start | bytes 884744 | tf_op jit(solution)/shard_map/ppermute | solution.py:41
  5.2 1.5 %collective-permute-start.7 = (bf16[576,256]{1,0:T(8,128)(2,1)S(1)}, bf16[576,256]{1,0:T(8,128)(2,1)S(1)}, u32[]{:S(2)}, u32[]{:S(2)}) collective-permute-start(bf16[576,256]{1,0:T(8,128)(2,1)S(1)} %get-tuple-element.24), channel_id=1, source_target_pairs={{0,16},{4,20},{8,24},{12,28},{16,0},{20,4},{24,8},{28,12},{1,17},{... | collective-permute-start | bytes 884744 | tf_op jit(solution)/shard_map/ppermute | solution.py:41
  6.7 0.0 collective-permute-start.8
  6.8 4.1 %collective-permute-start.1 = (bf16[2,8,16,256]{3,2,1,0:T(8,128)(2,1)S(1)}, bf16[2,8,16,256]{3,2,1,0:T(8,128)(2,1)S(1)}, u32[]{:S(2)}, u32[]{:S(2)}) collective-permute-start(bf16[2,8,16,256]{3,2,1,0:T(8,128)(2,1)S(1)} %bitcast.16), channel_id=1, source_target_pairs={{0,3},{1,2},{2,1},{3,0},{4,7},{5,6},{6,5},{7,4},{8,11},{9,10},{10,... | collective-permute-start | bytes 393224 | tf_op jit(solution)/shard_map/ppermute | solution.py:41
  10.8 0.0 collective-permute-start
  10.8 4.1 %collective-permute-done.1.refs_3_.refs_6_ = bf16[2,8,16,256]{3,2,1,0:T(8,128)(2,1)S(1)} collective-permute-done((bf16[2,8,16,256]{3,2,1,0:T(8,128)(2,1)S(1)}, bf16[2,8,16,256]{3,2,1,0:T(8,128)(2,1)S(1)}, u32[]{:S(2)}, u32[]{:S(2)}) %collective-permute-start.1) | collective-permute-done | bytes 131104 | tf_op jit(solution)/shard_map/ppermute | solution.py:41
  15.0 1.0 %collective-permute-start.2 = (bf16[2,8,16,256]{3,2,1,0:T(8,128)(2,1)S(1)}, bf16[2,8,16,256]{3,2,1,0:T(8,128)(2,1)S(1)}, u32[]{:S(2)}, u32[]{:S(2)}) collective-permute-start(bf16[2,8,16,256]{3,2,1,0:T(8,128)(2,1)S(1)} %collective-permute-done.1.refs_3_.refs_6_), channel_id=1, source_target_pairs={{0,1},{1,0},{2,3},{3,2},{4,5},{5,4},{6,7},{7,6},{8,9},{9,8},{10,11... | collective-permute-start | bytes 393224 | tf_op jit(solution)/shard_map/ppermute | solution.py:41
  16.0 1.6 %collective-permute-done.refs_1_.refs_4_ = bf16[2,8,16,256]{3,2,1,0:T(8,128)(2,1)S(1)} collective-permute-done((bf16[2,8,16,256]{3,2,1,0:T(8,128)(2,1)S(1)}, bf16[2,8,16,256]{3,2,1,0:T(8,128)(2,1)S(1)}, u32[]{:S(2)}, u32[]{:S(2)}) %collective-permute-start) | collective-permute-done | bytes 131104 | tf_op jit(solution)/shard_map/ppermute | solution.py:41
  17.6 2.3 %collective-permute-done.2.refs_2_.refs_5_ = bf16[2,8,16,256]{3,2,1,0:T(8,128)(2,1)S(1)} collective-permute-done((bf16[2,8,16,256]{3,2,1,0:T(8,128)(2,1)S(1)}, bf16[2,8,16,256]{3,2,1,0:T(8,128)(2,1)S(1)}, u32[]{:S(2)}, u32[]{:S(2)}) %collective-permute-start.2) | collective-permute-done | bytes 131104 | tf_op jit(solution)/shard_map/ppermute | solution.py:41
  19.9 0.0 collective-permute-done.6
  19.9 0.1 collective-permute-done.7
  20.0 0.0 collective-permute-done.8
  20.0 0.1 shard_map.113.refs_4_
  20.1 0.1 collective-permute-start.9
  20.2 2.6 %collective-permute-start.3 = (bf16[2,2,64,256]{3,2,1,0:T(8,128)(2,1)S(1)}, bf16[2,2,64,256]{3,2,1,0:T(8,128)(2,1)S(1)}, u32[]{:S(2)}, u32[]{:S(2)}) collective-permute-start(bf16[2,2,64,256]{3,2,1,0:T(8,128)(2,1)S(1)} %get-tuple-element.21), channel_id=1, source_target_pairs={{0,24},{4,28},{8,16},{12,20},{16,8},{20,12},{24,0},{28,4},{1,25},{... | collective-permute-start | bytes 393224 | tf_op jit(solution)/shard_map/ppermute | solution.py:41
  22.8 0.5 %collective-permute-start.4 = (bf16[2,2,64,256]{3,2,1,0:T(8,128)(2,1)S(1)}, bf16[2,2,64,256]{3,2,1,0:T(8,128)(2,1)S(1)}, u32[]{:S(2)}, u32[]{:S(2)}) collective-permute-start(bf16[2,2,64,256]{3,2,1,0:T(8,128)(2,1)S(1)} %get-tuple-element.22), channel_id=1, source_target_pairs={{0,8},{4,20},{8,0},{12,28},{16,24},{20,4},{24,16},{28,12},{1,9},{5... | collective-permute-start | bytes 393224 | tf_op jit(solution)/shard_map/ppermute | solution.py:46
  23.3 1.0 %collective-permute-start.5 = (bf16[2,2,64,256]{3,2,1,0:T(8,128)(2,1)S(1)}, bf16[2,2,64,256]{3,2,1,0:T(8,128)(2,1)S(1)}, u32[]{:S(2)}, u32[]{:S(2)}) collective-permute-start(bf16[2,2,64,256]{3,2,1,0:T(8,128)(2,1)S(1)} %get-tuple-element.23), channel_id=1, source_target_pairs={{0,20},{4,8},{8,28},{12,0},{16,4},{20,24},{24,12},{28,16},{1,21},{... | collective-permute-start | bytes 393224 | tf_op jit(solution)/shard_map/ppermute | solution.py:51
  24.4 0.0 collective-permute-done.9.refs_5_
  24.4 1.5 %shard_map.114 = (bf16[64,576]{1,0:T(8,128)(2,1)S(1)}, bf16[2,8,16,256]{3,2,1,0:T(8,128)(2,1)S(1)}, bf16[1,8,16,256]{3,2,1,0:T(8,128)(2,1)S(1)}, bf16[1,8,16,256]{3,2,1,0:T(8,128)(2,1)S(1)}) custom-call(bf16[2,8,16,256]{3,2,1,0:T(8,128)(2,1)S(1)} %bitcast.19, bf16[2,8,16,256]{3,2,1,0:T(8,128)(2,1)S(1)} %collective-permute-done.refs_1_.refs_4_, ...), custom_call_target="tpu_custom_call" | custom-call | flops 5000000000 | tf_op jit(solution)/shard_map/pallas_call | solution.py:28
  25.9 0.7 %collective-permute-start.11 = (bf16[64,576]{1,0:T(8,128)(2,1)S(1)}, bf16[64,576]{1,0:T(8,128)(2,1)S(1)}, u32[]{:S(2)}, u32[]{:S(2)}) collective-permute-start(bf16[64,576]{1,0:T(8,128)(2,1)S(1)} %get-tuple-element.25.refs_0_.refs_4_), channel_id=1, source_target_pairs={{0,4},{4,0},{8,12},{12,8},{16,20},{20,16},{24,28},{28,24},{1,5},{5... | collective-permute-start | bytes 221192 | tf_op jit(solution)/shard_map/ppermute | solution.py:41
  26.5 0.9 %collective-permute-start.13 = (bf16[1,8,16,256]{3,2,1,0:T(8,128)(2,1)S(1)}, bf16[1,8,16,256]{3,2,1,0:T(8,128)(2,1)S(1)}, u32[]{:S(2)}, u32[]{:S(2)}) collective-permute-start(bf16[1,8,16,256]{3,2,1,0:T(8,128)(2,1)S(1)} %get-tuple-element.27), channel_id=1, source_target_pairs={{0,1},{1,0},{2,3},{3,2},{4,5},{5,4},{6,7},{7,6},{8,9},{9,8},{10,11... | collective-permute-start | bytes 196616 | tf_op jit(solution)/shard_map/ppermute | solution.py:41
  27.5 0.0 collective-permute-done.11.refs_1_
  27.5 1.2 %collective-permute-start.12 = (bf16[128,576]{1,0:T(8,128)(2,1)S(1)}, bf16[128,576]{1,0:T(8,128)(2,1)S(1)}, u32[]{:S(2)}, u32[]{:S(2)}) collective-permute-start(bf16[128,576]{1,0:T(8,128)(2,1)S(1)} %shard_map.115), channel_id=1, source_target_pairs={{0,8},{4,20},{8,0},{12,28},{16,24},{20,4},{24,16},{28,12},{1,9},{5... | collective-permute-start | bytes 442376 | tf_op jit(solution)/shard_map/ppermute | solution.py:46
  28.7 0.0 collective-permute-done.3.refs_2_.refs_1_
  28.7 1.4 %collective-permute-start.10 = (bf16[64,576]{1,0:T(8,128)(2,1)S(1)}, bf16[64,576]{1,0:T(8,128)(2,1)S(1)}, u32[]{:S(2)}, u32[]{:S(2)}) collective-permute-start(bf16[64,576]{1,0:T(8,128)(2,1)S(1)} %get-tuple-element.25.refs_0_.refs_4_), channel_id=1, source_target_pairs={{0,24},{4,28},{8,16},{12,20},{16,8},{20,12},{24,0},{28,4},{1,25},{... | collective-permute-start | bytes 221192 | tf_op jit(solution)/shard_map/ppermute | solution.py:41
  30.0 0.0 collective-permute-done.4.refs_3_.refs_2_
  30.0 1.5 %collective-permute-start.16 = (bf16[1,8,16,256]{3,2,1,0:T(8,128)(2,1)S(1)}, bf16[1,8,16,256]{3,2,1,0:T(8,128)(2,1)S(1)}, u32[]{:S(2)}, u32[]{:S(2)}) collective-permute-start(bf16[1,8,16,256]{3,2,1,0:T(8,128)(2,1)S(1)} %get-tuple-element.29), channel_id=1, source_target_pairs={{0,1},{1,0},{2,3},{3,2},{4,5},{5,4},{6,7},{7,6},{8,9},{9,8},{10,11... | collective-permute-start | bytes 196616 | tf_op jit(solution)/shard_map/ppermute | solution.py:41
  31.6 0.0 collective-permute-done.5.refs_4_.refs_3_
  31.6 0.0 collective-permute-done.13.refs_1_
  31.6 2.7 %collective-permute-start.15 = (bf16[1,8,16,256]{3,2,1,0:T(8,128)(2,1)S(1)}, bf16[1,8,16,256]{3,2,1,0:T(8,128)(2,1)S(1)}, u32[]{:S(2)}, u32[]{:S(2)}) collective-permute-start(bf16[1,8,16,256]{3,2,1,0:T(8,128)(2,1)S(1)} %shard_map.116.refs_7_), channel_id=1, source_target_pairs={{0,3},{1,2},{2,1},{3,0},{4,7},{5,6},{6,5},{7,4},{8,11},{9,10},{10,... | collective-permute-start | bytes 196616 | tf_op jit(solution)/shard_map/ppermute | solution.py:41
  34.3 0.6 %collective-permute-done.10.refs_5_ = bf16[64,576]{1,0:T(8,128)(2,1)S(1)} collective-permute-done((bf16[64,576]{1,0:T(8,128)(2,1)S(1)}, bf16[64,576]{1,0:T(8,128)(2,1)S(1)}, u32[]{:S(2)}, u32[]{:S(2)}) %collective-permute-start.10) | collective-permute-done | bytes 73760 | tf_op jit(solution)/shard_map/ppermute | solution.py:41
  34.9 0.0 collective-permute-done.12.refs_6_
  34.9 0.3 shard_map.117.refs_7_
  35.2 0.1 collective-permute-start.14
  35.3 0.3 shard_map.118.own_ref
  35.6 0.0 collective-permute-done.16.refs_2_
  35.6 2.2 %collective-permute-done.15.refs_1_ = bf16[1,8,16,256]{3,2,1,0:T(8,128)(2,1)S(1)} collective-permute-done((bf16[1,8,16,256]{3,2,1,0:T(8,128)(2,1)S(1)}, bf16[1,8,16,256]{3,2,1,0:T(8,128)(2,1)S(1)}, u32[]{:S(2)}, u32[]{:S(2)}) %collective-permute-start.15) | collective-permute-done | bytes 65568 | tf_op jit(solution)/shard_map/ppermute | solution.py:41
  37.8 0.0 collective-permute-done.14.other_ref
  37.8 1.2 %shard_map.119 = (bf16[128,2048]{1,0:T(8,128)(2,1)}, f32[192,256]{1,0:T(8,128)}, f32[192,256]{1,0:T(8,128)}, f32[192,256]{1,0:T(8,128)}) custom-call(f32[576,256]{1,0:T(8,128)S(1)} %shard_map.118.own_ref, bf16[576,256]{1,0:T(8,128)(2,1)S(1)} %collective-permute-done.14.other_ref, bf16[1,16,128]{2,1,0:T(8,128)(2,1)S(1)} %get-tuple-element.28.hot_ref, ...), custom_call_target="tpu_custom_call" | custom-call | tf_op jit(solution)/shard_map/pallas_call | solution.py:336
  (3 shorter events, 0.1 us)
Async XLA Ops:
  2.2 17.7 %collective-permute-start.6 = (bf16[576,256]{1,0:T(8,128)(2,1)S(1)}, bf16[576,256]{1,0:T(8,128)(2,1)S(1)}, u32[]{:S(2)}, u32[]{:S(2)}) collective-permute-start(bf16[576,256]{1,0:T(8,128)(2,1)S(1)} %get-tuple-element.24), channel_id=1, source_target_pairs={{0,8},{4,12},{8,0},{12,4},{16,24},{20,28},{24,16},{28,20},{1,9},{5... | collective-permute-start | bytes 884744 | tf_op jit(solution)/shard_map/ppermute | solution.py:41
  5.2 14.8 %collective-permute-start.7 = (bf16[576,256]{1,0:T(8,128)(2,1)S(1)}, bf16[576,256]{1,0:T(8,128)(2,1)S(1)}, u32[]{:S(2)}, u32[]{:S(2)}) collective-permute-start(bf16[576,256]{1,0:T(8,128)(2,1)S(1)} %get-tuple-element.24), channel_id=1, source_target_pairs={{0,16},{4,20},{8,24},{12,28},{16,0},{20,4},{24,8},{28,12},{1,17},{... | collective-permute-start | bytes 884744 | tf_op jit(solution)/shard_map/ppermute | solution.py:41
  6.7 13.3 %collective-permute-start.8 = (bf16[576,256]{1,0:T(8,128)(2,1)S(1)}, bf16[576,256]{1,0:T(8,128)(2,1)S(1)}, u32[]{:S(2)}, u32[]{:S(2)}) collective-permute-start(bf16[576,256]{1,0:T(8,128)(2,1)S(1)} %get-tuple-element.24), channel_id=1, source_target_pairs={{0,24},{4,28},{8,16},{12,20},{16,8},{20,12},{24,0},{28,4},{1,25},{... | collective-permute-start | bytes 884744 | tf_op jit(solution)/shard_map/ppermute | solution.py:41
  6.8 8.2 %collective-permute-start.1 = (bf16[2,8,16,256]{3,2,1,0:T(8,128)(2,1)S(1)}, bf16[2,8,16,256]{3,2,1,0:T(8,128)(2,1)S(1)}, u32[]{:S(2)}, u32[]{:S(2)}) collective-permute-start(bf16[2,8,16,256]{3,2,1,0:T(8,128)(2,1)S(1)} %bitcast.16), channel_id=1, source_target_pairs={{0,3},{1,2},{2,1},{3,0},{4,7},{5,6},{6,5},{7,4},{8,11},{9,10},{10,... | collective-permute-start | bytes 393224 | tf_op jit(solution)/shard_map/ppermute | solution.py:41
  10.8 6.8 %collective-permute-start = (bf16[2,8,16,256]{3,2,1,0:T(8,128)(2,1)S(1)}, bf16[2,8,16,256]{3,2,1,0:T(8,128)(2,1)S(1)}, u32[]{:S(2)}, u32[]{:S(2)}) collective-permute-start(bf16[2,8,16,256]{3,2,1,0:T(8,128)(2,1)S(1)} %bitcast.17), channel_id=1, source_target_pairs={{0,1},{1,0},{2,3},{3,2},{4,5},{5,4},{6,7},{7,6},{8,9},{9,8},{10,11... | collective-permute-start | bytes 393224 | tf_op jit(solution)/shard_map/ppermute | solution.py:41
  15.0 5.0 %collective-permute-start.2 = (bf16[2,8,16,256]{3,2,1,0:T(8,128)(2,1)S(1)}, bf16[2,8,16,256]{3,2,1,0:T(8,128)(2,1)S(1)}, u32[]{:S(2)}, u32[]{:S(2)}) collective-permute-start(bf16[2,8,16,256]{3,2,1,0:T(8,128)(2,1)S(1)} %collective-permute-done.1.refs_3_.refs_6_), channel_id=1, source_target_pairs={{0,1},{1,0},{2,3},{3,2},{4,5},{5,4},{6,7},{7,6},{8,9},{9,8},{10,11... | collective-permute-start | bytes 393224 | tf_op jit(solution)/shard_map/ppermute | solution.py:41
  20.1 4.3 %collective-permute-start.9 = (bf16[4,576,256]{2,1,0:T(8,128)(2,1)S(1)}, bf16[4,576,256]{2,1,0:T(8,128)(2,1)S(1)}, u32[]{:S(2)}, u32[]{:S(2)}) collective-permute-start(bf16[4,576,256]{2,1,0:T(8,128)(2,1)S(1)} %shard_map.113.refs_4_), channel_id=1, source_target_pairs={{0,4},{4,0},{8,12},{12,8},{16,20},{20,16},{24,28},{28,24},{1,5},{5... | collective-permute-start | bytes 3538952 | tf_op jit(solution)/shard_map/ppermute | solution.py:41
  20.2 8.4 %collective-permute-start.3 = (bf16[2,2,64,256]{3,2,1,0:T(8,128)(2,1)S(1)}, bf16[2,2,64,256]{3,2,1,0:T(8,128)(2,1)S(1)}, u32[]{:S(2)}, u32[]{:S(2)}) collective-permute-start(bf16[2,2,64,256]{3,2,1,0:T(8,128)(2,1)S(1)} %get-tuple-element.21), channel_id=1, source_target_pairs={{0,24},{4,28},{8,16},{12,20},{16,8},{20,12},{24,0},{28,4},{1,25},{... | collective-permute-start | bytes 393224 | tf_op jit(solution)/shard_map/ppermute | solution.py:41
  22.8 7.2 %collective-permute-start.4 = (bf16[2,2,64,256]{3,2,1,0:T(8,128)(2,1)S(1)}, bf16[2,2,64,256]{3,2,1,0:T(8,128)(2,1)S(1)}, u32[]{:S(2)}, u32[]{:S(2)}) collective-permute-start(bf16[2,2,64,256]{3,2,1,0:T(8,128)(2,1)S(1)} %get-tuple-element.22), channel_id=1, source_target_pairs={{0,8},{4,20},{8,0},{12,28},{16,24},{20,4},{24,16},{28,12},{1,9},{5... | collective-permute-start | bytes 393224 | tf_op jit(solution)/shard_map/ppermute | solution.py:46
  23.3 8.2 %collective-permute-start.5 = (bf16[2,2,64,256]{3,2,1,0:T(8,128)(2,1)S(1)}, bf16[2,2,64,256]{3,2,1,0:T(8,128)(2,1)S(1)}, u32[]{:S(2)}, u32[]{:S(2)}) collective-permute-start(bf16[2,2,64,256]{3,2,1,0:T(8,128)(2,1)S(1)} %get-tuple-element.23), channel_id=1, source_target_pairs={{0,20},{4,8},{8,28},{12,0},{16,4},{20,24},{24,12},{28,16},{1,21},{... | collective-permute-start | bytes 393224 | tf_op jit(solution)/shard_map/ppermute | solution.py:51
  25.9 1.6 %collective-permute-start.11 = (bf16[64,576]{1,0:T(8,128)(2,1)S(1)}, bf16[64,576]{1,0:T(8,128)(2,1)S(1)}, u32[]{:S(2)}, u32[]{:S(2)}) collective-permute-start(bf16[64,576]{1,0:T(8,128)(2,1)S(1)} %get-tuple-element.25.refs_0_.refs_4_), channel_id=1, source_target_pairs={{0,4},{4,0},{8,12},{12,8},{16,20},{20,16},{24,28},{28,24},{1,5},{5... | collective-permute-start | bytes 221192 | tf_op jit(solution)/shard_map/ppermute | solution.py:41
  26.5 5.0 %collective-permute-start.13 = (bf16[1,8,16,256]{3,2,1,0:T(8,128)(2,1)S(1)}, bf16[1,8,16,256]{3,2,1,0:T(8,128)(2,1)S(1)}, u32[]{:S(2)}, u32[]{:S(2)}) collective-permute-start(bf16[1,8,16,256]{3,2,1,0:T(8,128)(2,1)S(1)} %get-tuple-element.27), channel_id=1, source_target_pairs={{0,1},{1,0},{2,3},{3,2},{4,5},{5,4},{6,7},{7,6},{8,9},{9,8},{10,11... | collective-permute-start | bytes 196616 | tf_op jit(solution)/shard_map/ppermute | solution.py:41
  27.5 7.4 %collective-permute-start.12 = (bf16[128,576]{1,0:T(8,128)(2,1)S(1)}, bf16[128,576]{1,0:T(8,128)(2,1)S(1)}, u32[]{:S(2)}, u32[]{:S(2)}) collective-permute-start(bf16[128,576]{1,0:T(8,128)(2,1)S(1)} %shard_map.115), channel_id=1, source_target_pairs={{0,8},{4,20},{8,0},{12,28},{16,24},{20,4},{24,16},{28,12},{1,9},{5... | collective-permute-start | bytes 442376 | tf_op jit(solution)/shard_map/ppermute | solution.py:46
  28.7 6.2 %collective-permute-start.10 = (bf16[64,576]{1,0:T(8,128)(2,1)S(1)}, bf16[64,576]{1,0:T(8,128)(2,1)S(1)}, u32[]{:S(2)}, u32[]{:S(2)}) collective-permute-start(bf16[64,576]{1,0:T(8,128)(2,1)S(1)} %get-tuple-element.25.refs_0_.refs_4_), channel_id=1, source_target_pairs={{0,24},{4,28},{8,16},{12,20},{16,8},{20,12},{24,0},{28,4},{1,25},{... | collective-permute-start | bytes 221192 | tf_op jit(solution)/shard_map/ppermute | solution.py:41
  30.0 5.5 %collective-permute-start.16 = (bf16[1,8,16,256]{3,2,1,0:T(8,128)(2,1)S(1)}, bf16[1,8,16,256]{3,2,1,0:T(8,128)(2,1)S(1)}, u32[]{:S(2)}, u32[]{:S(2)}) collective-permute-start(bf16[1,8,16,256]{3,2,1,0:T(8,128)(2,1)S(1)} %get-tuple-element.29), channel_id=1, source_target_pairs={{0,1},{1,0},{2,3},{3,2},{4,5},{5,4},{6,7},{7,6},{8,9},{9,8},{10,11... | collective-permute-start | bytes 196616 | tf_op jit(solution)/shard_map/ppermute | solution.py:41
  31.6 6.2 %collective-permute-start.15 = (bf16[1,8,16,256]{3,2,1,0:T(8,128)(2,1)S(1)}, bf16[1,8,16,256]{3,2,1,0:T(8,128)(2,1)S(1)}, u32[]{:S(2)}, u32[]{:S(2)}) collective-permute-start(bf16[1,8,16,256]{3,2,1,0:T(8,128)(2,1)S(1)} %shard_map.116.refs_7_), channel_id=1, source_target_pairs={{0,3},{1,2},{2,1},{3,0},{4,7},{5,6},{6,5},{7,4},{8,11},{9,10},{10,... | collective-permute-start | bytes 196616 | tf_op jit(solution)/shard_map/ppermute | solution.py:41
  35.2 2.6 %collective-permute-start.14 = (bf16[576,256]{1,0:T(8,128)(2,1)S(1)}, bf16[576,256]{1,0:T(8,128)(2,1)S(1)}, u32[]{:S(2)}, u32[]{:S(2)}) collective-permute-start(bf16[576,256]{1,0:T(8,128)(2,1)S(1)} %shard_map.117.refs_7_), channel_id=1, source_target_pairs={{0,4},{4,0},{8,12},{12,8},{16,20},{20,16},{24,28},{28,24},{1,5},{5... | collective-permute-start | bytes 884744 | tf_op jit(solution)/shard_map/ppermute | solution.py:41
